TPU v7x, 32 devices: a whole 2x2x4 slice. The times are simulated.
32 devices in a mesh: seg: 4 (over y, core), op: 8 (over z, x).
Axes of the slice: x: 2, y: 2, z: 4, core: 2. Of those that a mesh axis runs over, the one named last changes fastest.
Arguments:
- psi_start: bfloat16 [4, 32, 128, 128], P('seg', 'op'), may hold values from -4 to 4
- left_ops: bfloat16 [4, 32, 32, 128, 128], P('seg', 'op'), may hold values from -2 to 9, as said below
- right_ops: bfloat16 [4, 32, 32, 128, 128], P('seg', 'op'), may hold values from -2 to 9, as said below
- shifts: int32 [4, 32], P('seg', 'op'), may hold values from 0 to 31
- active: int32 [4, 32, 32], P('seg', 'op'), may hold values 0 or 1
Outputs:
- state: bfloat16 [4, 32, 128, 128], P('seg', 'op')
- rdm_pieces: float32 [4, 32], P('seg', 'op')
Inputs may be any that keep to these rules, and one draw needn't show every extreme that they name: `left_ops`: each block is a diagonal of entries between 1 and 7.8 plus off-diagonal entries of size about 2 / sqrt(128). `right_ops`: each block is a diagonal of entries between 1 and 7.8 plus off-diagonal entries of size about 2 / sqrt(128).
All inputs are finite; a program needn't handle non-finite values. No bound on the sum of `active` on one device may be relied on, other than what follows from the above.
Results may differ from a plain program's by a relative error of at most 0.0046.
Values may be sent and summed in bfloat16 or wider, within the bound.
No kernel may reach another device: no remote copies, remote signals or barrier semaphores. Data moves between devices by JAX's collectives and lax.ppermute only.
A program may use at most 64 MiB of HBM per device.

v0:
```python
import jax
import jax.numpy as jnp
from jax import lax
from jax.sharding import PartitionSpec as P

ITERS = 3


precise = lax.Precision.HIGHEST
step_size = 0.3


def shifted(block, axis, distance):
    devices = range(lax.axis_size(axis))
    route = [(i - distance, i) for i in devices if i - distance in devices]
    return lax.ppermute(block, axis, route)


def blockmul(left, right):
    return jnp.einsum("sij,sjl->sil", left, right, precision=precise)


def neighbour_gram(piece):
    return jnp.einsum("sji,sjl->sil", piece, piece, preferred_element_type=jnp.float32)


def term_products(state_low, lefts, rights):
    half = jnp.einsum(
        "ksij,sjl->ksil", lefts, state_low, preferred_element_type=jnp.float32
    ).astype(jnp.bfloat16)
    return jnp.einsum("ksil,ksml->ksim", half, rights, preferred_element_type=jnp.float32)


def route_table(shift_row, weights, blocks_all):
    sources = lax.broadcasted_iota(jnp.int32, (shift_row.shape[0], blocks_all), 1)
    targets = (sources + shift_row[:, None]) % blocks_all
    places = lax.broadcasted_iota(jnp.int32, (shift_row.shape[0], blocks_all, blocks_all), 1)
    return (places == targets[:, None, :]).astype(jnp.float32) * weights[:, None, :]


def place_terms(table, products):
    return jnp.einsum("kts,ksim->tim", table, products, precision=precise)


def term_values(state_low, products, table, value_scale):
    cross = jnp.einsum("ksim,tim->kst", products, state_low.astype(jnp.float32), precision=precise)
    return jnp.einsum("kts,kst->k", table, cross, precision=precise) * value_scale


def shards(psi_start, left_ops, right_ops, shifts, active):
    lefts = left_ops[0]
    rights = right_ops[0]
    weights = active[0].astype(jnp.float32)
    shift_row = shifts[0]
    own_start = psi_start[0]
    blocks_dev = own_start.shape[0]
    width = own_start.shape[1]
    blocks_all = lefts.shape[1]
    term_scale = 1.0 / (lefts.shape[0] * lax.axis_size("op"))
    count = float(blocks_all * width * width)
    own_offset = lax.axis_index("op") * blocks_dev
    table = route_table(shift_row, weights, blocks_all)
    full_state = lax.all_gather(own_start, "op", axis=0, tiled=True).astype(jnp.float32)
    for sweep_index in range(ITERS):
        full_low = full_state.astype(jnp.bfloat16)
        products = term_products(full_low, lefts, rights)
        partial_terms = place_terms(table, products) * term_scale
        own_part = lax.dynamic_slice_in_dim(full_state, own_offset, blocks_dev, 0)
        env_own_low = own_part.astype(jnp.bfloat16)
        from_left = shifted(env_own_low, "seg", 1)
        from_right = shifted(env_own_low, "seg", -1)
        env = neighbour_gram(from_left) + neighbour_gram(from_right)
        placed = lax.dynamic_update_slice_in_dim(
            jnp.zeros_like(partial_terms), blockmul(own_part, env) * (0.5 / width), own_offset, 0
        )
        applied = lax.psum(partial_terms + placed, "op")
        rho = jnp.sum(full_state * applied) / jnp.sum(full_state * full_state)
        stepped = full_state - step_size * (applied - rho * full_state)
        full_state = stepped * jnp.sqrt(count / jnp.sum(stepped * stepped))
    full_low = full_state.astype(jnp.bfloat16)
    own_low = lax.dynamic_slice_in_dim(full_low, own_offset, blocks_dev, 0)
    final_products = term_products(full_low, lefts, rights)
    pieces = term_values(full_low, final_products, table, 1.0 / count)
    return (own_low[None], pieces[None])


def solution(mesh):
    return jax.shard_map(
        shards,
        mesh=mesh,
        in_specs=(
            P("seg", "op", None, None),
            P("seg", "op", None, None, None),
            P("seg", "op", None, None, None),
            P("seg", "op"),
            P("seg", "op", None),
        ),
        out_specs=(P("seg", "op", None, None), P("seg", "op")),
        check_vma=False,
    )
```

profile of v0, /device:TPU:0, one launch (start us, length us, event | category | flops | bytes accessed | tf_op | source)
XLA Modules:
  0.0 526.8 jit_solution(15666688570660256642)
XLA Ops:
  7.2 0.7 all-gather.3.cloned.1.call-update
  7.9 0.7 add_select_fusion
  8.7 0.7 convert_bitcast_fusion.4
  9.4 43.6 %all-gather.3.cloned.1.call-done = bf16[1,32,128,128]{3,2,0,1:T(8,128)(2,1)} async-done(((bf16[1,4,128,128]{3,2,0,1:T(8,128)(2,1)}), bf16[1,32,128,128]{3,2,0,1:T(8,128)(2,1)}) %all-gather.3.cloned.1.call-update) | async-done | bytes 1048592 | tf_op jit(solution)/shard_map/all_gather | solution.py:63
  53.0 1.7 copy.22
  54.7 1.3 collective-permute-start.1
  56.0 3.0 collective-permute-start
  59.1 3.6 convert_bitcast_fusion.3
  62.8 3.1 fusion.17
  65.8 11.4 %fusion.36 = f32[32,128,128]{2,0,1:T(8,128)S(1)} fusion(f32[4,32,128,128]{3,2,1,0:T(8,128)S(1)} %fusion.17, f32[4,32]{1,0:T(4,128)S(1)} %convert_bitcast_fusion.4, s32[4,32]{1,0:T(4,128)S(1)} %add_select_fusion), kind=kOutput, calls=%fused_computation.45 | convolution fusion | flops 805314560 | bytes 10486784 | tf_op jit(solution)/shard_map/kts,ksim->tim/dot_general | solution.py:42
  77.2 1.9 copy.26
  79.2 1.7 broadcast_multiply_fusion.3
  81.4 1.3 fusion.50
  82.7 1.3 copy-done.8
  84.1 100.6 %all-reduce.4.cloned.1.call-done = f32[32,128,128]{1,2,0:T(8,128)} async-done(((f32[32,128,128]{1,2,0:T(8,128)}), f32[32,128,128]{1,2,0:T(8,128)}) %all-reduce.4.cloned.1.call-update) | async-done | bytes 2097168 | tf_op jit(solution)/shard_map/psum | solution.py:76
  184.7 2.9 multiply_reduce_fusion.7
  188.9 1.2 multiply_reduce_fusion.6
  190.8 2.2 fusion.60
  193.0 0.6 copy-done
  193.6 3.4 convert_bitcast_fusion.2
  197.0 1.4 collective-permute-start.3
  198.5 3.0 collective-permute-start.2
  201.5 5.3 %fusion.12 = f32[4,32,128,128]{3,2,1,0:T(8,128)S(1)} fusion(bf16[4,32,128,128]{2,3,0,1:T(8,128)(2,1)} %convert_bitcast_fusion.2, bf16[1,4,32,128,128]{4,3,2,1,0:T(8,128)(2,1)S(1)} %copy-done.4), kind=kOutput, calls=%fused_computation.12 | convolution fusion | flops 536870912 | bytes 16777216 | tf_op jit(solution)/shard_map/ksil,ksml->ksim/dot_general | solution.py:31
  206.8 24.2 %fusion.39 = f32[32,128,128]{2,0,1:T(8,128)} fusion(f32[4,32,128,128]{3,2,1,0:T(8,128)S(1)} %fusion.12, f32[4,32]{1,0:T(4,128)S(1)} %convert_bitcast_fusion.4, s32[4,32]{1,0:T(4,128)S(1)} %add_select_fusion), kind=kOutput, calls=%fused_computation.46 | convolution fusion | flops 805314560 | bytes 10486784 | tf_op jit(solution)/shard_map/kts,ksim->tim/dot_general | solution.py:42
  231.0 3.0 copy.34
  234.0 3.1 broadcast_multiply_fusion.2
  237.6 2.3 fusion.48
  239.9 101.7 %all-reduce.6.cloned.1.call-done = f32[32,128,128]{1,2,0:T(8,128)} async-done(((f32[32,128,128]{1,2,0:T(8,128)}), f32[32,128,128]{1,2,0:T(8,128)}) %all-reduce.6.cloned.1.call-update) | async-done | bytes 2097168 | tf_op jit(solution)/shard_map/psum | solution.py:76
  341.6 2.7 multiply_reduce_fusion.4
  345.7 2.7 multiply_reduce_fusion.3
  349.2 2.8 broadcast_multiply_fusion
  352.6 3.2 convert_bitcast_fusion.1
  355.8 1.3 collective-permute-start.5
  357.1 3.0 collective-permute-start.4
  360.2 5.3 %fusion.10 = f32[4,32,128,128]{3,2,1,0:T(8,128)S(1)} fusion(bf16[4,32,128,128]{2,3,0,1:T(8,128)(2,1)} %convert_bitcast_fusion.1, bf16[1,4,32,128,128]{4,3,2,1,0:T(8,128)(2,1)S(1)} %copy-done.5), kind=kOutput, calls=%fused_computation.10 | convolution fusion | flops 536870912 | bytes 16777216 | tf_op jit(solution)/shard_map/ksil,ksml->ksim/dot_general | solution.py:31
  365.5 12.6 %fusion.42 = f32[32,128,128]{2,0,1:T(8,128)} fusion(f32[4,32,128,128]{3,2,1,0:T(8,128)S(1)} %fusion.10, f32[4,32]{1,0:T(4,128)S(1)} %convert_bitcast_fusion.4, s32[4,32]{1,0:T(4,128)S(1)} %add_select_fusion), kind=kOutput, calls=%fused_computation.47 | convolution fusion | flops 805314560 | bytes 10486784 | tf_op jit(solution)/shard_map/kts,ksim->tim/dot_general | solution.py:42
  378.1 3.0 copy.42
  381.1 3.1 broadcast_multiply_fusion.1
  384.7 2.3 fusion.46
  387.1 101.5 %all-reduce.8.cloned.1.call-done = f32[32,128,128]{1,2,0:T(8,128)} async-done(((f32[32,128,128]{1,2,0:T(8,128)}), f32[32,128,128]{1,2,0:T(8,128)}) %all-reduce.8.cloned.1.call-update) | async-done | bytes 2097168 | tf_op jit(solution)/shard_map/psum | solution.py:76
  488.6 2.7 multiply_reduce_fusion.1
  492.7 2.7 multiply_reduce_fusion
  496.2 2.2 multiply_convert_fusion
  499.0 3.2 convert_bitcast_fusion
  502.2 1.0 copy.51
  503.2 0.8 copy.47
  503.9 6.5 %fusion.8 = f32[4,32,128,128]{3,2,1,0:T(8,128)S(1)} fusion(bf16[4,32,128,128]{2,3,0,1:T(8,128)(2,1)} %convert_bitcast_fusion, bf16[1,4,32,128,128]{4,3,2,1,0:T(8,128)(2,1)} %param.7), kind=kOutput, calls=%fused_computation.8 | convolution fusion | flops 536870912 | bytes 16777216 | tf_op jit(solution)/shard_map/ksil,ksml->ksim/dot_general | solution.py:31
  510.5 8.9 %fusion.57 = f32[4]{0:T(128)S(1)} fusion(f32[4,32,32]{2,1,0:T(8,128)S(1)} %copy.79, f32[4,32,128,128]{3,2,1,0:T(8,128)S(1)} %fusion.8, bf16[32,128,128]{2,0,1:T(8,128)(2,1)S(1)} %copy.51), kind=kOutput, calls=%fused_computation.62 | convolution fusion | flops 805314560 | bytes 9453584 | tf_op jit(solution)/shard_map/ksim,tim->kst/dot_general | solution.py:46
  (44 shorter events, 3.4 us)
Async XLA Ops:
  7.2 45.8 %all-gather.3.cloned.1.call-start = ((), (), s32[]{:S(2)}) async-start(), calls=%async_computation.3 | async-start | bytes 1179648 | tf_op jit(solution)/shard_map/all_gather | solution.py:63
  7.9 176.8 %all-reduce.4.cloned.1.call-start = ((), (), s32[]{:S(2)}) async-start(), calls=%async_computation | async-start | bytes 4194304 | tf_op jit(solution)/shard_map/psum | solution.py:76
  53.0 6.1 %copy-start.9 = (bf16[1,32,128,128]{3,2,0,1:T(8,128)(2,1)S(1)}, bf16[1,32,128,128]{3,2,0,1:T(8,128)(2,1)}, u32[]{:S(2)}) copy-start(bf16[1,32,128,128]{3,2,0,1:T(8,128)(2,1)} %all-gather.3.cloned.1.call-done) | copy-start | bytes 3145732
  54.7 26.2 %collective-permute-start.1 = (bf16[4,128,128]{1,2,0:T(8,128)(2,1)S(1)}, bf16[4,128,128]{1,2,0:T(8,128)(2,1)S(1)}, u32[]{:S(2)}, u32[]{:S(2)}) collective-permute-start(bf16[4,128,128]{1,2,0:T(8,128)(2,1)S(1)} %dynamic-slice_convert_fusion), channel_id=1, source_target_pairs={{8,0},{16,8},{24,16},{9,1},{17,9},{25,17},{10,2},{18,10},{26,18},{... | collective-permute-start | bytes 393224 | tf_op jit(solution)/shard_map/ppermute | solution.py:16
  56.0 25.1 %collective-permute-start = (bf16[4,128,128]{1,2,0:T(8,128)(2,1)S(1)}, bf16[4,128,128]{1,2,0:T(8,128)(2,1)S(1)}, u32[]{:S(2)}, u32[]{:S(2)}) collective-permute-start(bf16[4,128,128]{1,2,0:T(8,128)(2,1)S(1)} %dynamic-slice_convert_fusion), channel_id=1, source_target_pairs={{0,8},{8,16},{16,24},{1,9},{9,17},{17,25},{2,10},{10,18},{18,26},{... | collective-permute-start | bytes 393224 | tf_op jit(solution)/shard_map/ppermute | solution.py:16
  59.1 3.7 copy-start.3
  82.7 1.3 copy-start.8
  84.0 257.6 %all-reduce.6.cloned.1.call-start = ((), (), s32[]{:S(2)}) async-start(), calls=%async_computation.1 | async-start | bytes 4194304 | tf_op jit(solution)/shard_map/psum | solution.py:76
  184.7 4.2 copy-start.7
  190.8 2.8 copy-start
  193.6 152.1 %copy-start.6 = (f32[32,128,128]{1,2,0:T(8,128)}, f32[32,128,128]{1,2,0:T(8,128)S(1)}, u32[]{:S(2)}) copy-start(f32[32,128,128]{1,2,0:T(8,128)S(1)} %fusion.60) | copy-start | bytes 6291460
  193.6 7.9 %copy-start.4 = (bf16[1,4,32,128,128]{4,3,2,1,0:T(8,128)(2,1)S(1)}, bf16[1,4,32,128,128]{4,3,2,1,0:T(8,128)(2,1)}, u32[]{:S(2)}) copy-start(bf16[1,4,32,128,128]{4,3,2,1,0:T(8,128)(2,1)} %param.7) | copy-start | bytes 12582916
  197.0 40.1 %collective-permute-start.3 = (bf16[4,128,128]{1,2,0:T(8,128)(2,1)S(1)}, bf16[4,128,128]{1,2,0:T(8,128)(2,1)S(1)}, u32[]{:S(2)}, u32[]{:S(2)}) collective-permute-start(bf16[4,128,128]{1,2,0:T(8,128)(2,1)S(1)} %dynamic-slice_convert_fusion.2), channel_id=1, source_target_pairs={{8,0},{16,8},{24,16},{9,1},{17,9},{25,17},{10,2},{18,10},{26,18},{... | collective-permute-start | bytes 393224 | tf_op jit(solution)/shard_map/ppermute | solution.py:16
  198.5 38.9 %collective-permute-start.2 = (bf16[4,128,128]{1,2,0:T(8,128)(2,1)S(1)}, bf16[4,128,128]{1,2,0:T(8,128)(2,1)S(1)}, u32[]{:S(2)}, u32[]{:S(2)}) collective-permute-start(bf16[4,128,128]{1,2,0:T(8,128)(2,1)S(1)} %dynamic-slice_convert_fusion.2), channel_id=1, source_target_pairs={{0,8},{8,16},{16,24},{1,9},{9,17},{17,25},{2,10},{10,18},{18,26},{... | collective-permute-start | bytes 393224 | tf_op jit(solution)/shard_map/ppermute | solution.py:16
  239.9 248.7 %all-reduce.8.cloned.1.call-start = ((), (), s32[]{:S(2)}) async-start(), calls=%async_computation.2 | async-start | bytes 4194304 | tf_op jit(solution)/shard_map/psum | solution.py:76
  349.2 3.5 copy-start.1
  352.6 7.6 %copy-start.5 = (bf16[1,4,32,128,128]{4,3,2,1,0:T(8,128)(2,1)S(1)}, bf16[1,4,32,128,128]{4,3,2,1,0:T(8,128)(2,1)}, u32[]{:S(2)}) copy-start(bf16[1,4,32,128,128]{4,3,2,1,0:T(8,128)(2,1)} %param.7) | copy-start | bytes 12582916
  355.8 28.4 %collective-permute-start.5 = (bf16[4,128,128]{1,2,0:T(8,128)(2,1)S(1)}, bf16[4,128,128]{1,2,0:T(8,128)(2,1)S(1)}, u32[]{:S(2)}, u32[]{:S(2)}) collective-permute-start(bf16[4,128,128]{1,2,0:T(8,128)(2,1)S(1)} %dynamic-slice_convert_fusion.1), channel_id=1, source_target_pairs={{8,0},{16,8},{24,16},{9,1},{17,9},{25,17},{10,2},{18,10},{26,18},{... | collective-permute-start | bytes 393224 | tf_op jit(solution)/shard_map/ppermute | solution.py:16
  357.1 27.4 %collective-permute-start.4 = (bf16[4,128,128]{1,2,0:T(8,128)(2,1)S(1)}, bf16[4,128,128]{1,2,0:T(8,128)(2,1)S(1)}, u32[]{:S(2)}, u32[]{:S(2)}) collective-permute-start(bf16[4,128,128]{1,2,0:T(8,128)(2,1)S(1)} %dynamic-slice_convert_fusion.1), channel_id=1, source_target_pairs={{0,8},{8,16},{16,24},{1,9},{9,17},{17,25},{2,10},{10,18},{18,26},{... | collective-permute-start | bytes 393224 | tf_op jit(solution)/shard_map/ppermute | solution.py:16
  496.2 2.8 copy-start.2
Sparse Core Ops, SparseCore 0:
  10.1 42.8 all-gather.2
  84.1 100.4 all-reduce.3
  240.0 101.5 all-reduce.5
  387.1 101.4 all-reduce.7
where the time goes:
time: 536 us; the launch traced here: 527 us
  waiting for transfers between devices  348 us (65%)
  matrix products  97.8 us (18%)
  other arithmetic  32.1 us (6%)
  between operations  20.7 us (4%)
  local copies, waits for them, and re-layouts  14.7 us (3%)
  starting transfers between devices  13.3 us (2%)
    psum x3, waiting for transfers between devices, shards(): applied = lax.psum(partial_terms + placed, 'op')  304 us
    dot_general x3, matrix products, place_terms(): return jnp.einsum('kts,ksim->tim', table, products, precision=precise)  48.2 us
    all_gather x1, waiting for transfers between devices, shards(): lax.all_gather(own_start, 'op', axis=0, tiled=True).astype(jnp.float32)  43.6 us
    dot_general x4, matrix products, term_products(): jnp.einsum('ksil,ksml->ksim', half, rights, preferred_element_type=jnp.fl...  20.2 us
    dot_general x4, matrix products, term_products(): jnp.einsum('ksij,sjl->ksil', lefts, state_low, preferred_element_type=jnp...  13.4 us
    ppermute x6, starting transfers between devices, shifted(): return lax.ppermute(block, axis, route)  13.1 us
  transfers between devices with their start and end apart: 10, of which 4 were waited for; matrix products, arithmetic and copies ran while one was open for 16% of the time, Pallas kernels for 0%

commit v1 on v0

v1 whole, which is shorter than its diff:
```python
import functools

import jax
import jax.numpy as jnp
from jax import lax
from jax.experimental import pallas as pl
from jax.experimental.pallas import tpu as pltpu
from jax.sharding import PartitionSpec as P

ITERS = 3
GROUP = 8
TAIL = 16
STRIP = 64

step_size = 0.3
low_type = jnp.bfloat16
wide_type = jnp.float32
VMEM = pl.BlockSpec(memory_space=pltpu.VMEM)
SMEM = pl.BlockSpec(memory_space=pltpu.SMEM)


def params(megabytes):
    return pltpu.CompilerParams(vmem_limit_bytes=megabytes << 20)


def traded(block, distance):
    route = [(i, i ^ distance) for i in range(lax.axis_size("op"))]
    return lax.ppermute(block, "op", route)


def shifted(block, distance):
    devices = range(lax.axis_size("seg"))
    route = [(i - distance, i) for i in devices if i - distance in devices]
    return lax.ppermute(block, "seg", route)


def gathered(block):
    devices = lax.axis_size("op")
    held = [block] + [None] * (devices - 1)
    for distance in range(devices - 2, 0, -2):
        held[distance] = traded(block, distance)
    held[1] = traded(block, 1)
    for distance in range(2, devices, 2):
        held[distance + 1] = traded(held[distance], 1)
    return held


def plan_kernel(blocks_dev, me_ref, shifts_ref, active_ref, pair_ref, source_ref, target_ref, term_ref, count_ref):
    terms, blocks_all = active_ref.shape
    me = me_ref[0]

    def slot(block):
        return ((block // blocks_dev) ^ me) * blocks_dev + block % blocks_dev

    def one(flat, found):
        term = flat // blocks_all
        block = flat % blocks_all
        target = block + shifts_ref[0, term]
        target = jnp.where(target >= blocks_all, target - blocks_all, target)
        pair_ref[found] = flat
        source_ref[found] = slot(block)
        target_ref[found] = slot(target)
        term_ref[found] = term
        return found + active_ref[term, block]

    found = lax.fori_loop(0, terms * blocks_all, one, 0)
    count_ref[0] = found
    for extra in range(GROUP):
        pair_ref[found + extra] = 0
        source_ref[found + extra] = 0
        target_ref[found + extra] = blocks_all
        term_ref[found + extra] = terms


def make_plan(me, shifts, active, blocks_dev):
    terms, blocks_all = active.shape
    entries = jax.ShapeDtypeStruct((terms * blocks_all + GROUP,), jnp.int32)
    return pl.pallas_call(
        functools.partial(plan_kernel, blocks_dev),
        out_shape=[entries] * 4 + [jax.ShapeDtypeStruct((1,), jnp.int32)],
        in_specs=[SMEM] * 3,
        out_specs=[SMEM] * 5,
    )(me, shifts, active)


def pair_product(index, pair_ref, source_ref, left_ref, right_ref, low_ref):
    pair = pair_ref[index]
    half = jnp.dot(left_ref[pair], low_ref[source_ref[index]], preferred_element_type=wide_type).astype(low_type)
    return lax.dot_general(half, right_ref[pair], (((1,), (1,)), ((), ())), preferred_element_type=wide_type)


def fill_low(first, chunk_refs, own_ref, old_refs, low_ref, fresh_ref, count):
    rows = own_ref.shape[0]
    width = own_ref.shape[1]
    if first:
        for place, chunk_ref in enumerate(chunk_refs):
            blocks = rows // width
            low_ref[place * blocks : (place + 1) * blocks] = chunk_ref[...].reshape(blocks, width, width)
        return
    tails = sum(ref[rows:, :].astype(wide_type) for ref in chunk_refs)

    def total(which):
        return tails[3 * which : 3 * which + 1] + tails[3 * which + 1 : 3 * which + 2] + tails[3 * which + 2 : 3 * which + 3]

    squares, cross, applied_squares = total(0), total(1), total(2)
    rho = cross / squares
    length = squares + step_size * step_size * (applied_squares - rho * cross)
    scale = jnp.sqrt(count / length)
    keep = scale * (1.0 + step_size * rho)
    take = scale * step_size
    for place, chunk_ref in enumerate(chunk_refs):
        source = own_ref if place == 0 else chunk_ref

        def strip(part, carried, place=place, source=source):
            start = pl.multiple_of(part * STRIP, STRIP)
            if len(old_refs) == 1:
                old = old_refs[0][pl.ds(place * rows + start, STRIP), :]
            else:
                old = old_refs[place][pl.ds(start, STRIP), :].astype(wide_type)
            new = keep * old - take * source[pl.ds(start, STRIP), :].astype(wide_type)
            if fresh_ref is not None:
                fresh_ref[pl.ds(place * rows + start, STRIP), :] = new
            low = new.astype(low_type)
            at = place * rows + start
            low_ref[at // width, pl.ds(pl.multiple_of(at % width, STRIP), STRIP), :] = low
            return carried

        lax.fori_loop(0, rows // STRIP, strip, 0, unroll=True)


def apply_kernel(first, devices, olds, count, term_scale, *refs):
    pair_ref, source_ref, target_ref, count_ref, left_ref, right_ref = refs[:6]
    chunk_refs = refs[6 : 6 + devices]
    own_ref = refs[6 + devices]
    old_refs = refs[7 + devices : 7 + devices + olds]
    rest = refs[7 + devices + olds :]
    half = devices // 2
    send_refs, keep_refs = rest[:half], rest[half : 2 * half]
    rest = rest[2 * half :]
    if first:
        fresh_ref = None
    else:
        fresh_ref, own_low_ref, own_wide_ref = rest[:3]
        rest = rest[3:]
    low_ref, sum_ref = rest
    rows, width = own_ref.shape
    blocks = rows // width
    fill_low(first, chunk_refs, own_ref, old_refs, low_ref, fresh_ref, count)
    if not first:
        own_low_ref[...] = low_ref[:blocks].reshape(rows, width)
        own_wide_ref[...] = fresh_ref[:rows, :]
    sum_ref[...] = jnp.zeros_like(sum_ref)

    def group(index, carried):
        products = [
            pair_product(index * GROUP + inner, pair_ref, source_ref, left_ref, right_ref, low_ref)
            for inner in range(GROUP)
        ]
        for inner, product in enumerate(products):
            sum_ref[target_ref[index * GROUP + inner]] += product
        return carried

    lax.fori_loop(0, (count_ref[0] + GROUP - 1) // GROUP, group, 0)
    for place in range(half):
        keep_at = 2 * place * blocks
        keep_refs[place][...] = sum_ref[keep_at : keep_at + blocks].reshape(rows, width) * term_scale
        send_at = keep_at + blocks
        send_refs[place][...] = (sum_ref[send_at : send_at + blocks].reshape(rows, width) * term_scale).astype(low_type)


def apply_terms(plan, lefts, rights, chunks, own, olds, count, term_scale):
    first = not olds
    devices = len(chunks)
    rows, width = own.shape
    total = devices * rows
    pairs, sources, targets, _, found = plan
    outs = [jax.ShapeDtypeStruct((rows, width), low_type)] * (devices // 2)
    outs += [jax.ShapeDtypeStruct((rows, width), wide_type)] * (devices // 2)
    if not first:
        outs += [
            jax.ShapeDtypeStruct((total, width), wide_type),
            jax.ShapeDtypeStruct((rows, width), low_type),
            jax.ShapeDtypeStruct((rows, width), wide_type),
        ]
    pairs_all = lefts.shape[0]
    return pl.pallas_call(
        functools.partial(apply_kernel, first, devices, len(olds), count, term_scale),
        out_shape=outs,
        in_specs=[SMEM] * 4 + [VMEM] * (3 + devices + len(olds)),
        out_specs=[VMEM] * len(outs),
        scratch_shapes=[
            pltpu.VMEM((total // width, width, width), low_type),
            pltpu.VMEM((total // width + 1, width, width), wide_type),
        ],
        compiler_params=params(32),
        cost_estimate=pl.CostEstimate(flops=2 * pairs_all * width**3, bytes_accessed=4 << 20, transcendentals=0),
    )(pairs, sources, targets, found, lefts, rights, *chunks, own, *olds)


def values_kernel(devices, olds, count, *refs):
    pair_ref, source_ref, target_ref, term_ref, count_ref, left_ref, right_ref = refs[:7]
    chunk_refs = refs[7 : 7 + devices]
    own_ref = refs[7 + devices]
    old_refs = refs[8 + devices : 8 + devices + olds]
    state_ref, value_ref, low_ref, sum_ref = refs[8 + devices + olds :]
    rows, width = own_ref.shape
    blocks = rows // width
    fill_low(False, chunk_refs, own_ref, old_refs, low_ref, None, count)
    state_ref[...] = low_ref[:blocks].reshape(rows, width)
    low_ref[devices * blocks] = jnp.zeros((width, width), low_type)
    sum_ref[...] = jnp.zeros_like(sum_ref)

    def group(index, carried):
        products = [
            pair_product(index * GROUP + inner, pair_ref, source_ref, left_ref, right_ref, low_ref)
            for inner in range(GROUP)
        ]
        for inner, product in enumerate(products):
            place = index * GROUP + inner
            target = low_ref[target_ref[place]].astype(wide_type)
            folded = (product * target).reshape(width // 8, 8, width).sum(axis=0)
            sum_ref[term_ref[place]] += folded
        return carried

    lax.fori_loop(0, (count_ref[0] + GROUP - 1) // GROUP, group, 0)
    terms = value_ref.shape[0]
    for term in range(terms):
        value_ref[term : term + 1, :] = jnp.full((1, width), jnp.sum(sum_ref[term]) * (1.0 / count))


def term_values(plan, lefts, rights, chunks, own, olds, count, terms):
    devices = len(chunks)
    rows, width = own.shape
    total = devices * rows
    pairs_all = lefts.shape[0]
    return pl.pallas_call(
        functools.partial(values_kernel, devices, len(olds), count),
        out_shape=[jax.ShapeDtypeStruct((rows, width), low_type), jax.ShapeDtypeStruct((terms, width), wide_type)],
        in_specs=[SMEM] * 5 + [VMEM] * (3 + devices + len(olds)),
        out_specs=[VMEM] * 2,
        scratch_shapes=[
            pltpu.VMEM((total // width + 1, width, width), low_type),
            pltpu.VMEM((terms + 1, 8, width), wide_type),
        ],
        compiler_params=params(32),
        cost_estimate=pl.CostEstimate(flops=2 * pairs_all * width**3, bytes_accessed=4 << 20, transcendentals=0),
    )(*plan, lefts, rights, *chunks, own, *olds)


def coupling_kernel(own_ref, before_ref, after_ref, out_ref):
    rows, width = own_ref.shape
    for block in range(rows // width):
        at = pl.ds(block * width, width)
        gram = sum(
            lax.dot_general(ref[at, :], ref[at, :], (((0,), (0,)), ((), ())), preferred_element_type=wide_type)
            for ref in (before_ref, after_ref)
        )
        out_ref[at, :] = jnp.dot(
            own_ref[at, :], gram, precision=lax.Precision.HIGHEST, preferred_element_type=wide_type
        ) * (0.5 / width)


def coupling(own, before, after):
    rows, width = own.shape
    return pl.pallas_call(
        coupling_kernel,
        out_shape=jax.ShapeDtypeStruct(own.shape, wide_type),
        in_specs=[VMEM] * 3,
        out_specs=VMEM,
        cost_estimate=pl.CostEstimate(flops=16 * rows * width**2, bytes_accessed=rows * width * 12, transcendentals=0),
    )(own, before, after)


def total_kernel(parts, own_ref, coupled_ref, *refs):
    part_refs, (applied_ref, sent_ref) = refs[:parts], refs[parts:]
    rows, width = own_ref.shape
    sums = [jnp.zeros((8, width), wide_type)] * 3
    for start in range(0, rows, STRIP):
        at = pl.ds(start, STRIP)
        applied = coupled_ref[at, :] + sum(ref[at, :].astype(wide_type) for ref in part_refs)
        own = own_ref[at, :].astype(wide_type)
        applied_ref[at, :] = applied
        sent_ref[at, :] = applied.astype(low_type)
        for which, product in enumerate((own * own, own * applied, applied * applied)):
            sums[which] = sums[which] + product.reshape(STRIP // 8, 8, width).sum(axis=0)
    row = lax.broadcasted_iota(jnp.int32, (TAIL, width), 0)
    tail = jnp.zeros((TAIL, width), wide_type)
    for which in range(3):
        rest = jnp.full((TAIL, width), jnp.sum(sums[which]))
        for digit in range(3):
            rounded = rest.astype(low_type).astype(wide_type)
            tail = jnp.where(row == 3 * which + digit, rounded, tail)
            rest = rest - rounded
    sent_ref[rows:, :] = tail.astype(low_type)


def total_applied(own, coupled, parts):
    rows, width = own.shape
    return pl.pallas_call(
        functools.partial(total_kernel, len(parts)),
        out_shape=[jax.ShapeDtypeStruct((rows, width), wide_type), jax.ShapeDtypeStruct((rows + TAIL, width), low_type)],
        in_specs=[VMEM] * (2 + len(parts)),
        out_specs=[VMEM] * 2,
        cost_estimate=pl.CostEstimate(flops=10 * rows * width, bytes_accessed=rows * width * 16, transcendentals=0),
    )(own, coupled, *parts)


def shards(psi_start, left_ops, right_ops, shifts, active):
    devices = lax.axis_size("op")
    terms, blocks_all, width = left_ops.shape[1:4]
    blocks_dev = psi_start.shape[1]
    rows = blocks_dev * width
    count = float(blocks_all * width * width)
    term_scale = 1.0 / (terms * devices)
    lefts = pltpu.with_memory_space_constraint(left_ops.reshape(terms * blocks_all, width, width), pltpu.VMEM)
    rights = pltpu.with_memory_space_constraint(right_ops.reshape(terms * blocks_all, width, width), pltpu.VMEM)
    own_low = psi_start.reshape(rows, width)
    own_wide = own_low
    me = lax.axis_index("op").astype(jnp.int32).reshape(1)
    plan = make_plan(me, shifts, active[0], blocks_dev)
    chunks = gathered(own_low)
    own_source = own_low
    olds = []
    for sweep_index in range(ITERS):
        outs = apply_terms(plan, lefts, rights, chunks, own_source, olds, count, term_scale)
        half = devices // 2
        sends, keeps = outs[:half], outs[half : 2 * half]
        if olds:
            fresh, own_low, own_wide = outs[2 * half :]
            olds = [fresh]
        else:
            olds = chunks
        before, after = shifted(own_low, 1), shifted(own_low, -1)
        parts = [keeps[0]]
        for place in range(half - 1, -1, -1):
            arrived = traded(sends[place], 1)
            if place:
                joined = (keeps[place] + arrived.astype(wide_type)).astype(low_type)
                parts.append(traded(joined, 2 * place))
            else:
                parts.append(arrived)
        coupled = coupling(own_wide.astype(wide_type), before, after)
        own_source, sent = total_applied(own_wide, coupled, parts)
        chunks = gathered(sent)
    state, values = term_values(plan, lefts, rights, chunks, own_source, olds, count, terms)
    return state.reshape(psi_start.shape), values[:, 0].reshape(shifts.shape)


def solution(mesh):
    return jax.shard_map(
        shards,
        mesh=mesh,
        in_specs=(
            P("seg", "op", None, None),
            P("seg", "op", None, None, None),
            P("seg", "op", None, None, None),
            P("seg", "op"),
            P("seg", "op", None),
        ),
        out_specs=(P("seg", "op", None, None), P("seg", "op")),
        check_vma=False,
    )
```

time: 536 us -> 236 us (0.44); the launches traced: 527 us -> 236 us
  waiting for transfers between devices: 348 us -> 65.6 us
  matrix products: 97.8 us -> 0 us
  starting transfers between devices: 13.3 us -> 81 us
  Pallas kernels: 0 us -> 52.5 us
  other arithmetic: 32.1 us -> 1.03 us
  local copies, waits for them, and re-layouts: 14.7 us -> 34.9 us
  between operations: 20.7 us -> 1.05 us
    psum x3 -> x0, waiting for transfers between devices: 304 us -> none  [shards(): applied = lax.psum(partial_terms + placed, 'op')]
    dot_general x21 -> x0, matrix products: 97.8 us -> none  [the longest x3 48.2 us: place_terms(): return jnp.einsum('kts,ksim->tim', table, products, precision=precise)]
    ppermute x6 -> x55, starting transfers between devices: 13.1 us -> 81 us  [the longest x49 67.9 us: traded(): return lax.ppermute(block, 'op', route)]
    ppermute x6 -> x55, waiting for transfers between devices: 0.02 us -> 65.6 us  [the longest x49 65.6 us: traded(): return lax.ppermute(block, 'op', route)]
    pallas_call x0 -> x11, Pallas kernels: none -> 52.5 us  [the longest x3 24.9 us: apply_terms(): pl.pallas_call(functools.partial(apply_kernel, first, devices, len(olds),...]
    all_gather x1 -> x0, waiting for transfers between devices: 43.6 us -> none  [shards(): lax.all_gather(own_start, 'op', axis=0, tiled=True).astype(jnp.float32)]
    unnamed x21 -> x96, local copies, waits for them, and re-layouts: 3.25 us -> 34.2 us
    reduce_sum x6 -> x0, other arithmetic: 15 us -> none  [the longest x3 8.36 us: shards(): rho = jnp.sum(full_state * applied) / jnp.sum(full_state * full_state)]
  transfers between devices with their start and end apart: 10 -> 55, of which waited for: 4 -> 22; matrix products, arithmetic and copies ran while one was open for 16% -> 0% of each run, Pallas kernels for 0% -> 5%
where the time goes in v1:
time: 236 us
  starting transfers between devices  81 us (34%)
  waiting for transfers between devices  65.6 us (28%)
  Pallas kernels  52.5 us (22%)
  local copies, waits for them, and re-layouts  34.9 us (15%)
    ppermute x49, starting transfers between devices, traded(): return lax.ppermute(block, 'op', route)  67.9 us
    ppermute x49, waiting for transfers between devices, traded(): return lax.ppermute(block, 'op', route)  65.6 us
    unnamed x96, local copies, waits for them, and re-layouts  34.2 us
    pallas_call x3, Pallas kernels, apply_terms(): pl.pallas_call(functools.partial(apply_kernel, first, devices, len(olds),...  24.9 us
    ppermute x6, starting transfers between devices, shifted(): return lax.ppermute(block, 'seg', route)  13.1 us
    pallas_call x1, Pallas kernels, term_values(): pl.pallas_call(functools.partial(values_kernel, devices, len(olds), count...  8.79 us
    pallas_call x3, Pallas kernels, coupling(): pl.pallas_call(coupling_kernel, out_shape=jax.ShapeDtypeStruct(own.shape,...  7.42 us
    pallas_call x3, Pallas kernels, total_applied(): pl.pallas_call(functools.partial(total_kernel, len(parts)), out_shape=[ja...  6.63 us
  transfers between devices with their start and end apart: 55, of which 22 were waited for; matrix products, arithmetic and copies ran while one was open for 0% of the time, Pallas kernels for 5%

profile of v1, /device:TPU:0, one launch (start us, length us, event | category | flops | bytes accessed | tf_op | source)
XLA Modules:
  0.0 236.0 jit_solution(15393824202293907098)
XLA Ops:
  0.6 5.1 %collective-permute-start.7 = (bf16[512,128]{1,0:T(8,128)(2,1)}, bf16[512,128]{1,0:T(8,128)(2,1)S(1)}, u32[]{:S(2)}, u32[]{:S(2)}) collective-permute-start(bf16[512,128]{1,0:T(8,128)(2,1)} %bitcast.16), channel_id=1, source_target_pairs={{0,6},{1,7},{2,4},{3,5},{4,2},{5,3},{6,0},{7,1},{8,14},{9,15},{10,... | collective-permute-start | bytes 393224 | tf_op jit(solution)/shard_map/ppermute | solution.py:28
  8.0 2.4 %collective-permute-done.7.refs_12_.refs_21_ = bf16[512,128]{1,0:T(8,128)(2,1)S(1)} collective-permute-done((bf16[512,128]{1,0:T(8,128)(2,1)}, bf16[512,128]{1,0:T(8,128)(2,1)S(1)}, u32[]{:S(2)}, u32[]{:S(2)}) %collective-permute-start.7) | collective-permute-done | bytes 131104 | tf_op jit(solution)/shard_map/ppermute | solution.py:28
  12.1 5.0 %collective-permute-done.5.refs_10_.refs_19_ = bf16[512,128]{1,0:T(8,128)(2,1)S(1)} collective-permute-done((bf16[512,128]{1,0:T(8,128)(2,1)}, bf16[512,128]{1,0:T(8,128)(2,1)S(1)}, u32[]{:S(2)}, u32[]{:S(2)}) %collective-permute-start.5) | collective-permute-done | bytes 131104 | tf_op jit(solution)/shard_map/ppermute | solution.py:28
  19.1 4.8 %shard_map.68 = (s32[136]{0:T(256)}, s32[136]{0:T(256)}, s32[136]{0:T(256)}, s32[136]{0:T(256)}, s32[1]{0:T(128)}) custom-call(s32[1]{0:T(128)} %bitcast.me_ref, s32[1,4]{1,0:T(1,128)} %shifts_ref.1, s32[4,32]{1,0:T(4,128)} %bitcast.26), custom_call_target="tpu_custom_call" | custom-call | tf_op jit(solution)/shard_map/pallas_call | solution.py:78
  24.4 2.2 copy-done
  26.6 2.2 copy-done.4
  31.7 8.1 %shard_map.70 = (bf16[512,128]{1,0:T(8,128)(2,1)S(1)}, bf16[512,128]{1,0:T(8,128)(2,1)S(1)}, bf16[512,128]{1,0:T(8,128)(2,1)S(1)}, bf16[512,128]{1,0:T(8,128)(2,...) custom-call(s32[136]{0:T(256)S(1)} %copy-done.23, ...), custom_call_target="tpu_custom_call" | custom-call | flops 536870912 | bytes 4194304 | tf_op jit(solution)/shard_map/pallas_call | solution.py:186
  41.9 3.0 %collective-permute-start = (bf16[512,128]{1,0:T(8,128)(2,1)S(1)}, bf16[512,128]{1,0:T(8,128)(2,1)S(1)}, u32[]{:S(2)}, u32[]{:S(2)}) collective-permute-start(bf16[512,128]{1,0:T(8,128)(2,1)S(1)} %bitcast.24), channel_id=1, source_target_pairs={{0,8},{8,16},{16,24},{1,9},{9,17},{17,25},{2,10},{10,18},{18,26},{... | collective-permute-start | bytes 393224 | tf_op jit(solution)/shard_map/ppermute | solution.py:34
  50.0 4.4 %collective-permute-start.10 = (bf16[512,128]{1,0:T(8,128)(2,1)S(1)}, bf16[512,128]{1,0:T(8,128)(2,1)S(1)}, u32[]{:S(2)}, u32[]{:S(2)}) collective-permute-start(bf16[512,128]{1,0:T(8,128)(2,1)S(1)} %add_convert_fusion.8), channel_id=1, source_target_pairs={{0,6},{1,7},{2,4},{3,5},{4,2},{5,3},{6,0},{7,1},{8,14},{9,15},{10,... | collective-permute-start | bytes 393224 | tf_op jit(solution)/shard_map/ppermute | solution.py:28
  59.3 2.5 %shard_map.69.coupled_ref = f32[512,128]{1,0:T(8,128)} custom-call(f32[512,128]{1,0:T(8,128)} %bitcast_convert_fusion.own_ref, bf16[512,128]{1,0:T(8,128)(2,1)} %copy-done.45, bf16[512,128]{1,0:T(8,128)(2,1)} %copy-done.42), custom_call_target="tpu_custom_call" | custom-call | flops 134217728 | bytes 786432 | tf_op jit(solution)/shard_map/pallas_call | solution.py:265
  61.8 4.2 %collective-permute-done.12.refs_2_ = bf16[512,128]{1,0:T(8,128)(2,1)S(1)} collective-permute-done((bf16[512,128]{1,0:T(8,128)(2,1)S(1)}, bf16[512,128]{1,0:T(8,128)(2,1)S(1)}, u32[]{:S(2)}, u32[]{:S(2)}) %collective-permute-start.12) | collective-permute-done | bytes 131104 | tf_op jit(solution)/shard_map/ppermute | solution.py:28
  66.7 2.2 shard_map.71
  70.3 2.9 %collective-permute-start.17 = (bf16[528,128]{1,0:T(8,128)(2,1)}, bf16[528,128]{1,0:T(8,128)(2,1)S(1)}, u32[]{:S(2)}, u32[]{:S(2)}) collective-permute-start(bf16[528,128]{1,0:T(8,128)(2,1)} %get-tuple-element.58.refs_6_), channel_id=1, source_target_pairs={{0,2},{1,3},{2,0},{3,1},{4,6},{5,7},{6,4},{7,5},{8,10},{9,11},{10,... | collective-permute-start | bytes 405512 | tf_op jit(solution)/shard_map/ppermute | solution.py:28
  73.7 3.7 %collective-permute-done.21.refs_12_ = bf16[528,128]{1,0:T(8,128)(2,1)S(1)} collective-permute-done((bf16[528,128]{1,0:T(8,128)(2,1)}, bf16[528,128]{1,0:T(8,128)(2,1)S(1)}, u32[]{:S(2)}, u32[]{:S(2)}) %collective-permute-start.21) | collective-permute-done | bytes 135200 | tf_op jit(solution)/shard_map/ppermute | solution.py:28
  77.9 3.9 %collective-permute-done.19.refs_10_ = bf16[528,128]{1,0:T(8,128)(2,1)S(1)} collective-permute-done((bf16[528,128]{1,0:T(8,128)(2,1)}, bf16[528,128]{1,0:T(8,128)(2,1)S(1)}, u32[]{:S(2)}, u32[]{:S(2)}) %collective-permute-start.19) | collective-permute-done | bytes 135200 | tf_op jit(solution)/shard_map/ppermute | solution.py:28
  83.8 4.4 %collective-permute-done.20.refs_11_ = bf16[528,128]{1,0:T(8,128)(2,1)S(1)} collective-permute-done((bf16[528,128]{1,0:T(8,128)(2,1)S(1)}, bf16[528,128]{1,0:T(8,128)(2,1)S(1)}, u32[]{:S(2)}, u32[]{:S(2)}) %collective-permute-start.20) | collective-permute-done | bytes 135200 | tf_op jit(solution)/shard_map/ppermute | solution.py:28
  90.2 2.2 copy-done.1
  92.4 2.2 copy-done.5
  96.4 8.4 %shard_map.72 = (bf16[512,128]{1,0:T(8,128)(2,1)S(1)}, bf16[512,128]{1,0:T(8,128)(2,1)S(1)}, bf16[512,128]{1,0:T(8,128)(2,1)S(1)}, bf16[512,128]{1,0:T(8,128)(2,...) custom-call(s32[136]{0:T(256)S(1)} %copy-done.24, ...), custom_call_target="tpu_custom_call" | custom-call | flops 536870912 | bytes 4194304 | tf_op jit(solution)/shard_map/pallas_call | solution.py:186
  107.7 3.0 %collective-permute-start.23 = (bf16[512,128]{1,0:T(8,128)(2,1)S(1)}, bf16[512,128]{1,0:T(8,128)(2,1)S(1)}, u32[]{:S(2)}, u32[]{:S(2)}) collective-permute-start(bf16[512,128]{1,0:T(8,128)(2,1)S(1)} %get-tuple-element.61), channel_id=1, source_target_pairs={{0,8},{8,16},{16,24},{1,9},{9,17},{17,25},{2,10},{10,18},{18,26},{... | collective-permute-start | bytes 393224 | tf_op jit(solution)/shard_map/ppermute | solution.py:34
  114.8 2.4 %collective-permute-done.27 = bf16[512,128]{1,0:T(8,128)(2,1)S(1)} collective-permute-done((bf16[512,128]{1,0:T(8,128)(2,1)S(1)}, bf16[512,128]{1,0:T(8,128)(2,1)S(1)}, u32[]{:S(2)}, u32[]{:S(2)}) %collective-permute-start.27) | collective-permute-done | bytes 131104 | tf_op jit(solution)/shard_map/ppermute | solution.py:28
  117.2 3.1 %collective-permute-start.26 = (bf16[512,128]{1,0:T(8,128)(2,1)S(1)}, bf16[512,128]{1,0:T(8,128)(2,1)S(1)}, u32[]{:S(2)}, u32[]{:S(2)}) collective-permute-start(bf16[512,128]{1,0:T(8,128)(2,1)S(1)} %add_convert_fusion.5), channel_id=1, source_target_pairs={{0,6},{1,7},{2,4},{3,5},{4,2},{5,3},{6,0},{7,1},{8,14},{9,15},{10,... | collective-permute-start | bytes 393224 | tf_op jit(solution)/shard_map/ppermute | solution.py:28
  120.5 3.3 %collective-permute-start.30 = (bf16[512,128]{1,0:T(8,128)(2,1)S(1)}, bf16[512,128]{1,0:T(8,128)(2,1)S(1)}, u32[]{:S(2)}, u32[]{:S(2)}) collective-permute-start(bf16[512,128]{1,0:T(8,128)(2,1)S(1)} %add_convert_fusion.3), channel_id=1, source_target_pairs={{0,2},{1,3},{2,0},{3,1},{4,6},{5,7},{6,4},{7,5},{8,10},{9,11},{10,... | collective-permute-start | bytes 393224 | tf_op jit(solution)/shard_map/ppermute | solution.py:28
  124.5 2.5 %shard_map.73.coupled_ref = f32[512,128]{1,0:T(8,128)} custom-call(f32[512,128]{1,0:T(8,128)} %copy-done.12, bf16[512,128]{1,0:T(8,128)(2,1)} %copy-done.46, bf16[512,128]{1,0:T(8,128)(2,1)} %copy-done.43), custom_call_target="tpu_custom_call" | custom-call | flops 134217728 | bytes 786432 | tf_op jit(solution)/shard_map/pallas_call | solution.py:265
  126.9 2.8 %collective-permute-done.28.refs_2_ = bf16[512,128]{1,0:T(8,128)(2,1)S(1)} collective-permute-done((bf16[512,128]{1,0:T(8,128)(2,1)S(1)}, bf16[512,128]{1,0:T(8,128)(2,1)S(1)}, u32[]{:S(2)}, u32[]{:S(2)}) %collective-permute-start.28) | collective-permute-done | bytes 131104 | tf_op jit(solution)/shard_map/ppermute | solution.py:28
  130.5 2.2 shard_map.74
  132.7 2.1 collective-permute-start.37
  134.8 2.3 collective-permute-start.33
  138.2 3.1 %collective-permute-done.37.refs_12_ = bf16[528,128]{1,0:T(8,128)(2,1)S(1)} collective-permute-done((bf16[528,128]{1,0:T(8,128)(2,1)}, bf16[528,128]{1,0:T(8,128)(2,1)S(1)}, u32[]{:S(2)}, u32[]{:S(2)}) %collective-permute-start.37) | collective-permute-done | bytes 135200 | tf_op jit(solution)/shard_map/ppermute | solution.py:28
  142.4 3.6 %collective-permute-done.35.refs_10_ = bf16[528,128]{1,0:T(8,128)(2,1)S(1)} collective-permute-done((bf16[528,128]{1,0:T(8,128)(2,1)}, bf16[528,128]{1,0:T(8,128)(2,1)S(1)}, u32[]{:S(2)}, u32[]{:S(2)}) %collective-permute-start.35) | collective-permute-done | bytes 135200 | tf_op jit(solution)/shard_map/ppermute | solution.py:28
  148.1 4.4 %collective-permute-done.36.refs_11_ = bf16[528,128]{1,0:T(8,128)(2,1)S(1)} collective-permute-done((bf16[528,128]{1,0:T(8,128)(2,1)S(1)}, bf16[528,128]{1,0:T(8,128)(2,1)S(1)}, u32[]{:S(2)}, u32[]{:S(2)}) %collective-permute-start.36) | collective-permute-done | bytes 135200 | tf_op jit(solution)/shard_map/ppermute | solution.py:28
  154.4 2.2 copy-done.2
  156.6 2.2 copy-done.6
  160.7 8.4 %shard_map.75 = (bf16[512,128]{1,0:T(8,128)(2,1)S(1)}, bf16[512,128]{1,0:T(8,128)(2,1)S(1)}, bf16[512,128]{1,0:T(8,128)(2,1)S(1)}, bf16[512,128]{1,0:T(8,128)(2,...) custom-call(s32[136]{0:T(256)S(1)} %copy-done.24, ...), custom_call_target="tpu_custom_call" | custom-call | flops 536870912 | bytes 4194304 | tf_op jit(solution)/shard_map/pallas_call | solution.py:186
  173.6 3.0 %collective-permute-start.39 = (bf16[512,128]{1,0:T(8,128)(2,1)S(1)}, bf16[512,128]{1,0:T(8,128)(2,1)S(1)}, u32[]{:S(2)}, u32[]{:S(2)}) collective-permute-start(bf16[512,128]{1,0:T(8,128)(2,1)S(1)} %get-tuple-element.74), channel_id=1, source_target_pairs={{0,8},{8,16},{16,24},{1,9},{9,17},{17,25},{2,10},{10,18},{18,26},{... | collective-permute-start | bytes 393224 | tf_op jit(solution)/shard_map/ppermute | solution.py:34
  180.3 2.8 %collective-permute-done.43 = bf16[512,128]{1,0:T(8,128)(2,1)S(1)} collective-permute-done((bf16[512,128]{1,0:T(8,128)(2,1)S(1)}, bf16[512,128]{1,0:T(8,128)(2,1)S(1)}, u32[]{:S(2)}, u32[]{:S(2)}) %collective-permute-start.43) | collective-permute-done | bytes 131104 | tf_op jit(solution)/shard_map/ppermute | solution.py:28
  183.1 2.5 %collective-permute-start.42 = (bf16[512,128]{1,0:T(8,128)(2,1)S(1)}, bf16[512,128]{1,0:T(8,128)(2,1)S(1)}, u32[]{:S(2)}, u32[]{:S(2)}) collective-permute-start(bf16[512,128]{1,0:T(8,128)(2,1)S(1)} %add_convert_fusion.2), channel_id=1, source_target_pairs={{0,6},{1,7},{2,4},{3,5},{4,2},{5,3},{6,0},{7,1},{8,14},{9,15},{10,... | collective-permute-start | bytes 393224 | tf_op jit(solution)/shard_map/ppermute | solution.py:28
  186.2 2.9 %collective-permute-start.46 = (bf16[512,128]{1,0:T(8,128)(2,1)S(1)}, bf16[512,128]{1,0:T(8,128)(2,1)S(1)}, u32[]{:S(2)}, u32[]{:S(2)}) collective-permute-start(bf16[512,128]{1,0:T(8,128)(2,1)S(1)} %add_convert_fusion), channel_id=1, source_target_pairs={{0,2},{1,3},{2,0},{3,1},{4,6},{5,7},{6,4},{7,5},{8,10},{9,11},{10,... | collective-permute-start | bytes 393224 | tf_op jit(solution)/shard_map/ppermute | solution.py:28
  189.8 2.5 %shard_map.76.coupled_ref = f32[512,128]{1,0:T(8,128)} custom-call(f32[512,128]{1,0:T(8,128)} %copy-done.13, bf16[512,128]{1,0:T(8,128)(2,1)} %copy-done.47, bf16[512,128]{1,0:T(8,128)(2,1)} %copy-done.44), custom_call_target="tpu_custom_call" | custom-call | flops 134217728 | bytes 786432 | tf_op jit(solution)/shard_map/pallas_call | solution.py:265
  192.3 3.4 %collective-permute-done.44.refs_2_ = bf16[512,128]{1,0:T(8,128)(2,1)S(1)} collective-permute-done((bf16[512,128]{1,0:T(8,128)(2,1)S(1)}, bf16[512,128]{1,0:T(8,128)(2,1)S(1)}, u32[]{:S(2)}, u32[]{:S(2)}) %collective-permute-start.44) | collective-permute-done | bytes 131104 | tf_op jit(solution)/shard_map/ppermute | solution.py:28
  196.4 2.2 shard_map.77
  200.6 2.4 %collective-permute-start.49 = (bf16[528,128]{1,0:T(8,128)(2,1)}, bf16[528,128]{1,0:T(8,128)(2,1)S(1)}, u32[]{:S(2)}, u32[]{:S(2)}) collective-permute-start(bf16[528,128]{1,0:T(8,128)(2,1)} %get-tuple-element.83.refs_7_), channel_id=1, source_target_pairs={{0,2},{1,3},{2,0},{3,1},{4,6},{5,7},{6,4},{7,5},{8,10},{9,11},{10,... | collective-permute-start | bytes 405512 | tf_op jit(solution)/shard_map/ppermute | solution.py:28
  204.1 3.1 %collective-permute-done.53.refs_13_ = bf16[528,128]{1,0:T(8,128)(2,1)S(1)} collective-permute-done((bf16[528,128]{1,0:T(8,128)(2,1)}, bf16[528,128]{1,0:T(8,128)(2,1)S(1)}, u32[]{:S(2)}, u32[]{:S(2)}) %collective-permute-start.53) | collective-permute-done | bytes 135200 | tf_op jit(solution)/shard_map/ppermute | solution.py:28
  208.3 3.6 %collective-permute-done.51.refs_11_ = bf16[528,128]{1,0:T(8,128)(2,1)S(1)} collective-permute-done((bf16[528,128]{1,0:T(8,128)(2,1)}, bf16[528,128]{1,0:T(8,128)(2,1)S(1)}, u32[]{:S(2)}, u32[]{:S(2)}) %collective-permute-start.51) | collective-permute-done | bytes 135200 | tf_op jit(solution)/shard_map/ppermute | solution.py:28
  214.0 4.4 %collective-permute-done.52.refs_12_ = bf16[528,128]{1,0:T(8,128)(2,1)S(1)} collective-permute-done((bf16[528,128]{1,0:T(8,128)(2,1)S(1)}, bf16[528,128]{1,0:T(8,128)(2,1)S(1)}, u32[]{:S(2)}, u32[]{:S(2)}) %collective-permute-start.52) | collective-permute-done | bytes 135200 | tf_op jit(solution)/shard_map/ppermute | solution.py:28
  220.4 2.2 copy-done.3
  222.6 2.2 copy-done.7
  226.6 8.8 %shard_map.78 = (bf16[512,128]{1,0:T(8,128)(2,1)}, f32[4,128]{1,0:T(4,128)S(1)}) custom-call(s32[136]{0:T(256)S(1)} %copy-done.24, s32[136]{0:T(256)S(1)} %copy-done.26, s32[136]{0:T(256)S(1)} %copy-done.28, s32[136]{0:T(256)S(1)} %copy-done.29, s32[1]{0:T(128)} %get-tuple-element.49.refs_3_.refs_4_, bf16[128,128,128]{2,1,0:T(8,128)(2,1)S(1)} %bitcast.11, ...), custom_call_target="tpu_custom_call" | custom-call | flops 536870912 | bytes 4194304 | tf_op jit(solution)/shard_map/pallas_call | solution.py:236
  (180 shorter events, 67.7 us)
Async XLA Ops:
  0.6 9.8 %collective-permute-start.7 = (bf16[512,128]{1,0:T(8,128)(2,1)}, bf16[512,128]{1,0:T(8,128)(2,1)S(1)}, u32[]{:S(2)}, u32[]{:S(2)}) collective-permute-start(bf16[512,128]{1,0:T(8,128)(2,1)} %bitcast.16), channel_id=1, source_target_pairs={{0,6},{1,7},{2,4},{3,5},{4,2},{5,3},{6,0},{7,1},{8,14},{9,15},{10,... | collective-permute-start | bytes 393224 | tf_op jit(solution)/shard_map/ppermute | solution.py:28
  5.7 11.3 %collective-permute-start.5 = (bf16[512,128]{1,0:T(8,128)(2,1)}, bf16[512,128]{1,0:T(8,128)(2,1)S(1)}, u32[]{:S(2)}, u32[]{:S(2)}) collective-permute-start(bf16[512,128]{1,0:T(8,128)(2,1)} %bitcast.17), channel_id=1, source_target_pairs={{0,4},{1,5},{2,6},{3,7},{4,0},{5,1},{6,2},{7,3},{8,12},{9,13},{10,... | collective-permute-start | bytes 393224 | tf_op jit(solution)/shard_map/ppermute | solution.py:28
  5.7 12.8 %collective-permute-start.3 = (bf16[512,128]{1,0:T(8,128)(2,1)}, bf16[512,128]{1,0:T(8,128)(2,1)S(1)}, u32[]{:S(2)}, u32[]{:S(2)}) collective-permute-start(bf16[512,128]{1,0:T(8,128)(2,1)} %bitcast.18), channel_id=1, source_target_pairs={{0,2},{1,3},{2,0},{3,1},{4,6},{5,7},{6,4},{7,5},{8,10},{9,11},{10,... | collective-permute-start | bytes 393224 | tf_op jit(solution)/shard_map/ppermute | solution.py:28
  6.4 17.5 %collective-permute-start.2 = (bf16[512,128]{1,0:T(8,128)(2,1)}, bf16[512,128]{1,0:T(8,128)(2,1)S(1)}, u32[]{:S(2)}, u32[]{:S(2)}) collective-permute-start(bf16[512,128]{1,0:T(8,128)(2,1)} %bitcast.19), channel_id=1, source_target_pairs={{0,1},{1,0},{2,3},{3,2},{4,5},{5,4},{6,7},{7,6},{8,9},{9,8},{10,11... | collective-permute-start | bytes 393224 | tf_op jit(solution)/shard_map/ppermute | solution.py:28
  10.4 13.5 %collective-permute-start.8 = (bf16[512,128]{1,0:T(8,128)(2,1)S(1)}, bf16[512,128]{1,0:T(8,128)(2,1)S(1)}, u32[]{:S(2)}, u32[]{:S(2)}) collective-permute-start(bf16[512,128]{1,0:T(8,128)(2,1)S(1)} %collective-permute-done.7.refs_12_.refs_21_), channel_id=1, source_target_pairs={{0,1},{1,0},{2,3},{3,2},{4,5},{5,4},{6,7},{7,6},{8,9},{9,8},{10,11... | collective-permute-start | bytes 393224 | tf_op jit(solution)/shard_map/ppermute | solution.py:28
  17.0 6.8 %collective-permute-start.6 = (bf16[512,128]{1,0:T(8,128)(2,1)S(1)}, bf16[512,128]{1,0:T(8,128)(2,1)S(1)}, u32[]{:S(2)}, u32[]{:S(2)}) collective-permute-start(bf16[512,128]{1,0:T(8,128)(2,1)S(1)} %collective-permute-done.5.refs_10_.refs_19_), channel_id=1, source_target_pairs={{0,1},{1,0},{2,3},{3,2},{4,5},{5,4},{6,7},{7,6},{8,9},{9,8},{10,11... | collective-permute-start | bytes 393224 | tf_op jit(solution)/shard_map/ppermute | solution.py:28
  39.8 7.3 %collective-permute-start.9 = (bf16[512,128]{1,0:T(8,128)(2,1)S(1)}, bf16[512,128]{1,0:T(8,128)(2,1)S(1)}, u32[]{:S(2)}, u32[]{:S(2)}) collective-permute-start(bf16[512,128]{1,0:T(8,128)(2,1)S(1)} %get-tuple-element.52), channel_id=1, source_target_pairs={{0,1},{1,0},{2,3},{3,2},{4,5},{5,4},{6,7},{7,6},{8,9},{9,8},{10,11... | collective-permute-start | bytes 393224 | tf_op jit(solution)/shard_map/ppermute | solution.py:28
  40.7 15.3 %collective-permute-start.1 = (bf16[512,128]{1,0:T(8,128)(2,1)S(1)}, bf16[512,128]{1,0:T(8,128)(2,1)S(1)}, u32[]{:S(2)}, u32[]{:S(2)}) collective-permute-start(bf16[512,128]{1,0:T(8,128)(2,1)S(1)} %bitcast.23), channel_id=1, source_target_pairs={{8,0},{16,8},{24,16},{9,1},{17,9},{25,17},{10,2},{18,10},{26,18},{... | collective-permute-start | bytes 393224 | tf_op jit(solution)/shard_map/ppermute | solution.py:34
  41.9 16.7 %collective-permute-start = (bf16[512,128]{1,0:T(8,128)(2,1)S(1)}, bf16[512,128]{1,0:T(8,128)(2,1)S(1)}, u32[]{:S(2)}, u32[]{:S(2)}) collective-permute-start(bf16[512,128]{1,0:T(8,128)(2,1)S(1)} %bitcast.24), channel_id=1, source_target_pairs={{0,8},{8,16},{16,24},{1,9},{9,17},{17,25},{2,10},{10,18},{18,26},{... | collective-permute-start | bytes 393224 | tf_op jit(solution)/shard_map/ppermute | solution.py:34
  46.3 8.1 %collective-permute-start.13 = (bf16[512,128]{1,0:T(8,128)(2,1)S(1)}, bf16[512,128]{1,0:T(8,128)(2,1)S(1)}, u32[]{:S(2)}, u32[]{:S(2)}) collective-permute-start(bf16[512,128]{1,0:T(8,128)(2,1)S(1)} %get-tuple-element.56), channel_id=1, source_target_pairs={{0,1},{1,0},{2,3},{3,2},{4,5},{5,4},{6,7},{7,6},{8,9},{9,8},{10,11... | collective-permute-start | bytes 393224 | tf_op jit(solution)/shard_map/ppermute | solution.py:28
  47.1 14.7 %collective-permute-start.15 = (bf16[512,128]{1,0:T(8,128)(2,1)S(1)}, bf16[512,128]{1,0:T(8,128)(2,1)S(1)}, u32[]{:S(2)}, u32[]{:S(2)}) collective-permute-start(bf16[512,128]{1,0:T(8,128)(2,1)S(1)} %get-tuple-element.57), channel_id=1, source_target_pairs={{0,1},{1,0},{2,3},{3,2},{4,5},{5,4},{6,7},{7,6},{8,9},{9,8},{10,11... | collective-permute-start | bytes 393224 | tf_op jit(solution)/shard_map/ppermute | solution.py:28
  50.0 11.8 %collective-permute-start.10 = (bf16[512,128]{1,0:T(8,128)(2,1)S(1)}, bf16[512,128]{1,0:T(8,128)(2,1)S(1)}, u32[]{:S(2)}, u32[]{:S(2)}) collective-permute-start(bf16[512,128]{1,0:T(8,128)(2,1)S(1)} %add_convert_fusion.8), channel_id=1, source_target_pairs={{0,6},{1,7},{2,4},{3,5},{4,2},{5,3},{6,0},{7,1},{8,14},{9,15},{10,... | collective-permute-start | bytes 393224 | tf_op jit(solution)/shard_map/ppermute | solution.py:28
  54.4 11.5 %collective-permute-start.12 = (bf16[512,128]{1,0:T(8,128)(2,1)S(1)}, bf16[512,128]{1,0:T(8,128)(2,1)S(1)}, u32[]{:S(2)}, u32[]{:S(2)}) collective-permute-start(bf16[512,128]{1,0:T(8,128)(2,1)S(1)} %add_convert_fusion.7), channel_id=1, source_target_pairs={{0,4},{1,5},{2,6},{3,7},{4,0},{5,1},{6,2},{7,3},{8,12},{9,13},{10,... | collective-permute-start | bytes 393224 | tf_op jit(solution)/shard_map/ppermute | solution.py:28
  56.0 10.0 %collective-permute-start.14 = (bf16[512,128]{1,0:T(8,128)(2,1)S(1)}, bf16[512,128]{1,0:T(8,128)(2,1)S(1)}, u32[]{:S(2)}, u32[]{:S(2)}) collective-permute-start(bf16[512,128]{1,0:T(8,128)(2,1)S(1)} %add_convert_fusion.6), channel_id=1, source_target_pairs={{0,2},{1,3},{2,0},{3,1},{4,6},{5,7},{6,4},{7,5},{8,10},{9,11},{10,... | collective-permute-start | bytes 393224 | tf_op jit(solution)/shard_map/ppermute | solution.py:28
  68.8 8.6 %collective-permute-start.21 = (bf16[528,128]{1,0:T(8,128)(2,1)}, bf16[528,128]{1,0:T(8,128)(2,1)S(1)}, u32[]{:S(2)}, u32[]{:S(2)}) collective-permute-start(bf16[528,128]{1,0:T(8,128)(2,1)} %get-tuple-element.58.refs_6_), channel_id=1, source_target_pairs={{0,6},{1,7},{2,4},{3,5},{4,2},{5,3},{6,0},{7,1},{8,14},{9,15},{10,... | collective-permute-start | bytes 405512 | tf_op jit(solution)/shard_map/ppermute | solution.py:28
  70.3 11.5 %collective-permute-start.19 = (bf16[528,128]{1,0:T(8,128)(2,1)}, bf16[528,128]{1,0:T(8,128)(2,1)S(1)}, u32[]{:S(2)}, u32[]{:S(2)}) collective-permute-start(bf16[528,128]{1,0:T(8,128)(2,1)} %get-tuple-element.58.refs_6_), channel_id=1, source_target_pairs={{0,4},{1,5},{2,6},{3,7},{4,0},{5,1},{6,2},{7,3},{8,12},{9,13},{10,... | collective-permute-start | bytes 405512 | tf_op jit(solution)/shard_map/ppermute | solution.py:28
  70.3 12.3 %collective-permute-start.17 = (bf16[528,128]{1,0:T(8,128)(2,1)}, bf16[528,128]{1,0:T(8,128)(2,1)S(1)}, u32[]{:S(2)}, u32[]{:S(2)}) collective-permute-start(bf16[528,128]{1,0:T(8,128)(2,1)} %get-tuple-element.58.refs_6_), channel_id=1, source_target_pairs={{0,2},{1,3},{2,0},{3,1},{4,6},{5,7},{6,4},{7,5},{8,10},{9,11},{10,... | collective-permute-start | bytes 405512 | tf_op jit(solution)/shard_map/ppermute | solution.py:28
  73.2 10.6 %collective-permute-start.16 = (bf16[528,128]{1,0:T(8,128)(2,1)}, bf16[528,128]{1,0:T(8,128)(2,1)S(1)}, u32[]{:S(2)}, u32[]{:S(2)}) collective-permute-start(bf16[528,128]{1,0:T(8,128)(2,1)} %get-tuple-element.58.refs_6_), channel_id=1, source_target_pairs={{0,1},{1,0},{2,3},{3,2},{4,5},{5,4},{6,7},{7,6},{8,9},{9,8},{10,11... | collective-permute-start | bytes 405512 | tf_op jit(solution)/shard_map/ppermute | solution.py:28
  81.8 6.4 %collective-permute-start.20 = (bf16[528,128]{1,0:T(8,128)(2,1)S(1)}, bf16[528,128]{1,0:T(8,128)(2,1)S(1)}, u32[]{:S(2)}, u32[]{:S(2)}) collective-permute-start(bf16[528,128]{1,0:T(8,128)(2,1)S(1)} %collective-permute-done.19.refs_10_), channel_id=1, source_target_pairs={{0,1},{1,0},{2,3},{3,2},{4,5},{5,4},{6,7},{7,6},{8,9},{9,8},{10,11... | collective-permute-start | bytes 405512 | tf_op jit(solution)/shard_map/ppermute | solution.py:28
  82.7 7.5 %collective-permute-start.18 = (bf16[528,128]{1,0:T(8,128)(2,1)S(1)}, bf16[528,128]{1,0:T(8,128)(2,1)S(1)}, u32[]{:S(2)}, u32[]{:S(2)}) collective-permute-start(bf16[528,128]{1,0:T(8,128)(2,1)S(1)} %collective-permute-done.17.refs_8_), channel_id=1, source_target_pairs={{0,1},{1,0},{2,3},{3,2},{4,5},{5,4},{6,7},{7,6},{8,9},{9,8},{10,11... | collective-permute-start | bytes 405512 | tf_op jit(solution)/shard_map/ppermute | solution.py:28
  106.3 6.5 %collective-permute-start.25 = (bf16[512,128]{1,0:T(8,128)(2,1)S(1)}, bf16[512,128]{1,0:T(8,128)(2,1)S(1)}, u32[]{:S(2)}, u32[]{:S(2)}) collective-permute-start(bf16[512,128]{1,0:T(8,128)(2,1)S(1)} %get-tuple-element.64), channel_id=1, source_target_pairs={{0,1},{1,0},{2,3},{3,2},{4,5},{5,4},{6,7},{7,6},{8,9},{9,8},{10,11... | collective-permute-start | bytes 393224 | tf_op jit(solution)/shard_map/ppermute | solution.py:28
  106.5 14.0 %collective-permute-start.24 = (bf16[512,128]{1,0:T(8,128)(2,1)S(1)}, bf16[512,128]{1,0:T(8,128)(2,1)S(1)}, u32[]{:S(2)}, u32[]{:S(2)}) collective-permute-start(bf16[512,128]{1,0:T(8,128)(2,1)S(1)} %get-tuple-element.61), channel_id=1, source_target_pairs={{8,0},{16,8},{24,16},{9,1},{17,9},{25,17},{10,2},{18,10},{26,18},{... | collective-permute-start | bytes 393224 | tf_op jit(solution)/shard_map/ppermute | solution.py:34
  107.7 16.1 %collective-permute-start.23 = (bf16[512,128]{1,0:T(8,128)(2,1)S(1)}, bf16[512,128]{1,0:T(8,128)(2,1)S(1)}, u32[]{:S(2)}, u32[]{:S(2)}) collective-permute-start(bf16[512,128]{1,0:T(8,128)(2,1)S(1)} %get-tuple-element.61), channel_id=1, source_target_pairs={{0,8},{8,16},{16,24},{1,9},{9,17},{17,25},{2,10},{10,18},{18,26},{... | collective-permute-start | bytes 393224 | tf_op jit(solution)/shard_map/ppermute | solution.py:34
  112.8 7.6 %collective-permute-start.29 = (bf16[512,128]{1,0:T(8,128)(2,1)S(1)}, bf16[512,128]{1,0:T(8,128)(2,1)S(1)}, u32[]{:S(2)}, u32[]{:S(2)}) collective-permute-start(bf16[512,128]{1,0:T(8,128)(2,1)S(1)} %get-tuple-element.68), channel_id=1, source_target_pairs={{0,1},{1,0},{2,3},{3,2},{4,5},{5,4},{6,7},{7,6},{8,9},{9,8},{10,11... | collective-permute-start | bytes 393224 | tf_op jit(solution)/shard_map/ppermute | solution.py:28
  112.9 14.0 %collective-permute-start.31 = (bf16[512,128]{1,0:T(8,128)(2,1)S(1)}, bf16[512,128]{1,0:T(8,128)(2,1)S(1)}, u32[]{:S(2)}, u32[]{:S(2)}) collective-permute-start(bf16[512,128]{1,0:T(8,128)(2,1)S(1)} %get-tuple-element.69), channel_id=1, source_target_pairs={{0,1},{1,0},{2,3},{3,2},{4,5},{5,4},{6,7},{7,6},{8,9},{9,8},{10,11... | collective-permute-start | bytes 393224 | tf_op jit(solution)/shard_map/ppermute | solution.py:28
  117.2 9.7 %collective-permute-start.26 = (bf16[512,128]{1,0:T(8,128)(2,1)S(1)}, bf16[512,128]{1,0:T(8,128)(2,1)S(1)}, u32[]{:S(2)}, u32[]{:S(2)}) collective-permute-start(bf16[512,128]{1,0:T(8,128)(2,1)S(1)} %add_convert_fusion.5), channel_id=1, source_target_pairs={{0,6},{1,7},{2,4},{3,5},{4,2},{5,3},{6,0},{7,1},{8,14},{9,15},{10,... | collective-permute-start | bytes 393224 | tf_op jit(solution)/shard_map/ppermute | solution.py:28
  120.4 9.4 %collective-permute-start.28 = (bf16[512,128]{1,0:T(8,128)(2,1)S(1)}, bf16[512,128]{1,0:T(8,128)(2,1)S(1)}, u32[]{:S(2)}, u32[]{:S(2)}) collective-permute-start(bf16[512,128]{1,0:T(8,128)(2,1)S(1)} %add_convert_fusion.4), channel_id=1, source_target_pairs={{0,4},{1,5},{2,6},{3,7},{4,0},{5,1},{6,2},{7,3},{8,12},{9,13},{10,... | collective-permute-start | bytes 393224 | tf_op jit(solution)/shard_map/ppermute | solution.py:28
  120.5 9.3 %collective-permute-start.30 = (bf16[512,128]{1,0:T(8,128)(2,1)S(1)}, bf16[512,128]{1,0:T(8,128)(2,1)S(1)}, u32[]{:S(2)}, u32[]{:S(2)}) collective-permute-start(bf16[512,128]{1,0:T(8,128)(2,1)S(1)} %add_convert_fusion.3), channel_id=1, source_target_pairs={{0,2},{1,3},{2,0},{3,1},{4,6},{5,7},{6,4},{7,5},{8,10},{9,11},{10,... | collective-permute-start | bytes 393224 | tf_op jit(solution)/shard_map/ppermute | solution.py:28
  132.7 8.6 %collective-permute-start.37 = (bf16[528,128]{1,0:T(8,128)(2,1)}, bf16[528,128]{1,0:T(8,128)(2,1)S(1)}, u32[]{:S(2)}, u32[]{:S(2)}) collective-permute-start(bf16[528,128]{1,0:T(8,128)(2,1)} %get-tuple-element.70.refs_6_), channel_id=1, source_target_pairs={{0,6},{1,7},{2,4},{3,5},{4,2},{5,3},{6,0},{7,1},{8,14},{9,15},{10,... | collective-permute-start | bytes 405512 | tf_op jit(solution)/shard_map/ppermute | solution.py:28
  134.8 11.2 %collective-permute-start.35 = (bf16[528,128]{1,0:T(8,128)(2,1)}, bf16[528,128]{1,0:T(8,128)(2,1)S(1)}, u32[]{:S(2)}, u32[]{:S(2)}) collective-permute-start(bf16[528,128]{1,0:T(8,128)(2,1)} %get-tuple-element.70.refs_6_), channel_id=1, source_target_pairs={{0,4},{1,5},{2,6},{3,7},{4,0},{5,1},{6,2},{7,3},{8,12},{9,13},{10,... | collective-permute-start | bytes 405512 | tf_op jit(solution)/shard_map/ppermute | solution.py:28
  134.8 12.3 %collective-permute-start.33 = (bf16[528,128]{1,0:T(8,128)(2,1)}, bf16[528,128]{1,0:T(8,128)(2,1)S(1)}, u32[]{:S(2)}, u32[]{:S(2)}) collective-permute-start(bf16[528,128]{1,0:T(8,128)(2,1)} %get-tuple-element.70.refs_6_), channel_id=1, source_target_pairs={{0,2},{1,3},{2,0},{3,1},{4,6},{5,7},{6,4},{7,5},{8,10},{9,11},{10,... | collective-permute-start | bytes 405512 | tf_op jit(solution)/shard_map/ppermute | solution.py:28
  137.1 11.0 %collective-permute-start.32 = (bf16[528,128]{1,0:T(8,128)(2,1)}, bf16[528,128]{1,0:T(8,128)(2,1)S(1)}, u32[]{:S(2)}, u32[]{:S(2)}) collective-permute-start(bf16[528,128]{1,0:T(8,128)(2,1)} %get-tuple-element.70.refs_6_), channel_id=1, source_target_pairs={{0,1},{1,0},{2,3},{3,2},{4,5},{5,4},{6,7},{7,6},{8,9},{9,8},{10,11... | collective-permute-start | bytes 405512 | tf_op jit(solution)/shard_map/ppermute | solution.py:28
  141.3 6.8 %collective-permute-start.38 = (bf16[528,128]{1,0:T(8,128)(2,1)S(1)}, bf16[528,128]{1,0:T(8,128)(2,1)S(1)}, u32[]{:S(2)}, u32[]{:S(2)}) collective-permute-start(bf16[528,128]{1,0:T(8,128)(2,1)S(1)} %collective-permute-done.37.refs_12_), channel_id=1, source_target_pairs={{0,1},{1,0},{2,3},{3,2},{4,5},{5,4},{6,7},{7,6},{8,9},{9,8},{10,11... | collective-permute-start | bytes 405512 | tf_op jit(solution)/shard_map/ppermute | solution.py:28
  147.1 7.3 %collective-permute-start.34 = (bf16[528,128]{1,0:T(8,128)(2,1)S(1)}, bf16[528,128]{1,0:T(8,128)(2,1)S(1)}, u32[]{:S(2)}, u32[]{:S(2)}) collective-permute-start(bf16[528,128]{1,0:T(8,128)(2,1)S(1)} %collective-permute-done.33.refs_8_), channel_id=1, source_target_pairs={{0,1},{1,0},{2,3},{3,2},{4,5},{5,4},{6,7},{7,6},{8,9},{9,8},{10,11... | collective-permute-start | bytes 405512 | tf_op jit(solution)/shard_map/ppermute | solution.py:28
  171.8 7.0 %collective-permute-start.41 = (bf16[512,128]{1,0:T(8,128)(2,1)S(1)}, bf16[512,128]{1,0:T(8,128)(2,1)S(1)}, u32[]{:S(2)}, u32[]{:S(2)}) collective-permute-start(bf16[512,128]{1,0:T(8,128)(2,1)S(1)} %get-tuple-element.77), channel_id=1, source_target_pairs={{0,1},{1,0},{2,3},{3,2},{4,5},{5,4},{6,7},{7,6},{8,9},{9,8},{10,11... | collective-permute-start | bytes 393224 | tf_op jit(solution)/shard_map/ppermute | solution.py:28
  172.2 14.0 %collective-permute-start.40 = (bf16[512,128]{1,0:T(8,128)(2,1)S(1)}, bf16[512,128]{1,0:T(8,128)(2,1)S(1)}, u32[]{:S(2)}, u32[]{:S(2)}) collective-permute-start(bf16[512,128]{1,0:T(8,128)(2,1)S(1)} %get-tuple-element.74), channel_id=1, source_target_pairs={{8,0},{16,8},{24,16},{9,1},{17,9},{25,17},{10,2},{18,10},{26,18},{... | collective-permute-start | bytes 393224 | tf_op jit(solution)/shard_map/ppermute | solution.py:34
  173.6 15.5 %collective-permute-start.39 = (bf16[512,128]{1,0:T(8,128)(2,1)S(1)}, bf16[512,128]{1,0:T(8,128)(2,1)S(1)}, u32[]{:S(2)}, u32[]{:S(2)}) collective-permute-start(bf16[512,128]{1,0:T(8,128)(2,1)S(1)} %get-tuple-element.74), channel_id=1, source_target_pairs={{0,8},{8,16},{16,24},{1,9},{9,17},{17,25},{2,10},{10,18},{18,26},{... | collective-permute-start | bytes 393224 | tf_op jit(solution)/shard_map/ppermute | solution.py:34
  178.2 7.7 %collective-permute-start.45 = (bf16[512,128]{1,0:T(8,128)(2,1)S(1)}, bf16[512,128]{1,0:T(8,128)(2,1)S(1)}, u32[]{:S(2)}, u32[]{:S(2)}) collective-permute-start(bf16[512,128]{1,0:T(8,128)(2,1)S(1)} %get-tuple-element.81), channel_id=1, source_target_pairs={{0,1},{1,0},{2,3},{3,2},{4,5},{5,4},{6,7},{7,6},{8,9},{9,8},{10,11... | collective-permute-start | bytes 393224 | tf_op jit(solution)/shard_map/ppermute | solution.py:28
  178.8 13.5 %collective-permute-start.47 = (bf16[512,128]{1,0:T(8,128)(2,1)S(1)}, bf16[512,128]{1,0:T(8,128)(2,1)S(1)}, u32[]{:S(2)}, u32[]{:S(2)}) collective-permute-start(bf16[512,128]{1,0:T(8,128)(2,1)S(1)} %get-tuple-element.82), channel_id=1, source_target_pairs={{0,1},{1,0},{2,3},{3,2},{4,5},{5,4},{6,7},{7,6},{8,9},{9,8},{10,11... | collective-permute-start | bytes 393224 | tf_op jit(solution)/shard_map/ppermute | solution.py:28
  183.1 9.2 %collective-permute-start.42 = (bf16[512,128]{1,0:T(8,128)(2,1)S(1)}, bf16[512,128]{1,0:T(8,128)(2,1)S(1)}, u32[]{:S(2)}, u32[]{:S(2)}) collective-permute-start(bf16[512,128]{1,0:T(8,128)(2,1)S(1)} %add_convert_fusion.2), channel_id=1, source_target_pairs={{0,6},{1,7},{2,4},{3,5},{4,2},{5,3},{6,0},{7,1},{8,14},{9,15},{10,... | collective-permute-start | bytes 393224 | tf_op jit(solution)/shard_map/ppermute | solution.py:28
  185.9 9.8 %collective-permute-start.44 = (bf16[512,128]{1,0:T(8,128)(2,1)S(1)}, bf16[512,128]{1,0:T(8,128)(2,1)S(1)}, u32[]{:S(2)}, u32[]{:S(2)}) collective-permute-start(bf16[512,128]{1,0:T(8,128)(2,1)S(1)} %add_convert_fusion.1), channel_id=1, source_target_pairs={{0,4},{1,5},{2,6},{3,7},{4,0},{5,1},{6,2},{7,3},{8,12},{9,13},{10,... | collective-permute-start | bytes 393224 | tf_op jit(solution)/shard_map/ppermute | solution.py:28
  186.2 9.5 %collective-permute-start.46 = (bf16[512,128]{1,0:T(8,128)(2,1)S(1)}, bf16[512,128]{1,0:T(8,128)(2,1)S(1)}, u32[]{:S(2)}, u32[]{:S(2)}) collective-permute-start(bf16[512,128]{1,0:T(8,128)(2,1)S(1)} %add_convert_fusion), channel_id=1, source_target_pairs={{0,2},{1,3},{2,0},{3,1},{4,6},{5,7},{6,4},{7,5},{8,10},{9,11},{10,... | collective-permute-start | bytes 393224 | tf_op jit(solution)/shard_map/ppermute | solution.py:28
  198.6 8.6 %collective-permute-start.53 = (bf16[528,128]{1,0:T(8,128)(2,1)}, bf16[528,128]{1,0:T(8,128)(2,1)S(1)}, u32[]{:S(2)}, u32[]{:S(2)}) collective-permute-start(bf16[528,128]{1,0:T(8,128)(2,1)} %get-tuple-element.83.refs_7_), channel_id=1, source_target_pairs={{0,6},{1,7},{2,4},{3,5},{4,2},{5,3},{6,0},{7,1},{8,14},{9,15},{10,... | collective-permute-start | bytes 405512 | tf_op jit(solution)/shard_map/ppermute | solution.py:28
  200.6 11.4 %collective-permute-start.51 = (bf16[528,128]{1,0:T(8,128)(2,1)}, bf16[528,128]{1,0:T(8,128)(2,1)S(1)}, u32[]{:S(2)}, u32[]{:S(2)}) collective-permute-start(bf16[528,128]{1,0:T(8,128)(2,1)} %get-tuple-element.83.refs_7_), channel_id=1, source_target_pairs={{0,4},{1,5},{2,6},{3,7},{4,0},{5,1},{6,2},{7,3},{8,12},{9,13},{10,... | collective-permute-start | bytes 405512 | tf_op jit(solution)/shard_map/ppermute | solution.py:28
  200.6 12.6 %collective-permute-start.49 = (bf16[528,128]{1,0:T(8,128)(2,1)}, bf16[528,128]{1,0:T(8,128)(2,1)S(1)}, u32[]{:S(2)}, u32[]{:S(2)}) collective-permute-start(bf16[528,128]{1,0:T(8,128)(2,1)} %get-tuple-element.83.refs_7_), channel_id=1, source_target_pairs={{0,2},{1,3},{2,0},{3,1},{4,6},{5,7},{6,4},{7,5},{8,10},{9,11},{10,... | collective-permute-start | bytes 405512 | tf_op jit(solution)/shard_map/ppermute | solution.py:28
  203.0 11.0 %collective-permute-start.48 = (bf16[528,128]{1,0:T(8,128)(2,1)}, bf16[528,128]{1,0:T(8,128)(2,1)S(1)}, u32[]{:S(2)}, u32[]{:S(2)}) collective-permute-start(bf16[528,128]{1,0:T(8,128)(2,1)} %get-tuple-element.83.refs_7_), channel_id=1, source_target_pairs={{0,1},{1,0},{2,3},{3,2},{4,5},{5,4},{6,7},{7,6},{8,9},{9,8},{10,11... | collective-permute-start | bytes 405512 | tf_op jit(solution)/shard_map/ppermute | solution.py:28
  207.2 6.8 %collective-permute-start.54 = (bf16[528,128]{1,0:T(8,128)(2,1)S(1)}, bf16[528,128]{1,0:T(8,128)(2,1)S(1)}, u32[]{:S(2)}, u32[]{:S(2)}) collective-permute-start(bf16[528,128]{1,0:T(8,128)(2,1)S(1)} %collective-permute-done.53.refs_13_), channel_id=1, source_target_pairs={{0,1},{1,0},{2,3},{3,2},{4,5},{5,4},{6,7},{7,6},{8,9},{9,8},{10,11... | collective-permute-start | bytes 405512 | tf_op jit(solution)/shard_map/ppermute | solution.py:28
  213.2 7.1 %collective-permute-start.50 = (bf16[528,128]{1,0:T(8,128)(2,1)S(1)}, bf16[528,128]{1,0:T(8,128)(2,1)S(1)}, u32[]{:S(2)}, u32[]{:S(2)}) collective-permute-start(bf16[528,128]{1,0:T(8,128)(2,1)S(1)} %collective-permute-done.49.refs_9_), channel_id=1, source_target_pairs={{0,1},{1,0},{2,3},{3,2},{4,5},{5,4},{6,7},{7,6},{8,9},{9,8},{10,11... | collective-permute-start | bytes 405512 | tf_op jit(solution)/shard_map/ppermute | solution.py:28
  (55 other events, 470.2 us)

commit v2 on v1

v2 whole, which is shorter than its diff:
```python
import functools

import jax
import jax.numpy as jnp
from jax import lax
from jax.experimental import pallas as pl
from jax.experimental.pallas import tpu as pltpu
from jax.sharding import PartitionSpec as P

ITERS = 3
GROUP = 8
TAIL = 16
STRIP = 64

step_size = 0.3
low_type = jnp.bfloat16
wide_type = jnp.float32
VMEM = pl.BlockSpec(memory_space=pltpu.VMEM)
SMEM = pl.BlockSpec(memory_space=pltpu.SMEM)


def params(megabytes):
    return pltpu.CompilerParams(vmem_limit_bytes=megabytes << 20)


def pinned(array):
    return pltpu.with_memory_space_constraint(array, pltpu.VMEM)


def kept(shape, dtype):
    return pltpu.VMEM(shape, dtype)


def traded(block, distance):
    route = [(i, i ^ distance) for i in range(lax.axis_size("op"))]
    return lax.ppermute(block, "op", route)


def neighbours(block):
    devices = lax.axis_size("seg")
    found = []
    for first in (0, 1):
        pairs = [(i, i + 1) for i in range(first, devices - 1, 2)]
        found.append(lax.ppermute(block, "seg", pairs + [(j, i) for i, j in pairs]))
    return found


def hop(place):
    return 2 if place == 3 else place & -place


def branches(place, devices):
    return [further for further in range(1, devices) if further ^ hop(further) == place]


def depth(place):
    return 0 if place == 0 else 1 + depth(place ^ hop(place))


def leaves(devices):
    return [place for place in range(1, devices) if not branches(place, devices)]


def gathered(block):
    devices = lax.axis_size("op")
    held = {0: block}
    for place in sorted(range(1, devices), key=depth):
        held[place] = traded(held[place ^ hop(place)], hop(place))
    return [held[place] for place in range(devices)]


def summed(pieces):
    devices = len(pieces)
    came = {place: [] for place in range(devices)}
    for place in sorted(range(1, devices), key=depth, reverse=True):
        piece = pieces[place]
        if came[place]:
            piece = sum((part.astype(wide_type) for part in came[place]), piece).astype(low_type)
        came[place ^ hop(place)].append(traded(piece, hop(place)))
    return [pieces[0], *came[0]]


def plan_kernel(blocks_dev, me_ref, shifts_ref, active_ref, left_hbm, right_hbm, plan_ref, left_ref, turned_ref, right_ref, arrived):
    copies = [
        pltpu.make_async_copy(left_hbm, left_ref, arrived.at[0]),
        pltpu.make_async_copy(right_hbm, right_ref, arrived.at[1]),
    ]
    for copy in copies:
        copy.start()
    terms, blocks_all = active_ref.shape
    room = plan_ref.shape[1]
    mine = me_ref[0] * blocks_dev
    found = 0
    for term in range(terms):
        shift = shifts_ref[0, term]

        def one(block, found, term=term, shift=shift):
            target = block + shift
            target = jnp.where(target >= blocks_all, target - blocks_all, target)
            plan_ref[0, found] = term * blocks_all + block
            plan_ref[1, found] = block ^ mine
            plan_ref[2, found] = target ^ mine
            plan_ref[3, found] = term
            return found + active_ref[term, block]

        found = lax.fori_loop(0, blocks_all, one, found, unroll=8)
    for extra in range(GROUP):
        plan_ref[0, found + extra] = 0
        plan_ref[1, found + extra] = 0
        plan_ref[2, found + extra] = blocks_all
        plan_ref[3, found + extra] = terms
    plan_ref[0, room - 1] = found
    for copy in copies:
        copy.wait()

    def turn(index, carried):
        for inner in range(GROUP // 2):
            pair = plan_ref[0, index * (GROUP // 2) + inner]
            turned_ref[pair] = right_ref[pair].T
        return carried

    lax.fori_loop(0, (found + GROUP // 2) // (GROUP // 2), turn, 0)


def make_plan(me, shifts, active, lefts, rights, blocks_dev):
    terms, blocks_all = active.shape
    room = terms * blocks_all + GROUP + 1
    far = pl.BlockSpec(memory_space=pltpu.HBM)
    return pl.pallas_call(
        functools.partial(plan_kernel, blocks_dev),
        out_shape=[
            jax.ShapeDtypeStruct((4, room), jnp.int32),
            kept(lefts.shape, lefts.dtype),
            kept(rights.shape, rights.dtype),
        ],
        in_specs=[SMEM] * 3 + [far] * 2,
        out_specs=[SMEM, VMEM, VMEM],
        scratch_shapes=[pltpu.VMEM(rights.shape, rights.dtype), pltpu.SemaphoreType.DMA((2,))],
        compiler_params=params(8),
        cost_estimate=pl.CostEstimate(flops=0, bytes_accessed=16 << 20, transcendentals=0),
    )(me, shifts, active, *(pltpu.with_memory_space_constraint(array, pltpu.HBM) for array in (lefts, rights)))


def pair_product(index, plan_ref, left_ref, right_ref, low_ref):
    pair = plan_ref[0, index]
    half = jnp.dot(left_ref[pair], low_ref[plan_ref[1, index]], preferred_element_type=wide_type).astype(low_type)
    return jnp.dot(half, right_ref[pair], preferred_element_type=wide_type)


def fill_low(first, chunk_refs, own_ref, old_refs, low_ref, fresh_ref, count):
    rows = own_ref.shape[0]
    width = own_ref.shape[1]
    if first:
        for place, chunk_ref in enumerate(chunk_refs):
            blocks = rows // width
            low_ref[place * blocks : (place + 1) * blocks] = chunk_ref[...].reshape(blocks, width, width)
        return
    tails = sum(ref[rows:, :].astype(wide_type) for ref in chunk_refs)

    def total(which):
        return tails[3 * which : 3 * which + 1] + tails[3 * which + 1 : 3 * which + 2] + tails[3 * which + 2 : 3 * which + 3]

    squares, cross, applied_squares = total(0), total(1), total(2)
    rho = cross / squares
    length = squares + step_size * step_size * (applied_squares - rho * cross)
    scale = jnp.sqrt(count / length)
    keep = scale * (1.0 + step_size * rho)
    take = scale * step_size
    for place, chunk_ref in enumerate(chunk_refs):
        source = own_ref if place == 0 else chunk_ref

        def strip(part, carried, place=place, source=source):
            start = pl.multiple_of(part * STRIP, STRIP)
            if len(old_refs) == 1:
                old = old_refs[0][pl.ds(place * rows + start, STRIP), :]
            else:
                old = old_refs[place][pl.ds(start, STRIP), :].astype(wide_type)
            new = keep * old - take * source[pl.ds(start, STRIP), :].astype(wide_type)
            if fresh_ref is not None:
                fresh_ref[pl.ds(place * rows + start, STRIP), :] = new
            low = new.astype(low_type)
            at = place * rows + start
            low_ref[at // width, pl.ds(pl.multiple_of(at % width, STRIP), STRIP), :] = low
            return carried

        lax.fori_loop(0, rows // STRIP, strip, 0, unroll=True)


def apply_kernel(first, devices, olds, count, term_scale, *refs):
    plan_ref, left_ref, right_ref = refs[:3]
    chunk_refs = refs[3 : 3 + devices][::-1]
    own_ref = refs[3 + devices]
    old_refs = refs[4 + devices : 4 + devices + olds]
    rest = refs[4 + devices + olds :]
    piece_refs, rest = rest[:devices], rest[devices:]
    if first:
        fresh_ref = None
    else:
        fresh_ref, own_low_ref, own_wide_ref = rest[:3]
        rest = rest[3:]
    low_ref, sum_ref = rest
    rows, width = own_ref.shape
    blocks = rows // width
    fill_low(first, chunk_refs, own_ref, old_refs, low_ref, fresh_ref, count)
    if not first:
        own_low_ref[...] = low_ref[:blocks].reshape(rows, width)
        own_wide_ref[...] = fresh_ref[:rows, :]
    sum_ref[...] = jnp.zeros_like(sum_ref)

    def group(index, carried):
        products = [
            pair_product(index * GROUP + inner, plan_ref, left_ref, right_ref, low_ref)
            for inner in range(GROUP)
        ]
        for inner, product in enumerate(products):
            sum_ref[plan_ref[2, index * GROUP + inner]] += product
        return carried

    lax.fori_loop(0, (plan_ref[0, plan_ref.shape[1] - 1] + GROUP - 1) // GROUP, group, 0)
    for place, piece_ref in enumerate(piece_refs):
        piece = sum_ref[place * blocks : (place + 1) * blocks].reshape(rows, width) * term_scale
        piece_ref[...] = piece.astype(piece_ref.dtype)


def apply_terms(plan, lefts, rights, chunks, own, olds, count, term_scale):
    first = not olds
    devices = len(chunks)
    rows, width = own.shape
    total = devices * rows
    sent = leaves(devices)
    outs = [kept((rows, width), low_type if place in sent else wide_type) for place in range(devices)]
    if not first:
        outs += [kept((total, width), wide_type), kept((rows, width), low_type), kept((rows, width), wide_type)]
    pairs_all = lefts.shape[0]
    return pl.pallas_call(
        functools.partial(apply_kernel, first, devices, len(olds), count, term_scale),
        out_shape=outs,
        in_specs=[SMEM] + [VMEM] * (3 + devices + len(olds)),
        out_specs=[VMEM] * len(outs),
        scratch_shapes=[
            pltpu.VMEM((total // width, width, width), low_type),
            pltpu.VMEM((total // width + 1, width, width), wide_type),
        ],
        compiler_params=params(12),
        cost_estimate=pl.CostEstimate(flops=2 * pairs_all * width**3, bytes_accessed=4 << 20, transcendentals=0),
    )(plan, *map(pinned, (lefts, rights, *chunks[::-1], own, *olds)))


def values_kernel(devices, olds, count, *refs):
    plan_ref, left_ref, right_ref = refs[:3]
    chunk_refs = refs[3 : 3 + devices][::-1]
    own_ref = refs[3 + devices]
    old_refs = refs[4 + devices : 4 + devices + olds]
    state_ref, value_ref, low_ref, sum_ref = refs[4 + devices + olds :]
    rows, width = own_ref.shape
    blocks = rows // width
    fill_low(False, chunk_refs, own_ref, old_refs, low_ref, None, count)
    state_ref[...] = low_ref[:blocks].reshape(rows, width)
    low_ref[devices * blocks] = jnp.zeros((width, width), low_type)
    sum_ref[...] = jnp.zeros_like(sum_ref)

    def group(index, carried):
        products = [
            pair_product(index * GROUP + inner, plan_ref, left_ref, right_ref, low_ref)
            for inner in range(GROUP)
        ]
        for inner, product in enumerate(products):
            place = index * GROUP + inner
            target = low_ref[plan_ref[2, place]].astype(wide_type)
            folded = (product * target).reshape(width // 8, 8, width).sum(axis=0)
            sum_ref[plan_ref[3, place]] += folded
        return carried

    lax.fori_loop(0, (plan_ref[0, plan_ref.shape[1] - 1] + GROUP - 1) // GROUP, group, 0)
    terms = value_ref.shape[0]
    for term in range(terms):
        value_ref[term : term + 1, :] = jnp.full((1, width), jnp.sum(sum_ref[term]) * (1.0 / count))


def term_values(plan, lefts, rights, chunks, own, olds, count, terms):
    devices = len(chunks)
    rows, width = own.shape
    total = devices * rows
    pairs_all = lefts.shape[0]
    return pl.pallas_call(
        functools.partial(values_kernel, devices, len(olds), count),
        out_shape=[jax.ShapeDtypeStruct((rows, width), low_type), jax.ShapeDtypeStruct((terms, width), wide_type)],
        in_specs=[SMEM] + [VMEM] * (3 + devices + len(olds)),
        out_specs=[VMEM] * 2,
        scratch_shapes=[
            pltpu.VMEM((total // width + 1, width, width), low_type),
            pltpu.VMEM((terms + 1, 8, width), wide_type),
        ],
        compiler_params=params(12),
        cost_estimate=pl.CostEstimate(flops=2 * pairs_all * width**3, bytes_accessed=4 << 20, transcendentals=0),
    )(plan, *map(pinned, (lefts, rights, *chunks[::-1], own, *olds)))


def coupling_kernel(own_ref, before_ref, after_ref, out_ref):
    rows, width = own_ref.shape
    for block in range(rows // width):
        at = pl.ds(block * width, width)
        gram = sum(
            lax.dot_general(ref[at, :], ref[at, :], (((0,), (0,)), ((), ())), preferred_element_type=wide_type)
            for ref in (before_ref, after_ref)
        )
        out_ref[at, :] = jnp.dot(
            own_ref[at, :].astype(wide_type), gram, precision=lax.Precision.HIGHEST, preferred_element_type=wide_type
        ) * (0.5 / width)


def coupling(own, before, after):
    rows, width = own.shape
    return pl.pallas_call(
        coupling_kernel,
        out_shape=kept(own.shape, wide_type),
        in_specs=[VMEM] * 3,
        out_specs=VMEM,
        compiler_params=params(4),
        cost_estimate=pl.CostEstimate(flops=0, bytes_accessed=0, transcendentals=0),
    )(*map(pinned, (own, before, after)))


def parts_kernel(*refs):
    *part_refs, out_ref = refs
    for start in range(0, out_ref.shape[0], STRIP):
        at = pl.ds(start, STRIP)
        out_ref[at, :] = sum(ref[at, :].astype(wide_type) for ref in part_refs)


def added(parts):
    shape = parts[0].shape
    return pl.pallas_call(
        parts_kernel,
        out_shape=kept(shape, wide_type),
        in_specs=[VMEM] * len(parts),
        out_specs=VMEM,
        compiler_params=params(4),
        cost_estimate=pl.CostEstimate(flops=1 << 32, bytes_accessed=1 << 24, transcendentals=0),
    )(*map(pinned, parts))


def total_kernel(own_ref, coupled_ref, part_ref, applied_ref, sent_ref):
    rows, width = own_ref.shape
    sums = [jnp.zeros((8, width), wide_type)] * 3
    for start in range(0, rows, STRIP):
        at = pl.ds(start, STRIP)
        applied = coupled_ref[at, :] + part_ref[at, :]
        own = own_ref[at, :].astype(wide_type)
        applied_ref[at, :] = applied
        sent_ref[at, :] = applied.astype(low_type)
        for which, product in enumerate((own * own, own * applied, applied * applied)):
            sums[which] = sums[which] + product.reshape(STRIP // 8, 8, width).sum(axis=0)
    row = lax.broadcasted_iota(jnp.int32, (TAIL, width), 0)
    tail = jnp.zeros((TAIL, width), wide_type)
    for which in range(3):
        rest = jnp.full((TAIL, width), jnp.sum(sums[which]))
        for digit in range(3):
            rounded = rest.astype(low_type).astype(wide_type)
            tail = jnp.where(row == 3 * which + digit, rounded, tail)
            rest = rest - rounded
    sent_ref[rows:, :] = tail.astype(low_type)


def total_applied(own, coupled, part):
    rows, width = own.shape
    return pl.pallas_call(
        total_kernel,
        out_shape=[kept((rows, width), wide_type), kept((rows + TAIL, width), low_type)],
        in_specs=[VMEM] * 3,
        out_specs=[VMEM] * 2,
        compiler_params=params(4),
        cost_estimate=pl.CostEstimate(flops=10 * rows * width, bytes_accessed=rows * width * 16, transcendentals=0),
    )(*map(pinned, (own, coupled, part)))


def shards(psi_start, left_ops, right_ops, shifts, active):
    devices = lax.axis_size("op")
    terms, blocks_all, width = left_ops.shape[1:4]
    blocks_dev = psi_start.shape[1]
    rows = blocks_dev * width
    count = float(blocks_all * width * width)
    term_scale = 1.0 / (terms * devices)
    own_low = psi_start.reshape(rows, width)
    own_wide = own_low
    me = lax.axis_index("op").astype(jnp.int32).reshape(1)
    chunks = gathered(own_low)
    lefts = left_ops.reshape(terms * blocks_all, width, width)
    rights = right_ops.reshape(terms * blocks_all, width, width)
    plan, lefts, rights = make_plan(me, shifts, active[0], lefts, rights, blocks_dev)
    own_source = own_low
    olds = []
    for sweep_index in range(ITERS):
        outs = apply_terms(plan, lefts, rights, chunks, own_source, olds, count, term_scale)
        pieces = outs[:devices]
        if olds:
            fresh, own_low, own_wide = outs[devices:]
            olds = [fresh]
        else:
            olds = chunks
        parts = summed(pieces)
        own_low, _ = lax.optimization_barrier((own_low, parts[1]))
        coupled = coupling(own_wide, *neighbours(own_low))
        own_source, sent = total_applied(own_wide, coupled, added(parts))
        chunks = gathered(sent)
    state, values = term_values(plan, lefts, rights, chunks, own_source, olds, count, terms)
    return state.reshape(psi_start.shape), values[:, 0].reshape(shifts.shape)


def solution(mesh):
    return jax.shard_map(
        shards,
        mesh=mesh,
        in_specs=(
            P("seg", "op", None, None),
            P("seg", "op", None, None, None),
            P("seg", "op", None, None, None),
            P("seg", "op"),
            P("seg", "op", None),
        ),
        out_specs=(P("seg", "op", None, None), P("seg", "op")),
        check_vma=False,
    )
```

time: 236 us -> 175 us (0.74)
  local copies, waits for them, and re-layouts: 34.9 us -> 1.96 us
  starting transfers between devices: 81 us -> 54.6 us
  Pallas kernels: 52.5 us -> 26.8 us
  waiting for transfers between devices: 65.6 us -> 88.8 us
    unnamed x96 -> x6, local copies, waits for them, and re-layouts: 34.2 us -> 1.34 us
    ppermute x49, waiting for transfers between devices: 65.6 us -> 88.7 us  [traded(): return lax.ppermute(block, 'op', route)]
    ppermute x49, starting transfers between devices: 67.9 us -> 45.6 us  [traded(): return lax.ppermute(block, 'op', route)]
    pallas_call x3, Pallas kernels: 24.9 us -> 12.8 us  [apply_terms(): pl.pallas_call(functools.partial(apply_kernel, first, devices, len(olds),...]
    pallas_call x7 -> x10, Pallas kernels: 18.8 us -> 9.18 us  [the longest x1 6.17 us: make_plan(): pl.pallas_call(functools.partial(plan_kernel, blocks_dev), out_shape=[jax...]
    ppermute x6, starting transfers between devices: 13.1 us -> 9.02 us  [neighbours(): found.append(lax.ppermute(block, 'seg', pairs + [(j, i) for i, j in pairs]))]
    pallas_call x1, Pallas kernels: 8.79 us -> 4.84 us  [term_values(): pl.pallas_call(functools.partial(values_kernel, devices, len(olds), count...]
  transfers between devices with their start and end apart: 55 -> 55, of which waited for: 22 -> 30; matrix products, arithmetic and copies ran while one was open for 0% -> 0% of each run, Pallas kernels for 5% -> 5%
where the time goes in v2:
time: 175 us; the launch traced here: 173 us
  waiting for transfers between devices  88.8 us (51%)
  starting transfers between devices  54.6 us (31%)
  Pallas kernels  26.8 us (15%)
  local copies, waits for them, and re-layouts  1.96 us (1%)
    ppermute x49, waiting for transfers between devices, traded(): return lax.ppermute(block, 'op', route)  88.7 us
    ppermute x49, starting transfers between devices, traded(): return lax.ppermute(block, 'op', route)  45.6 us
    pallas_call x3, Pallas kernels, apply_terms(): pl.pallas_call(functools.partial(apply_kernel, first, devices, len(olds),...  12.8 us
    ppermute x6, starting transfers between devices, neighbours(): found.append(lax.ppermute(block, 'seg', pairs + [(j, i) for i, j in pairs]))  9.02 us
    pallas_call x1, Pallas kernels, make_plan(): pl.pallas_call(functools.partial(plan_kernel, blocks_dev), out_shape=[jax...  6.17 us
    pallas_call x1, Pallas kernels, term_values(): pl.pallas_call(functools.partial(values_kernel, devices, len(olds), count...  4.84 us
  transfers between devices with their start and end apart: 55, of which 30 were waited for; matrix products, arithmetic and copies ran while one was open for 0% of the time, Pallas kernels for 5%

profile of v2, /device:TPU:0, one launch (start us, length us, event | category | flops | bytes accessed | tf_op | source)
XLA Modules:
  0.0 173.4 jit_solution(3904995380812594199)
XLA Ops:
  0.6 4.1 %collective-permute-start = (bf16[512,128]{1,0:T(8,128)(2,1)}, bf16[512,128]{1,0:T(8,128)(2,1)S(1)}, u32[]{:S(2)}, u32[]{:S(2)}) collective-permute-start(bf16[512,128]{1,0:T(8,128)(2,1)} %bitcast.7), channel_id=1, source_target_pairs={{0,4},{1,5},{2,6},{3,7},{4,0},{5,1},{6,2},{7,3},{8,12},{9,13},{10,... | collective-permute-start | bytes 393224 | tf_op jit(solution)/shard_map/ppermute | solution.py:36
  4.7 1.5 collective-permute-start.4
  6.2 5.0 %collective-permute-done.refs_6_.refs_16_ = bf16[512,128]{1,0:T(8,128)(2,1)S(1)} collective-permute-done((bf16[512,128]{1,0:T(8,128)(2,1)}, bf16[512,128]{1,0:T(8,128)(2,1)S(1)}, u32[]{:S(2)}, u32[]{:S(2)}) %collective-permute-start) | collective-permute-done | bytes 131104 | tf_op jit(solution)/shard_map/ppermute | solution.py:36
  12.1 1.2 collective-permute-start.6
  13.3 1.5 collective-permute-start.3
  15.6 2.0 %collective-permute-done.1.refs_4_.refs_18_ = bf16[512,128]{1,0:T(8,128)(2,1)S(1)} collective-permute-done((bf16[512,128]{1,0:T(8,128)(2,1)S(1)}, bf16[512,128]{1,0:T(8,128)(2,1)S(1)}, u32[]{:S(2)}, u32[]{:S(2)}) %collective-permute-start.1) | collective-permute-done | bytes 131104 | tf_op jit(solution)/shard_map/ppermute | solution.py:36
  17.6 1.5 collective-permute-start.2
  20.5 6.2 %shard_map.68 = (s32[4,137]{1,0:T(4,128)S(1)}, bf16[128,128,128]{2,1,0:T(8,128)(2,1)S(1)}, bf16[128,128,128]{2,1,0:T(8,128)(2,1)S(1)}) custom-call(s32[1]{0:T(128)} %bitcast.me_ref, s32[1,4]{1,0:T(1,128)S(1)} %copy-done.2, s32[4,32]{1,0:T(4,128)S(1)} %bitcast.17, bf16[128,128,128]{2,1,0:T(8,128)(2,1)} %bitcast.18, bf16[128,128,128]{2,1,0:T(8,128)(2,1)} %bitcast.19), custom_call_target="tpu_custom_call" | custom-call | bytes 16777216 | tf_op jit(solution)/shard_map/pallas_call | solution.py:129
  26.7 4.1 %shard_map.69 = (f32[512,128]{1,0:T(8,128)S(1)}, f32[512,128]{1,0:T(8,128)S(1)}, bf16[512,128]{1,0:T(8,128)(2,1)S(1)}, bf16[512,128]{1,0:T(8,128)(2,1)S(1)}, f32...) custom-call(s32[4,137]{1,0:T(4,128)S(1)} %get-tuple-element.46.refs_0, ...), custom_call_target="tpu_custom_call" | custom-call | flops 536870912 | bytes 4194304 | tf_op jit(solution)/shard_map/pallas_call | solution.py:235
  33.1 2.8 %collective-permute-done.7 = bf16[512,128]{1,0:T(8,128)(2,1)S(1)} collective-permute-done((bf16[512,128]{1,0:T(8,128)(2,1)S(1)}, bf16[512,128]{1,0:T(8,128)(2,1)S(1)}, u32[]{:S(2)}, u32[]{:S(2)}) %collective-permute-start.7) | collective-permute-done | bytes 131104 | tf_op jit(solution)/shard_map/ppermute | solution.py:36
  35.9 1.1 collective-permute-start.8
  37.0 1.3 collective-permute-done.13
  38.4 1.4 collective-permute-start.14
  41.6 3.1 %collective-permute-start.9 = (bf16[512,128]{1,0:T(8,128)(2,1)S(1)}, bf16[512,128]{1,0:T(8,128)(2,1)S(1)}, u32[]{:S(2)}, u32[]{:S(2)}) collective-permute-start(bf16[512,128]{1,0:T(8,128)(2,1)S(1)} %bitcast.13), channel_id=1, source_target_pairs={{0,8},{16,24},{8,0},{24,16},{1,9},{17,25},{9,1},{25,17},{2,10},{18... | collective-permute-start | bytes 393224 | tf_op jit(solution)/shard_map/ppermute | solution.py:44
  44.7 3.8 %collective-permute-start.15 = (bf16[512,128]{1,0:T(8,128)(2,1)S(1)}, bf16[512,128]{1,0:T(8,128)(2,1)S(1)}, u32[]{:S(2)}, u32[]{:S(2)}) collective-permute-start(bf16[512,128]{1,0:T(8,128)(2,1)S(1)} %add_convert_fusion.6), channel_id=1, source_target_pairs={{0,4},{1,5},{2,6},{3,7},{4,0},{5,1},{6,2},{7,3},{8,12},{9,13},{10,... | collective-permute-start | bytes 393224 | tf_op jit(solution)/shard_map/ppermute | solution.py:36
  49.3 5.3 %collective-permute-done.15.refs_3_ = bf16[512,128]{1,0:T(8,128)(2,1)S(1)} collective-permute-done((bf16[512,128]{1,0:T(8,128)(2,1)S(1)}, bf16[512,128]{1,0:T(8,128)(2,1)S(1)}, u32[]{:S(2)}, u32[]{:S(2)}) %collective-permute-start.15) | collective-permute-done | bytes 131104 | tf_op jit(solution)/shard_map/ppermute | solution.py:36
  55.5 8.1 %collective-permute-done.16.refs_6_ = bf16[528,128]{1,0:T(8,128)(2,1)S(1)} collective-permute-done((bf16[528,128]{1,0:T(8,128)(2,1)S(1)}, bf16[528,128]{1,0:T(8,128)(2,1)S(1)}, u32[]{:S(2)}, u32[]{:S(2)}) %collective-permute-start.16) | collective-permute-done | bytes 135200 | tf_op jit(solution)/shard_map/ppermute | solution.py:36
  63.7 2.0 %collective-permute-start.22 = (bf16[528,128]{1,0:T(8,128)(2,1)S(1)}, bf16[528,128]{1,0:T(8,128)(2,1)S(1)}, u32[]{:S(2)}, u32[]{:S(2)}) collective-permute-start(bf16[528,128]{1,0:T(8,128)(2,1)S(1)} %get-tuple-element.58.refs_10_), channel_id=1, source_target_pairs={{0,2},{1,3},{2,0},{3,1},{4,6},{5,7},{6,4},{7,5},{8,10},{9,11},{10,... | collective-permute-start | bytes 405512 | tf_op jit(solution)/shard_map/ppermute | solution.py:36
  66.4 3.8 %collective-permute-done.17.refs_4_ = bf16[528,128]{1,0:T(8,128)(2,1)S(1)} collective-permute-done((bf16[528,128]{1,0:T(8,128)(2,1)S(1)}, bf16[528,128]{1,0:T(8,128)(2,1)S(1)}, u32[]{:S(2)}, u32[]{:S(2)}) %collective-permute-start.17) | collective-permute-done | bytes 135200 | tf_op jit(solution)/shard_map/ppermute | solution.py:36
  70.8 1.9 %collective-permute-done.22.refs_8_ = bf16[528,128]{1,0:T(8,128)(2,1)S(1)} collective-permute-done((bf16[528,128]{1,0:T(8,128)(2,1)S(1)}, bf16[528,128]{1,0:T(8,128)(2,1)S(1)}, u32[]{:S(2)}, u32[]{:S(2)}) %collective-permute-start.22) | collective-permute-done | bytes 135200 | tf_op jit(solution)/shard_map/ppermute | solution.py:36
  72.7 1.4 collective-permute-done.21.refs_7_
  75.2 4.4 %shard_map.73 = (f32[512,128]{1,0:T(8,128)S(1)}, f32[512,128]{1,0:T(8,128)S(1)}, bf16[512,128]{1,0:T(8,128)(2,1)S(1)}, bf16[512,128]{1,0:T(8,128)(2,1)S(1)}, f32...) custom-call(s32[4,137]{1,0:T(4,128)S(1)} %get-tuple-element.46.refs_, ...), custom_call_target="tpu_custom_call" | custom-call | flops 536870912 | bytes 4194304 | tf_op jit(solution)/shard_map/pallas_call | solution.py:235
  79.7 1.1 collective-permute-start.28
  81.8 2.9 %collective-permute-done.23 = bf16[512,128]{1,0:T(8,128)(2,1)S(1)} collective-permute-done((bf16[512,128]{1,0:T(8,128)(2,1)S(1)}, bf16[512,128]{1,0:T(8,128)(2,1)S(1)}, u32[]{:S(2)}, u32[]{:S(2)}) %collective-permute-start.23) | collective-permute-done | bytes 131104 | tf_op jit(solution)/shard_map/ppermute | solution.py:36
  85.8 1.8 %collective-permute-done.29 = bf16[512,128]{1,0:T(8,128)(2,1)S(1)} collective-permute-done((bf16[512,128]{1,0:T(8,128)(2,1)S(1)}, bf16[512,128]{1,0:T(8,128)(2,1)S(1)}, u32[]{:S(2)}, u32[]{:S(2)}) %collective-permute-start.29) | collective-permute-done | bytes 131104 | tf_op jit(solution)/shard_map/ppermute | solution.py:36
  87.6 1.2 collective-permute-start.30
  90.4 2.0 %collective-permute-start.25 = (bf16[512,128]{1,0:T(8,128)(2,1)S(1)}, bf16[512,128]{1,0:T(8,128)(2,1)S(1)}, u32[]{:S(2)}, u32[]{:S(2)}) collective-permute-start(bf16[512,128]{1,0:T(8,128)(2,1)S(1)} %get-tuple-element.64), channel_id=1, source_target_pairs={{0,8},{16,24},{8,0},{24,16},{1,9},{17,25},{9,1},{25,17},{2,10},{18... | collective-permute-start | bytes 393224 | tf_op jit(solution)/shard_map/ppermute | solution.py:44
  92.6 1.9 %collective-permute-start.31 = (bf16[512,128]{1,0:T(8,128)(2,1)S(1)}, bf16[512,128]{1,0:T(8,128)(2,1)S(1)}, u32[]{:S(2)}, u32[]{:S(2)}) collective-permute-start(bf16[512,128]{1,0:T(8,128)(2,1)S(1)} %add_convert_fusion.3), channel_id=1, source_target_pairs={{0,4},{1,5},{2,6},{3,7},{4,0},{5,1},{6,2},{7,3},{8,12},{9,13},{10,... | collective-permute-start | bytes 393224 | tf_op jit(solution)/shard_map/ppermute | solution.py:36
  95.3 6.4 %collective-permute-done.31.refs_3_ = bf16[512,128]{1,0:T(8,128)(2,1)S(1)} collective-permute-done((bf16[512,128]{1,0:T(8,128)(2,1)S(1)}, bf16[512,128]{1,0:T(8,128)(2,1)S(1)}, u32[]{:S(2)}, u32[]{:S(2)}) %collective-permute-start.31) | collective-permute-done | bytes 131104 | tf_op jit(solution)/shard_map/ppermute | solution.py:36
  102.8 6.8 %collective-permute-done.32.refs_6_ = bf16[528,128]{1,0:T(8,128)(2,1)S(1)} collective-permute-done((bf16[528,128]{1,0:T(8,128)(2,1)S(1)}, bf16[528,128]{1,0:T(8,128)(2,1)S(1)}, u32[]{:S(2)}, u32[]{:S(2)}) %collective-permute-start.32) | collective-permute-done | bytes 135200 | tf_op jit(solution)/shard_map/ppermute | solution.py:36
  109.7 2.0 %collective-permute-start.38 = (bf16[528,128]{1,0:T(8,128)(2,1)S(1)}, bf16[528,128]{1,0:T(8,128)(2,1)S(1)}, u32[]{:S(2)}, u32[]{:S(2)}) collective-permute-start(bf16[528,128]{1,0:T(8,128)(2,1)S(1)} %get-tuple-element.71.refs_10_), channel_id=1, source_target_pairs={{0,2},{1,3},{2,0},{3,1},{4,6},{5,7},{6,4},{7,5},{8,10},{9,11},{10,... | collective-permute-start | bytes 405512 | tf_op jit(solution)/shard_map/ppermute | solution.py:36
  111.8 4.3 %collective-permute-done.33.refs_4_ = bf16[528,128]{1,0:T(8,128)(2,1)S(1)} collective-permute-done((bf16[528,128]{1,0:T(8,128)(2,1)S(1)}, bf16[528,128]{1,0:T(8,128)(2,1)S(1)}, u32[]{:S(2)}, u32[]{:S(2)}) %collective-permute-start.33) | collective-permute-done | bytes 135200 | tf_op jit(solution)/shard_map/ppermute | solution.py:36
  116.2 2.9 %collective-permute-done.38.refs_8_ = bf16[528,128]{1,0:T(8,128)(2,1)S(1)} collective-permute-done((bf16[528,128]{1,0:T(8,128)(2,1)S(1)}, bf16[528,128]{1,0:T(8,128)(2,1)S(1)}, u32[]{:S(2)}, u32[]{:S(2)}) %collective-permute-start.38) | collective-permute-done | bytes 135200 | tf_op jit(solution)/shard_map/ppermute | solution.py:36
  119.0 2.0 %collective-permute-done.37.refs_7_ = bf16[528,128]{1,0:T(8,128)(2,1)S(1)} collective-permute-done((bf16[528,128]{1,0:T(8,128)(2,1)S(1)}, bf16[528,128]{1,0:T(8,128)(2,1)S(1)}, u32[]{:S(2)}, u32[]{:S(2)}) %collective-permute-start.37) | collective-permute-done | bytes 135200 | tf_op jit(solution)/shard_map/ppermute | solution.py:36
  121.1 4.3 %shard_map.77 = (f32[512,128]{1,0:T(8,128)S(1)}, f32[512,128]{1,0:T(8,128)S(1)}, bf16[512,128]{1,0:T(8,128)(2,1)S(1)}, bf16[512,128]{1,0:T(8,128)(2,1)S(1)}, f32...) custom-call(s32[4,137]{1,0:T(4,128)S(1)} %get-tuple-element.46.refs_, ...), custom_call_target="tpu_custom_call" | custom-call | flops 536870912 | bytes 4194304 | tf_op jit(solution)/shard_map/pallas_call | solution.py:235
  126.1 1.6 collective-permute-start.45
  127.7 2.9 %collective-permute-done.39 = bf16[512,128]{1,0:T(8,128)(2,1)S(1)} collective-permute-done((bf16[512,128]{1,0:T(8,128)(2,1)S(1)}, bf16[512,128]{1,0:T(8,128)(2,1)S(1)}, u32[]{:S(2)}, u32[]{:S(2)}) %collective-permute-start.39) | collective-permute-done | bytes 131104 | tf_op jit(solution)/shard_map/ppermute | solution.py:36
  131.1 3.6 %collective-permute-done.45 = bf16[512,128]{1,0:T(8,128)(2,1)S(1)} collective-permute-done((bf16[512,128]{1,0:T(8,128)(2,1)S(1)}, bf16[512,128]{1,0:T(8,128)(2,1)S(1)}, u32[]{:S(2)}, u32[]{:S(2)}) %collective-permute-start.45) | collective-permute-done | bytes 131104 | tf_op jit(solution)/shard_map/ppermute | solution.py:36
  134.7 1.7 collective-permute-start.46
  137.5 2.0 %collective-permute-start.41 = (bf16[512,128]{1,0:T(8,128)(2,1)S(1)}, bf16[512,128]{1,0:T(8,128)(2,1)S(1)}, u32[]{:S(2)}, u32[]{:S(2)}) collective-permute-start(bf16[512,128]{1,0:T(8,128)(2,1)S(1)} %get-tuple-element.78), channel_id=1, source_target_pairs={{0,8},{16,24},{8,0},{24,16},{1,9},{17,25},{9,1},{25,17},{2,10},{18... | collective-permute-start | bytes 393224 | tf_op jit(solution)/shard_map/ppermute | solution.py:44
  139.8 2.6 %collective-permute-start.47 = (bf16[512,128]{1,0:T(8,128)(2,1)S(1)}, bf16[512,128]{1,0:T(8,128)(2,1)S(1)}, u32[]{:S(2)}, u32[]{:S(2)}) collective-permute-start(bf16[512,128]{1,0:T(8,128)(2,1)S(1)} %add_convert_fusion), channel_id=1, source_target_pairs={{0,4},{1,5},{2,6},{3,7},{4,0},{5,1},{6,2},{7,3},{8,12},{9,13},{10,... | collective-permute-start | bytes 393224 | tf_op jit(solution)/shard_map/ppermute | solution.py:36
  143.1 5.6 %collective-permute-done.47.refs_3_ = bf16[512,128]{1,0:T(8,128)(2,1)S(1)} collective-permute-done((bf16[512,128]{1,0:T(8,128)(2,1)S(1)}, bf16[512,128]{1,0:T(8,128)(2,1)S(1)}, u32[]{:S(2)}, u32[]{:S(2)}) %collective-permute-start.47) | collective-permute-done | bytes 131104 | tf_op jit(solution)/shard_map/ppermute | solution.py:36
  149.4 7.1 %collective-permute-done.48.refs_6_ = bf16[528,128]{1,0:T(8,128)(2,1)S(1)} collective-permute-done((bf16[528,128]{1,0:T(8,128)(2,1)S(1)}, bf16[528,128]{1,0:T(8,128)(2,1)S(1)}, u32[]{:S(2)}, u32[]{:S(2)}) %collective-permute-start.48) | collective-permute-done | bytes 135200 | tf_op jit(solution)/shard_map/ppermute | solution.py:36
  156.5 2.0 %collective-permute-start.54 = (bf16[528,128]{1,0:T(8,128)(2,1)S(1)}, bf16[528,128]{1,0:T(8,128)(2,1)S(1)}, u32[]{:S(2)}, u32[]{:S(2)}) collective-permute-start(bf16[528,128]{1,0:T(8,128)(2,1)S(1)} %get-tuple-element.85.refs_10_), channel_id=1, source_target_pairs={{0,2},{1,3},{2,0},{3,1},{4,6},{5,7},{6,4},{7,5},{8,10},{9,11},{10,... | collective-permute-start | bytes 405512 | tf_op jit(solution)/shard_map/ppermute | solution.py:36
  158.9 4.0 %collective-permute-done.49.refs_4_ = bf16[528,128]{1,0:T(8,128)(2,1)S(1)} collective-permute-done((bf16[528,128]{1,0:T(8,128)(2,1)S(1)}, bf16[528,128]{1,0:T(8,128)(2,1)S(1)}, u32[]{:S(2)}, u32[]{:S(2)}) %collective-permute-start.49) | collective-permute-done | bytes 135200 | tf_op jit(solution)/shard_map/ppermute | solution.py:36
  163.3 2.6 %collective-permute-done.54.refs_8_ = bf16[528,128]{1,0:T(8,128)(2,1)S(1)} collective-permute-done((bf16[528,128]{1,0:T(8,128)(2,1)S(1)}, bf16[528,128]{1,0:T(8,128)(2,1)S(1)}, u32[]{:S(2)}, u32[]{:S(2)}) %collective-permute-start.54) | collective-permute-done | bytes 135200 | tf_op jit(solution)/shard_map/ppermute | solution.py:36
  165.8 2.0 %collective-permute-done.53.refs_7_ = bf16[528,128]{1,0:T(8,128)(2,1)S(1)} collective-permute-done((bf16[528,128]{1,0:T(8,128)(2,1)S(1)}, bf16[528,128]{1,0:T(8,128)(2,1)S(1)}, u32[]{:S(2)}, u32[]{:S(2)}) %collective-permute-start.53) | collective-permute-done | bytes 135200 | tf_op jit(solution)/shard_map/ppermute | solution.py:36
  167.9 4.8 %shard_map.81 = (bf16[512,128]{1,0:T(8,128)(2,1)}, f32[4,128]{1,0:T(4,128)S(1)}) custom-call(s32[4,137]{1,0:T(4,128)S(1)} %get-tuple-element.46.refs_0_, bf16[128,128,128]{2,1,0:T(8,128)(2,1)S(1)} %get-tuple-element.47.refs_1_, bf16[128,128,128]{2,1,0:T(8,128)(2,1)S(1)} %get-tuple-element.48.refs_2_, bf16[528,128]{1,0:T(8,128)(2,1)S(1)} %collective-permute-done.50.refs_3_, ...), custom_call_target="tpu_custom_call" | custom-call | flops 536870912 | bytes 4194304 | tf_op jit(solution)/shard_map/pallas_call | solution.py:285
  (92 shorter events, 22.8 us)
Async XLA Ops:
  0.6 10.6 %collective-permute-start = (bf16[512,128]{1,0:T(8,128)(2,1)}, bf16[512,128]{1,0:T(8,128)(2,1)S(1)}, u32[]{:S(2)}, u32[]{:S(2)}) collective-permute-start(bf16[512,128]{1,0:T(8,128)(2,1)} %bitcast.7), channel_id=1, source_target_pairs={{0,4},{1,5},{2,6},{3,7},{4,0},{5,1},{6,2},{7,3},{8,12},{9,13},{10,... | collective-permute-start | bytes 393224 | tf_op jit(solution)/shard_map/ppermute | solution.py:36
  4.7 10.1 %collective-permute-start.4 = (bf16[512,128]{1,0:T(8,128)(2,1)}, bf16[512,128]{1,0:T(8,128)(2,1)S(1)}, u32[]{:S(2)}, u32[]{:S(2)}) collective-permute-start(bf16[512,128]{1,0:T(8,128)(2,1)} %bitcast.8), channel_id=1, source_target_pairs={{0,1},{1,0},{2,3},{3,2},{4,5},{5,4},{6,7},{7,6},{8,9},{9,8},{10,11... | collective-permute-start | bytes 393224 | tf_op jit(solution)/shard_map/ppermute | solution.py:36
  11.2 6.4 %collective-permute-start.1 = (bf16[512,128]{1,0:T(8,128)(2,1)S(1)}, bf16[512,128]{1,0:T(8,128)(2,1)S(1)}, u32[]{:S(2)}, u32[]{:S(2)}) collective-permute-start(bf16[512,128]{1,0:T(8,128)(2,1)S(1)} %collective-permute-done.refs_6_.refs_16_), channel_id=1, source_target_pairs={{0,2},{1,3},{2,0},{3,1},{4,6},{5,7},{6,4},{7,5},{8,10},{9,11},{10,... | collective-permute-start | bytes 393224 | tf_op jit(solution)/shard_map/ppermute | solution.py:36
  12.1 14.6 %collective-permute-start.6 = (bf16[512,128]{1,0:T(8,128)(2,1)}, bf16[512,128]{1,0:T(8,128)(2,1)S(1)}, u32[]{:S(2)}, u32[]{:S(2)}) collective-permute-start(bf16[512,128]{1,0:T(8,128)(2,1)} %bitcast.9), channel_id=1, source_target_pairs={{0,2},{1,3},{2,0},{3,1},{4,6},{5,7},{6,4},{7,5},{8,10},{9,11},{10,... | collective-permute-start | bytes 393224 | tf_op jit(solution)/shard_map/ppermute | solution.py:36
  13.3 13.4 %collective-permute-start.3 = (bf16[512,128]{1,0:T(8,128)(2,1)S(1)}, bf16[512,128]{1,0:T(8,128)(2,1)S(1)}, u32[]{:S(2)}, u32[]{:S(2)}) collective-permute-start(bf16[512,128]{1,0:T(8,128)(2,1)S(1)} %collective-permute-done.refs_6_.refs_16_), channel_id=1, source_target_pairs={{0,1},{1,0},{2,3},{3,2},{4,5},{5,4},{6,7},{7,6},{8,9},{9,8},{10,11... | collective-permute-start | bytes 393224 | tf_op jit(solution)/shard_map/ppermute | solution.py:36
  14.8 11.9 %collective-permute-start.5 = (bf16[512,128]{1,0:T(8,128)(2,1)S(1)}, bf16[512,128]{1,0:T(8,128)(2,1)S(1)}, u32[]{:S(2)}, u32[]{:S(2)}) collective-permute-start(bf16[512,128]{1,0:T(8,128)(2,1)S(1)} %collective-permute-done.4.refs_9_.refs_13_), channel_id=1, source_target_pairs={{0,2},{1,3},{2,0},{3,1},{4,6},{5,7},{6,4},{7,5},{8,10},{9,11},{10,... | collective-permute-start | bytes 393224 | tf_op jit(solution)/shard_map/ppermute | solution.py:36
  17.6 9.1 %collective-permute-start.2 = (bf16[512,128]{1,0:T(8,128)(2,1)S(1)}, bf16[512,128]{1,0:T(8,128)(2,1)S(1)}, u32[]{:S(2)}, u32[]{:S(2)}) collective-permute-start(bf16[512,128]{1,0:T(8,128)(2,1)S(1)} %collective-permute-done.1.refs_4_.refs_18_), channel_id=1, source_target_pairs={{0,1},{1,0},{2,3},{3,2},{4,5},{5,4},{6,7},{7,6},{8,9},{9,8},{10,11... | collective-permute-start | bytes 393224 | tf_op jit(solution)/shard_map/ppermute | solution.py:36
  30.8 5.0 %collective-permute-start.7 = (bf16[512,128]{1,0:T(8,128)(2,1)S(1)}, bf16[512,128]{1,0:T(8,128)(2,1)S(1)}, u32[]{:S(2)}, u32[]{:S(2)}) collective-permute-start(bf16[512,128]{1,0:T(8,128)(2,1)S(1)} %get-tuple-element.50), channel_id=1, source_target_pairs={{0,2},{1,3},{2,0},{3,1},{4,6},{5,7},{6,4},{7,5},{8,10},{9,11},{10,... | collective-permute-start | bytes 393224 | tf_op jit(solution)/shard_map/ppermute | solution.py:36
  31.1 13.6 %collective-permute-start.12 = (bf16[512,128]{1,0:T(8,128)(2,1)S(1)}, bf16[512,128]{1,0:T(8,128)(2,1)S(1)}, u32[]{:S(2)}, u32[]{:S(2)}) collective-permute-start(bf16[512,128]{1,0:T(8,128)(2,1)S(1)} %get-tuple-element.55), channel_id=1, source_target_pairs={{0,1},{1,0},{2,3},{3,2},{4,5},{5,4},{6,7},{7,6},{8,9},{9,8},{10,11... | collective-permute-start | bytes 393224 | tf_op jit(solution)/shard_map/ppermute | solution.py:36
  32.0 6.3 %collective-permute-start.13 = (bf16[512,128]{1,0:T(8,128)(2,1)S(1)}, bf16[512,128]{1,0:T(8,128)(2,1)S(1)}, u32[]{:S(2)}, u32[]{:S(2)}) collective-permute-start(bf16[512,128]{1,0:T(8,128)(2,1)S(1)} %get-tuple-element.57), channel_id=1, source_target_pairs={{0,1},{1,0},{2,3},{3,2},{4,5},{5,4},{6,7},{7,6},{8,9},{9,8},{10,11... | collective-permute-start | bytes 393224 | tf_op jit(solution)/shard_map/ppermute | solution.py:36
  35.9 5.0 %collective-permute-start.8 = (bf16[512,128]{1,0:T(8,128)(2,1)S(1)}, bf16[512,128]{1,0:T(8,128)(2,1)S(1)}, u32[]{:S(2)}, u32[]{:S(2)}) collective-permute-start(bf16[512,128]{1,0:T(8,128)(2,1)S(1)} %add_convert_fusion.8), channel_id=1, source_target_pairs={{0,1},{1,0},{2,3},{3,2},{4,5},{5,4},{6,7},{7,6},{8,9},{9,8},{10,11... | collective-permute-start | bytes 393224 | tf_op jit(solution)/shard_map/ppermute | solution.py:36
  38.4 6.3 %collective-permute-start.14 = (bf16[512,128]{1,0:T(8,128)(2,1)S(1)}, bf16[512,128]{1,0:T(8,128)(2,1)S(1)}, u32[]{:S(2)}, u32[]{:S(2)}) collective-permute-start(bf16[512,128]{1,0:T(8,128)(2,1)S(1)} %add_convert_fusion.7), channel_id=1, source_target_pairs={{0,2},{1,3},{2,0},{3,1},{4,6},{5,7},{6,4},{7,5},{8,10},{9,11},{10,... | collective-permute-start | bytes 393224 | tf_op jit(solution)/shard_map/ppermute | solution.py:36
  39.8 9.5 %collective-permute-start.11 = (bf16[512,128]{1,0:T(8,128)(2,1)S(1)}, bf16[512,128]{1,0:T(8,128)(2,1)S(1)}, u32[]{:S(2)}, u32[]{:S(2)}) collective-permute-start(bf16[512,128]{1,0:T(8,128)(2,1)S(1)} %get-tuple-element.53), channel_id=1, source_target_pairs={{0,2},{1,3},{2,0},{3,1},{4,6},{5,7},{6,4},{7,5},{8,10},{9,11},{10,... | collective-permute-start | bytes 393224 | tf_op jit(solution)/shard_map/ppermute | solution.py:36
  40.9 7.6 %collective-permute-start.10 = (bf16[512,128]{1,0:T(8,128)(2,1)S(1)}, bf16[512,128]{1,0:T(8,128)(2,1)S(1)}, u32[]{:S(2)}, u32[]{:S(2)}) collective-permute-start(bf16[512,128]{1,0:T(8,128)(2,1)S(1)} %bitcast.12), channel_id=1, source_target_pairs={{8,16},{16,8},{9,17},{17,9},{10,18},{18,10},{11,19},{19,11},{12,20... | collective-permute-start | bytes 393224 | tf_op jit(solution)/shard_map/ppermute | solution.py:44
  41.6 7.0 %collective-permute-start.9 = (bf16[512,128]{1,0:T(8,128)(2,1)S(1)}, bf16[512,128]{1,0:T(8,128)(2,1)S(1)}, u32[]{:S(2)}, u32[]{:S(2)}) collective-permute-start(bf16[512,128]{1,0:T(8,128)(2,1)S(1)} %bitcast.13), channel_id=1, source_target_pairs={{0,8},{16,24},{8,0},{24,16},{1,9},{17,25},{9,1},{25,17},{2,10},{18... | collective-permute-start | bytes 393224 | tf_op jit(solution)/shard_map/ppermute | solution.py:44
  44.7 9.9 %collective-permute-start.15 = (bf16[512,128]{1,0:T(8,128)(2,1)S(1)}, bf16[512,128]{1,0:T(8,128)(2,1)S(1)}, u32[]{:S(2)}, u32[]{:S(2)}) collective-permute-start(bf16[512,128]{1,0:T(8,128)(2,1)S(1)} %add_convert_fusion.6), channel_id=1, source_target_pairs={{0,4},{1,5},{2,6},{3,7},{4,0},{5,1},{6,2},{7,3},{8,12},{9,13},{10,... | collective-permute-start | bytes 393224 | tf_op jit(solution)/shard_map/ppermute | solution.py:36
  54.8 8.8 %collective-permute-start.16 = (bf16[528,128]{1,0:T(8,128)(2,1)S(1)}, bf16[528,128]{1,0:T(8,128)(2,1)S(1)}, u32[]{:S(2)}, u32[]{:S(2)}) collective-permute-start(bf16[528,128]{1,0:T(8,128)(2,1)S(1)} %get-tuple-element.58.refs_10_), channel_id=1, source_target_pairs={{0,4},{1,5},{2,6},{3,7},{4,0},{5,1},{6,2},{7,3},{8,12},{9,13},{10,... | collective-permute-start | bytes 405512 | tf_op jit(solution)/shard_map/ppermute | solution.py:36
  54.9 11.4 %collective-permute-start.20 = (bf16[528,128]{1,0:T(8,128)(2,1)S(1)}, bf16[528,128]{1,0:T(8,128)(2,1)S(1)}, u32[]{:S(2)}, u32[]{:S(2)}) collective-permute-start(bf16[528,128]{1,0:T(8,128)(2,1)S(1)} %get-tuple-element.58.refs_10_), channel_id=1, source_target_pairs={{0,1},{1,0},{2,3},{3,2},{4,5},{5,4},{6,7},{7,6},{8,9},{9,8},{10,11... | collective-permute-start | bytes 405512 | tf_op jit(solution)/shard_map/ppermute | solution.py:36
  63.7 6.5 %collective-permute-start.17 = (bf16[528,128]{1,0:T(8,128)(2,1)S(1)}, bf16[528,128]{1,0:T(8,128)(2,1)S(1)}, u32[]{:S(2)}, u32[]{:S(2)}) collective-permute-start(bf16[528,128]{1,0:T(8,128)(2,1)S(1)} %collective-permute-done.16.refs_6_), channel_id=1, source_target_pairs={{0,2},{1,3},{2,0},{3,1},{4,6},{5,7},{6,4},{7,5},{8,10},{9,11},{10,... | collective-permute-start | bytes 405512 | tf_op jit(solution)/shard_map/ppermute | solution.py:36
  63.7 9.0 %collective-permute-start.22 = (bf16[528,128]{1,0:T(8,128)(2,1)S(1)}, bf16[528,128]{1,0:T(8,128)(2,1)S(1)}, u32[]{:S(2)}, u32[]{:S(2)}) collective-permute-start(bf16[528,128]{1,0:T(8,128)(2,1)S(1)} %get-tuple-element.58.refs_10_), channel_id=1, source_target_pairs={{0,2},{1,3},{2,0},{3,1},{4,6},{5,7},{6,4},{7,5},{8,10},{9,11},{10,... | collective-permute-start | bytes 405512 | tf_op jit(solution)/shard_map/ppermute | solution.py:36
  65.7 8.5 %collective-permute-start.19 = (bf16[528,128]{1,0:T(8,128)(2,1)S(1)}, bf16[528,128]{1,0:T(8,128)(2,1)S(1)}, u32[]{:S(2)}, u32[]{:S(2)}) collective-permute-start(bf16[528,128]{1,0:T(8,128)(2,1)S(1)} %collective-permute-done.16.refs_6_), channel_id=1, source_target_pairs={{0,1},{1,0},{2,3},{3,2},{4,5},{5,4},{6,7},{7,6},{8,9},{9,8},{10,11... | collective-permute-start | bytes 405512 | tf_op jit(solution)/shard_map/ppermute | solution.py:36
  66.3 7.8 %collective-permute-start.21 = (bf16[528,128]{1,0:T(8,128)(2,1)S(1)}, bf16[528,128]{1,0:T(8,128)(2,1)S(1)}, u32[]{:S(2)}, u32[]{:S(2)}) collective-permute-start(bf16[528,128]{1,0:T(8,128)(2,1)S(1)} %collective-permute-done.20.refs_9_), channel_id=1, source_target_pairs={{0,2},{1,3},{2,0},{3,1},{4,6},{5,7},{6,4},{7,5},{8,10},{9,11},{10,... | collective-permute-start | bytes 405512 | tf_op jit(solution)/shard_map/ppermute | solution.py:36
  79.6 5.0 %collective-permute-start.23 = (bf16[512,128]{1,0:T(8,128)(2,1)S(1)}, bf16[512,128]{1,0:T(8,128)(2,1)S(1)}, u32[]{:S(2)}, u32[]{:S(2)}) collective-permute-start(bf16[512,128]{1,0:T(8,128)(2,1)S(1)} %get-tuple-element.63), channel_id=1, source_target_pairs={{0,2},{1,3},{2,0},{3,1},{4,6},{5,7},{6,4},{7,5},{8,10},{9,11},{10,... | collective-permute-start | bytes 393224 | tf_op jit(solution)/shard_map/ppermute | solution.py:36
  79.7 12.7 %collective-permute-start.28 = (bf16[512,128]{1,0:T(8,128)(2,1)S(1)}, bf16[512,128]{1,0:T(8,128)(2,1)S(1)}, u32[]{:S(2)}, u32[]{:S(2)}) collective-permute-start(bf16[512,128]{1,0:T(8,128)(2,1)S(1)} %get-tuple-element.68), channel_id=1, source_target_pairs={{0,1},{1,0},{2,3},{3,2},{4,5},{5,4},{6,7},{7,6},{8,9},{9,8},{10,11... | collective-permute-start | bytes 393224 | tf_op jit(solution)/shard_map/ppermute | solution.py:36
  80.8 6.8 %collective-permute-start.29 = (bf16[512,128]{1,0:T(8,128)(2,1)S(1)}, bf16[512,128]{1,0:T(8,128)(2,1)S(1)}, u32[]{:S(2)}, u32[]{:S(2)}) collective-permute-start(bf16[512,128]{1,0:T(8,128)(2,1)S(1)} %get-tuple-element.70), channel_id=1, source_target_pairs={{0,1},{1,0},{2,3},{3,2},{4,5},{5,4},{6,7},{7,6},{8,9},{9,8},{10,11... | collective-permute-start | bytes 393224 | tf_op jit(solution)/shard_map/ppermute | solution.py:36
  84.7 5.0 %collective-permute-start.24 = (bf16[512,128]{1,0:T(8,128)(2,1)S(1)}, bf16[512,128]{1,0:T(8,128)(2,1)S(1)}, u32[]{:S(2)}, u32[]{:S(2)}) collective-permute-start(bf16[512,128]{1,0:T(8,128)(2,1)S(1)} %add_convert_fusion.5), channel_id=1, source_target_pairs={{0,1},{1,0},{2,3},{3,2},{4,5},{5,4},{6,7},{7,6},{8,9},{9,8},{10,11... | collective-permute-start | bytes 393224 | tf_op jit(solution)/shard_map/ppermute | solution.py:36
  88.8 6.5 %collective-permute-start.27 = (bf16[512,128]{1,0:T(8,128)(2,1)S(1)}, bf16[512,128]{1,0:T(8,128)(2,1)S(1)}, u32[]{:S(2)}, u32[]{:S(2)}) collective-permute-start(bf16[512,128]{1,0:T(8,128)(2,1)S(1)} %get-tuple-element.66), channel_id=1, source_target_pairs={{0,2},{1,3},{2,0},{3,1},{4,6},{5,7},{6,4},{7,5},{8,10},{9,11},{10,... | collective-permute-start | bytes 393224 | tf_op jit(solution)/shard_map/ppermute | solution.py:36
  92.6 9.0 %collective-permute-start.31 = (bf16[512,128]{1,0:T(8,128)(2,1)S(1)}, bf16[512,128]{1,0:T(8,128)(2,1)S(1)}, u32[]{:S(2)}, u32[]{:S(2)}) collective-permute-start(bf16[512,128]{1,0:T(8,128)(2,1)S(1)} %add_convert_fusion.3), channel_id=1, source_target_pairs={{0,4},{1,5},{2,6},{3,7},{4,0},{5,1},{6,2},{7,3},{8,12},{9,13},{10,... | collective-permute-start | bytes 393224 | tf_op jit(solution)/shard_map/ppermute | solution.py:36
  101.9 7.8 %collective-permute-start.32 = (bf16[528,128]{1,0:T(8,128)(2,1)S(1)}, bf16[528,128]{1,0:T(8,128)(2,1)S(1)}, u32[]{:S(2)}, u32[]{:S(2)}) collective-permute-start(bf16[528,128]{1,0:T(8,128)(2,1)S(1)} %get-tuple-element.71.refs_10_), channel_id=1, source_target_pairs={{0,4},{1,5},{2,6},{3,7},{4,0},{5,1},{6,2},{7,3},{8,12},{9,13},{10,... | collective-permute-start | bytes 405512 | tf_op jit(solution)/shard_map/ppermute | solution.py:36
  102.0 9.7 %collective-permute-start.36 = (bf16[528,128]{1,0:T(8,128)(2,1)S(1)}, bf16[528,128]{1,0:T(8,128)(2,1)S(1)}, u32[]{:S(2)}, u32[]{:S(2)}) collective-permute-start(bf16[528,128]{1,0:T(8,128)(2,1)S(1)} %get-tuple-element.71.refs_10_), channel_id=1, source_target_pairs={{0,1},{1,0},{2,3},{3,2},{4,5},{5,4},{6,7},{7,6},{8,9},{9,8},{10,11... | collective-permute-start | bytes 405512 | tf_op jit(solution)/shard_map/ppermute | solution.py:36
  109.7 6.4 %collective-permute-start.33 = (bf16[528,128]{1,0:T(8,128)(2,1)S(1)}, bf16[528,128]{1,0:T(8,128)(2,1)S(1)}, u32[]{:S(2)}, u32[]{:S(2)}) collective-permute-start(bf16[528,128]{1,0:T(8,128)(2,1)S(1)} %collective-permute-done.32.refs_6_), channel_id=1, source_target_pairs={{0,2},{1,3},{2,0},{3,1},{4,6},{5,7},{6,4},{7,5},{8,10},{9,11},{10,... | collective-permute-start | bytes 405512 | tf_op jit(solution)/shard_map/ppermute | solution.py:36
  109.7 9.3 %collective-permute-start.38 = (bf16[528,128]{1,0:T(8,128)(2,1)S(1)}, bf16[528,128]{1,0:T(8,128)(2,1)S(1)}, u32[]{:S(2)}, u32[]{:S(2)}) collective-permute-start(bf16[528,128]{1,0:T(8,128)(2,1)S(1)} %get-tuple-element.71.refs_10_), channel_id=1, source_target_pairs={{0,2},{1,3},{2,0},{3,1},{4,6},{5,7},{6,4},{7,5},{8,10},{9,11},{10,... | collective-permute-start | bytes 405512 | tf_op jit(solution)/shard_map/ppermute | solution.py:36
  111.7 9.3 %collective-permute-start.35 = (bf16[528,128]{1,0:T(8,128)(2,1)S(1)}, bf16[528,128]{1,0:T(8,128)(2,1)S(1)}, u32[]{:S(2)}, u32[]{:S(2)}) collective-permute-start(bf16[528,128]{1,0:T(8,128)(2,1)S(1)} %collective-permute-done.32.refs_6_), channel_id=1, source_target_pairs={{0,1},{1,0},{2,3},{3,2},{4,5},{5,4},{6,7},{7,6},{8,9},{9,8},{10,11... | collective-permute-start | bytes 405512 | tf_op jit(solution)/shard_map/ppermute | solution.py:36
  111.7 9.3 %collective-permute-start.37 = (bf16[528,128]{1,0:T(8,128)(2,1)S(1)}, bf16[528,128]{1,0:T(8,128)(2,1)S(1)}, u32[]{:S(2)}, u32[]{:S(2)}) collective-permute-start(bf16[528,128]{1,0:T(8,128)(2,1)S(1)} %collective-permute-done.36.refs_9_), channel_id=1, source_target_pairs={{0,2},{1,3},{2,0},{3,1},{4,6},{5,7},{6,4},{7,5},{8,10},{9,11},{10,... | collective-permute-start | bytes 405512 | tf_op jit(solution)/shard_map/ppermute | solution.py:36
  125.5 5.0 %collective-permute-start.39 = (bf16[512,128]{1,0:T(8,128)(2,1)S(1)}, bf16[512,128]{1,0:T(8,128)(2,1)S(1)}, u32[]{:S(2)}, u32[]{:S(2)}) collective-permute-start(bf16[512,128]{1,0:T(8,128)(2,1)S(1)} %get-tuple-element.77), channel_id=1, source_target_pairs={{0,2},{1,3},{2,0},{3,1},{4,6},{5,7},{6,4},{7,5},{8,10},{9,11},{10,... | collective-permute-start | bytes 393224 | tf_op jit(solution)/shard_map/ppermute | solution.py:36
  125.6 13.9 %collective-permute-start.44 = (bf16[512,128]{1,0:T(8,128)(2,1)S(1)}, bf16[512,128]{1,0:T(8,128)(2,1)S(1)}, u32[]{:S(2)}, u32[]{:S(2)}) collective-permute-start(bf16[512,128]{1,0:T(8,128)(2,1)S(1)} %get-tuple-element.82), channel_id=1, source_target_pairs={{0,1},{1,0},{2,3},{3,2},{4,5},{5,4},{6,7},{7,6},{8,9},{9,8},{10,11... | collective-permute-start | bytes 393224 | tf_op jit(solution)/shard_map/ppermute | solution.py:36
  126.1 8.6 %collective-permute-start.45 = (bf16[512,128]{1,0:T(8,128)(2,1)S(1)}, bf16[512,128]{1,0:T(8,128)(2,1)S(1)}, u32[]{:S(2)}, u32[]{:S(2)}) collective-permute-start(bf16[512,128]{1,0:T(8,128)(2,1)S(1)} %get-tuple-element.84), channel_id=1, source_target_pairs={{0,1},{1,0},{2,3},{3,2},{4,5},{5,4},{6,7},{7,6},{8,9},{9,8},{10,11... | collective-permute-start | bytes 393224 | tf_op jit(solution)/shard_map/ppermute | solution.py:36
  130.6 6.2 %collective-permute-start.40 = (bf16[512,128]{1,0:T(8,128)(2,1)S(1)}, bf16[512,128]{1,0:T(8,128)(2,1)S(1)}, u32[]{:S(2)}, u32[]{:S(2)}) collective-permute-start(bf16[512,128]{1,0:T(8,128)(2,1)S(1)} %add_convert_fusion.2), channel_id=1, source_target_pairs={{0,1},{1,0},{2,3},{3,2},{4,5},{5,4},{6,7},{7,6},{8,9},{9,8},{10,11... | collective-permute-start | bytes 393224 | tf_op jit(solution)/shard_map/ppermute | solution.py:36
  134.7 5.0 %collective-permute-start.46 = (bf16[512,128]{1,0:T(8,128)(2,1)S(1)}, bf16[512,128]{1,0:T(8,128)(2,1)S(1)}, u32[]{:S(2)}, u32[]{:S(2)}) collective-permute-start(bf16[512,128]{1,0:T(8,128)(2,1)S(1)} %add_convert_fusion.1), channel_id=1, source_target_pairs={{0,2},{1,3},{2,0},{3,1},{4,6},{5,7},{6,4},{7,5},{8,10},{9,11},{10,... | collective-permute-start | bytes 393224 | tf_op jit(solution)/shard_map/ppermute | solution.py:36
  136.4 6.7 %collective-permute-start.43 = (bf16[512,128]{1,0:T(8,128)(2,1)S(1)}, bf16[512,128]{1,0:T(8,128)(2,1)S(1)}, u32[]{:S(2)}, u32[]{:S(2)}) collective-permute-start(bf16[512,128]{1,0:T(8,128)(2,1)S(1)} %get-tuple-element.80), channel_id=1, source_target_pairs={{0,2},{1,3},{2,0},{3,1},{4,6},{5,7},{6,4},{7,5},{8,10},{9,11},{10,... | collective-permute-start | bytes 393224 | tf_op jit(solution)/shard_map/ppermute | solution.py:36
  136.8 5.6 %collective-permute-start.42 = (bf16[512,128]{1,0:T(8,128)(2,1)S(1)}, bf16[512,128]{1,0:T(8,128)(2,1)S(1)}, u32[]{:S(2)}, u32[]{:S(2)}) collective-permute-start(bf16[512,128]{1,0:T(8,128)(2,1)S(1)} %get-tuple-element.78), channel_id=1, source_target_pairs={{8,16},{16,8},{9,17},{17,9},{10,18},{18,10},{11,19},{19,11},{12,20... | collective-permute-start | bytes 393224 | tf_op jit(solution)/shard_map/ppermute | solution.py:44
  139.8 8.9 %collective-permute-start.47 = (bf16[512,128]{1,0:T(8,128)(2,1)S(1)}, bf16[512,128]{1,0:T(8,128)(2,1)S(1)}, u32[]{:S(2)}, u32[]{:S(2)}) collective-permute-start(bf16[512,128]{1,0:T(8,128)(2,1)S(1)} %add_convert_fusion), channel_id=1, source_target_pairs={{0,4},{1,5},{2,6},{3,7},{4,0},{5,1},{6,2},{7,3},{8,12},{9,13},{10,... | collective-permute-start | bytes 393224 | tf_op jit(solution)/shard_map/ppermute | solution.py:36
  149.0 7.5 %collective-permute-start.48 = (bf16[528,128]{1,0:T(8,128)(2,1)S(1)}, bf16[528,128]{1,0:T(8,128)(2,1)S(1)}, u32[]{:S(2)}, u32[]{:S(2)}) collective-permute-start(bf16[528,128]{1,0:T(8,128)(2,1)S(1)} %get-tuple-element.85.refs_10_), channel_id=1, source_target_pairs={{0,4},{1,5},{2,6},{3,7},{4,0},{5,1},{6,2},{7,3},{8,12},{9,13},{10,... | collective-permute-start | bytes 405512 | tf_op jit(solution)/shard_map/ppermute | solution.py:36
  149.1 9.8 %collective-permute-start.52 = (bf16[528,128]{1,0:T(8,128)(2,1)S(1)}, bf16[528,128]{1,0:T(8,128)(2,1)S(1)}, u32[]{:S(2)}, u32[]{:S(2)}) collective-permute-start(bf16[528,128]{1,0:T(8,128)(2,1)S(1)} %get-tuple-element.85.refs_10_), channel_id=1, source_target_pairs={{0,1},{1,0},{2,3},{3,2},{4,5},{5,4},{6,7},{7,6},{8,9},{9,8},{10,11... | collective-permute-start | bytes 405512 | tf_op jit(solution)/shard_map/ppermute | solution.py:36
  156.5 6.4 %collective-permute-start.49 = (bf16[528,128]{1,0:T(8,128)(2,1)S(1)}, bf16[528,128]{1,0:T(8,128)(2,1)S(1)}, u32[]{:S(2)}, u32[]{:S(2)}) collective-permute-start(bf16[528,128]{1,0:T(8,128)(2,1)S(1)} %collective-permute-done.48.refs_6_), channel_id=1, source_target_pairs={{0,2},{1,3},{2,0},{3,1},{4,6},{5,7},{6,4},{7,5},{8,10},{9,11},{10,... | collective-permute-start | bytes 405512 | tf_op jit(solution)/shard_map/ppermute | solution.py:36
  156.5 9.3 %collective-permute-start.54 = (bf16[528,128]{1,0:T(8,128)(2,1)S(1)}, bf16[528,128]{1,0:T(8,128)(2,1)S(1)}, u32[]{:S(2)}, u32[]{:S(2)}) collective-permute-start(bf16[528,128]{1,0:T(8,128)(2,1)S(1)} %get-tuple-element.85.refs_10_), channel_id=1, source_target_pairs={{0,2},{1,3},{2,0},{3,1},{4,6},{5,7},{6,4},{7,5},{8,10},{9,11},{10,... | collective-permute-start | bytes 405512 | tf_op jit(solution)/shard_map/ppermute | solution.py:36
  158.5 9.3 %collective-permute-start.51 = (bf16[528,128]{1,0:T(8,128)(2,1)S(1)}, bf16[528,128]{1,0:T(8,128)(2,1)S(1)}, u32[]{:S(2)}, u32[]{:S(2)}) collective-permute-start(bf16[528,128]{1,0:T(8,128)(2,1)S(1)} %collective-permute-done.48.refs_6_), channel_id=1, source_target_pairs={{0,1},{1,0},{2,3},{3,2},{4,5},{5,4},{6,7},{7,6},{8,9},{9,8},{10,11... | collective-permute-start | bytes 405512 | tf_op jit(solution)/shard_map/ppermute | solution.py:36
  158.8 8.9 %collective-permute-start.53 = (bf16[528,128]{1,0:T(8,128)(2,1)S(1)}, bf16[528,128]{1,0:T(8,128)(2,1)S(1)}, u32[]{:S(2)}, u32[]{:S(2)}) collective-permute-start(bf16[528,128]{1,0:T(8,128)(2,1)S(1)} %collective-permute-done.52.refs_9_), channel_id=1, source_target_pairs={{0,2},{1,3},{2,0},{3,1},{4,6},{5,7},{6,4},{7,5},{8,10},{9,11},{10,... | collective-permute-start | bytes 405512 | tf_op jit(solution)/shard_map/ppermute | solution.py:36
  (10 other events, 41.5 us)

commit v3 on v2

--- a/solution.py
+++ b/solution.py
@@ -11,6 +11,9 @@
 GROUP = 8
 TAIL = 16
 STRIP = 64
+GATHER_BY = {7: 2}
+GATHER_AFTER = {3: (1,), 6: (2,)}
+SUM_AFTER = {3: (7,)}
 
 step_size = 0.3
 low_type = jnp.bfloat16
@@ -45,39 +48,44 @@
     return found
 
 
-def hop(place):
-    return 2 if place == 3 else place & -place
-
-
-def branches(place, devices):
-    return [further for further in range(1, devices) if further ^ hop(further) == place]
+def hop(place, special={}):
+    return special.get(place, place & -place)
 
 
 def depth(place):
-    return 0 if place == 0 else 1 + depth(place ^ hop(place))
-
-
-def leaves(devices):
-    return [place for place in range(1, devices) if not branches(place, devices)]
-
-
-def gathered(block):
+    return place.bit_count()
+
+
+def after(array, others):
+    return lax.optimization_barrier((array, *others))[0] if others else array
+
+
+def gathered(block, meanwhile=()):
     devices = lax.axis_size("op")
     held = {0: block}
     for place in sorted(range(1, devices), key=depth):
-        held[place] = traded(held[place ^ hop(place)], hop(place))
+        source = held[place ^ hop(place, GATHER_BY)]
+        others = [held[other] for other in GATHER_AFTER.get(place, ())]
+        if place == 3:
+            others += list(meanwhile)
+        source = after(source, others)
+        held[place] = traded(source, hop(place, GATHER_BY))
     return [held[place] for place in range(devices)]
 
 
 def summed(pieces):
     devices = len(pieces)
     came = {place: [] for place in range(devices)}
-    for place in sorted(range(1, devices), key=depth, reverse=True):
+    arrived = {}
+    for place in sorted(range(1, devices), key=lambda place: (depth(place), place), reverse=True):
         piece = pieces[place]
+        step = hop(place)
         if came[place]:
-            piece = sum((part.astype(wide_type) for part in came[place]), piece).astype(low_type)
-        came[place ^ hop(place)].append(traded(piece, hop(place)))
-    return [pieces[0], *came[0]]
+            piece = sum((part.astype(wide_type) for part in came[place]), piece.astype(wide_type)).astype(low_type)
+        piece = after(piece, [arrived[other] for other in SUM_AFTER.get(place, ())])
+        arrived[place] = traded(piece, step)
+        came[place ^ step].append(arrived[place])
+    return [pieces[0], *came[0][::-1]], arrived
 
 
 def plan_kernel(blocks_dev, me_ref, shifts_ref, active_ref, left_hbm, right_hbm, plan_ref, left_ref, turned_ref, right_ref, arrived):
@@ -88,38 +96,50 @@
     for copy in copies:
         copy.start()
     terms, blocks_all = active_ref.shape
-    room = plan_ref.shape[1]
+    room = plan_ref.shape[1] // 2
     mine = me_ref[0] * blocks_dev
-    found = 0
+    bits = blocks_dev.bit_length() - 1
+    last = blocks_all // blocks_dev - 1
+    found = (0, 0)
     for term in range(terms):
         shift = shifts_ref[0, term]
 
         def one(block, found, term=term, shift=shift):
             target = block + shift
-            target = jnp.where(target >= blocks_all, target - blocks_all, target)
-            plan_ref[0, found] = term * blocks_all + block
-            plan_ref[1, found] = block ^ mine
-            plan_ref[2, found] = target ^ mine
-            plan_ref[3, found] = term
-            return found + active_ref[term, block]
+            target = jnp.where(target >= blocks_all, target - blocks_all, target) ^ mine
+            ahead = ((target >> bits) == last).astype(jnp.int32)
+            at = jnp.where(ahead == 1, found[0], room + found[1])
+            plan_ref[0, at] = term * blocks_all + block
+            plan_ref[1, at] = block ^ mine
+            plan_ref[2, at] = target - ahead * (last * blocks_dev)
+            plan_ref[3, at] = term
+            plan_ref[4, at] = target
+            is_active = active_ref[term, block]
+            counted = is_active & ahead
+            return found[0] + counted, found[1] + is_active - counted
 
         found = lax.fori_loop(0, blocks_all, one, found, unroll=8)
-    for extra in range(GROUP):
-        plan_ref[0, found + extra] = 0
-        plan_ref[1, found + extra] = 0
-        plan_ref[2, found + extra] = blocks_all
-        plan_ref[3, found + extra] = terms
-    plan_ref[0, room - 1] = found
+    for side in range(2):
+        for extra in range(GROUP):
+            at = side * room + found[side] + extra
+            plan_ref[0, at] = 0
+            plan_ref[1, at] = 0
+            plan_ref[2, at] = (1, last)[side] * blocks_dev
+            plan_ref[3, at] = terms
+            plan_ref[4, at] = blocks_all
+        plan_ref[0, (side + 1) * room - 1] = found[side]
     for copy in copies:
         copy.wait()
 
-    def turn(index, carried):
-        for inner in range(GROUP // 2):
-            pair = plan_ref[0, index * (GROUP // 2) + inner]
-            turned_ref[pair] = right_ref[pair].T
-        return carried
-
-    lax.fori_loop(0, (found + GROUP // 2) // (GROUP // 2), turn, 0)
+    for side in range(2):
+
+        def turn(index, carried, side=side):
+            for inner in range(GROUP // 2):
+                pair = plan_ref[0, side * room + index * (GROUP // 2) + inner]
+                turned_ref[pair] = right_ref[pair].T
+            return carried
+
+        lax.fori_loop(0, (found[side] + GROUP // 2) // (GROUP // 2), turn, 0)
 
 
 def make_plan(me, shifts, active, lefts, rights, blocks_dev):
@@ -129,7 +149,7 @@
     return pl.pallas_call(
         functools.partial(plan_kernel, blocks_dev),
         out_shape=[
-            jax.ShapeDtypeStruct((4, room), jnp.int32),
+            jax.ShapeDtypeStruct((5, 2 * room), jnp.int32),
             kept(lefts.shape, lefts.dtype),
             kept(rights.shape, rights.dtype),
         ],
@@ -186,69 +206,90 @@
         lax.fori_loop(0, rows // STRIP, strip, 0, unroll=True)
 
 
-def apply_kernel(first, devices, olds, count, term_scale, *refs):
-    plan_ref, left_ref, right_ref = refs[:3]
-    chunk_refs = refs[3 : 3 + devices][::-1]
-    own_ref = refs[3 + devices]
-    old_refs = refs[4 + devices : 4 + devices + olds]
-    rest = refs[4 + devices + olds :]
-    piece_refs, rest = rest[:devices], rest[devices:]
-    if first:
-        fresh_ref = None
-    else:
-        fresh_ref, own_low_ref, own_wide_ref = rest[:3]
-        rest = rest[3:]
-    low_ref, sum_ref = rest
-    rows, width = own_ref.shape
+def grouped(side, plan_ref, left_ref, right_ref, low_ref, take):
+    room = plan_ref.shape[1] // 2
+
+    def group(index, carried):
+        first = side * room + index * GROUP
+        products = [pair_product(first + inner, plan_ref, left_ref, right_ref, low_ref) for inner in range(GROUP)]
+        for inner, product in enumerate(products):
+            take(first + inner, product)
+        return carried
+
+    lax.fori_loop(0, (plan_ref[0, (side + 1) * room - 1] + GROUP - 1) // GROUP, group, 0)
+
+
+def add_terms(side, term_scale, plan_ref, left_ref, right_ref, low_ref, piece_refs, sum_ref):
+    rows, width = piece_refs[0].shape
     blocks = rows // width
-    fill_low(first, chunk_refs, own_ref, old_refs, low_ref, fresh_ref, count)
-    if not first:
-        own_low_ref[...] = low_ref[:blocks].reshape(rows, width)
-        own_wide_ref[...] = fresh_ref[:rows, :]
     sum_ref[...] = jnp.zeros_like(sum_ref)
 
-    def group(index, carried):
-        products = [
-            pair_product(index * GROUP + inner, plan_ref, left_ref, right_ref, low_ref)
-            for inner in range(GROUP)
-        ]
-        for inner, product in enumerate(products):
-            sum_ref[plan_ref[2, index * GROUP + inner]] += product
-        return carried
-
-    lax.fori_loop(0, (plan_ref[0, plan_ref.shape[1] - 1] + GROUP - 1) // GROUP, group, 0)
+    def take(place, product):
+        sum_ref[plan_ref[2, place]] += product
+
+    grouped(side, plan_ref, left_ref, right_ref, low_ref, take)
     for place, piece_ref in enumerate(piece_refs):
         piece = sum_ref[place * blocks : (place + 1) * blocks].reshape(rows, width) * term_scale
         piece_ref[...] = piece.astype(piece_ref.dtype)
+
+
+def far_kernel(first, devices, olds, count, term_scale, *refs):
+    plan_ref, left_ref, right_ref = refs[:3]
+    chunk_refs = refs[3 : 3 + devices]
+    own_ref = refs[3 + devices]
+    old_refs = refs[4 + devices : 4 + devices + olds]
+    piece_ref, low_ref, *rest, sum_ref = refs[4 + devices + olds :]
+    rows, width = own_ref.shape
+    fresh_ref = None if first else rest[0]
+    fill_low(first, chunk_refs, own_ref, old_refs, low_ref, fresh_ref, count)
+    if not first:
+        own_low_ref, own_wide_ref = rest[1:]
+        own_low_ref[...] = low_ref[: rows // width].reshape(rows, width)
+        own_wide_ref[...] = fresh_ref[:rows, :]
+    add_terms(0, term_scale, plan_ref, left_ref, right_ref, low_ref, [piece_ref], sum_ref)
+
+
+def near_kernel(term_scale, plan_ref, left_ref, right_ref, low_ref, *refs):
+    *piece_refs, sum_ref = refs
+    add_terms(1, term_scale, plan_ref, left_ref, right_ref, low_ref, piece_refs, sum_ref)
 
 
 def apply_terms(plan, lefts, rights, chunks, own, olds, count, term_scale):
     first = not olds
     devices = len(chunks)
     rows, width = own.shape
+    blocks = rows // width
     total = devices * rows
-    sent = leaves(devices)
-    outs = [kept((rows, width), low_type if place in sent else wide_type) for place in range(devices)]
+    blocks_all = total // width
+    outs = [kept((rows, width), low_type), kept((blocks_all, width, width), low_type)]
     if not first:
         outs += [kept((total, width), wide_type), kept((rows, width), low_type), kept((rows, width), wide_type)]
-    pairs_all = lefts.shape[0]
-    return pl.pallas_call(
-        functools.partial(apply_kernel, first, devices, len(olds), count, term_scale),
+    cost = pl.CostEstimate(flops=lefts.shape[0] * width**3, bytes_accessed=4 << 20, transcendentals=0)
+    sent = pl.pallas_call(
+        functools.partial(far_kernel, first, devices, len(olds), count, term_scale),
         out_shape=outs,
         in_specs=[SMEM] + [VMEM] * (3 + devices + len(olds)),
         out_specs=[VMEM] * len(outs),
-        scratch_shapes=[
-            pltpu.VMEM((total // width, width, width), low_type),
-            pltpu.VMEM((total // width + 1, width, width), wide_type),
-        ],
+        scratch_shapes=[pltpu.VMEM((blocks + 1, width, width), wide_type)],
         compiler_params=params(12),
-        cost_estimate=pl.CostEstimate(flops=2 * pairs_all * width**3, bytes_accessed=4 << 20, transcendentals=0),
-    )(plan, *map(pinned, (lefts, rights, *chunks[::-1], own, *olds)))
+        cost_estimate=cost,
+    )(plan, *map(pinned, (lefts, rights, *chunks, own, *olds)))
+    last, low, *current = sent
+    pieces = pl.pallas_call(
+        functools.partial(near_kernel, term_scale),
+        out_shape=[kept((rows, width), low_type if place % 2 else wide_type) for place in range(devices - 1)],
+        in_specs=[SMEM] + [VMEM] * 3,
+        out_specs=[VMEM] * (devices - 1),
+        scratch_shapes=[pltpu.VMEM((blocks_all - blocks + 1, width, width), wide_type)],
+        compiler_params=params(12),
+        cost_estimate=cost,
+    )(plan, *map(pinned, (lefts, rights, low)))
+    return [*pieces, last], current
 
 
 def values_kernel(devices, olds, count, *refs):
     plan_ref, left_ref, right_ref = refs[:3]
-    chunk_refs = refs[3 : 3 + devices][::-1]
+    chunk_refs = refs[3 : 3 + devices]
     own_ref = refs[3 + devices]
     old_refs = refs[4 + devices : 4 + devices + olds]
     state_ref, value_ref, low_ref, sum_ref = refs[4 + devices + olds :]
@@ -259,19 +300,13 @@
     low_ref[devices * blocks] = jnp.zeros((width, width), low_type)
     sum_ref[...] = jnp.zeros_like(sum_ref)
 
-    def group(index, carried):
-        products = [
-            pair_product(index * GROUP + inner, plan_ref, left_ref, right_ref, low_ref)
-            for inner in range(GROUP)
-        ]
-        for inner, product in enumerate(products):
-            place = index * GROUP + inner
-            target = low_ref[plan_ref[2, place]].astype(wide_type)
-            folded = (product * target).reshape(width // 8, 8, width).sum(axis=0)
-            sum_ref[plan_ref[3, place]] += folded
-        return carried
-
-    lax.fori_loop(0, (plan_ref[0, plan_ref.shape[1] - 1] + GROUP - 1) // GROUP, group, 0)
+    def take(place, product):
+        target = low_ref[plan_ref[4, place]].astype(wide_type)
+        folded = (product * target).reshape(width // 8, 8, width).sum(axis=0)
+        sum_ref[plan_ref[3, place]] += folded
+
+    for side in range(2):
+        grouped(side, plan_ref, left_ref, right_ref, low_ref, take)
     terms = value_ref.shape[0]
     for term in range(terms):
         value_ref[term : term + 1, :] = jnp.full((1, width), jnp.sum(sum_ref[term]) * (1.0 / count))
@@ -293,7 +328,7 @@
         ],
         compiler_params=params(12),
         cost_estimate=pl.CostEstimate(flops=2 * pairs_all * width**3, bytes_accessed=4 << 20, transcendentals=0),
-    )(plan, *map(pinned, (lefts, rights, *chunks[::-1], own, *olds)))
+    )(plan, *map(pinned, (lefts, rights, *chunks, own, *olds)))
 
 
 def coupling_kernel(own_ref, before_ref, after_ref, out_ref):
@@ -336,7 +371,7 @@
         in_specs=[VMEM] * len(parts),
         out_specs=VMEM,
         compiler_params=params(4),
-        cost_estimate=pl.CostEstimate(flops=1 << 32, bytes_accessed=1 << 24, transcendentals=0),
+        cost_estimate=pl.CostEstimate(flops=1 << 37, bytes_accessed=1 << 24, transcendentals=0),
     )(*map(pinned, parts))
 
 
@@ -384,23 +419,22 @@
     own_low = psi_start.reshape(rows, width)
     own_wide = own_low
     me = lax.axis_index("op").astype(jnp.int32).reshape(1)
-    chunks = gathered(own_low)
     lefts = left_ops.reshape(terms * blocks_all, width, width)
     rights = right_ops.reshape(terms * blocks_all, width, width)
     plan, lefts, rights = make_plan(me, shifts, active[0], lefts, rights, blocks_dev)
+    chunks = gathered(own_low, [plan])
     own_source = own_low
     olds = []
     for sweep_index in range(ITERS):
-        outs = apply_terms(plan, lefts, rights, chunks, own_source, olds, count, term_scale)
-        pieces = outs[:devices]
+        pieces, current = apply_terms(plan, lefts, rights, chunks, own_source, olds, count, term_scale)
         if olds:
-            fresh, own_low, own_wide = outs[devices:]
+            fresh, own_low, own_wide = current
             olds = [fresh]
         else:
             olds = chunks
-        parts = summed(pieces)
-        own_low, _ = lax.optimization_barrier((own_low, parts[1]))
-        coupled = coupling(own_wide, *neighbours(own_low))
+        parts, arrived = summed(pieces)
+        around = neighbours(after(own_low, [arrived[6]]))
+        coupled = coupling(own_wide, *around)
         own_source, sent = total_applied(own_wide, coupled, added(parts))
         chunks = gathered(sent)
     state, values = term_values(plan, lefts, rights, chunks, own_source, olds, count, terms)

time: 175 us -> 164 us (0.937)
  waiting for transfers between devices: 88.8 us -> 67 us
  Pallas kernels: 26.8 us -> 33.2 us
  starting transfers between devices: 54.6 us -> 60.4 us
    ppermute x49, waiting for transfers between devices: 88.7 us -> 67 us  [traded(): return lax.ppermute(block, 'op', route)]
    ppermute x49, starting transfers between devices: 45.6 us -> 52.5 us  [traded(): return lax.ppermute(block, 'op', route)]
    pallas_call x3 -> x6, Pallas kernels: 12.8 us -> 17.8 us  [the longest x3 12.3 us: apply_terms(): pl.pallas_call(functools.partial(near_kernel, term_scale), out_shape=[kep...]
  transfers between devices with their start and end apart: 55 -> 55, of which waited for: 30 -> 31; matrix products, arithmetic and copies ran while one was open for 0% -> 0% of each run, Pallas kernels for 5% -> 13%
where the time goes in v3:
time: 164 us
  waiting for transfers between devices  67 us (41%)
  starting transfers between devices  60.4 us (37%)
  Pallas kernels  33.2 us (20%)
  local copies, waits for them, and re-layouts  1.96 us (1%)
    ppermute x49, waiting for transfers between devices, traded(): return lax.ppermute(block, 'op', route)  67 us
    ppermute x49, starting transfers between devices, traded(): return lax.ppermute(block, 'op', route)  52.5 us
    pallas_call x3, Pallas kernels, apply_terms(): pl.pallas_call(functools.partial(near_kernel, term_scale), out_shape=[kep...  12.3 us
    ppermute x6, starting transfers between devices, neighbours(): found.append(lax.ppermute(block, 'seg', pairs + [(j, i) for i, j in pairs]))  7.88 us
    pallas_call x1, Pallas kernels, make_plan(): pl.pallas_call(functools.partial(plan_kernel, blocks_dev), out_shape=[jax...  6.63 us
    pallas_call x1, Pallas kernels, term_values(): pl.pallas_call(functools.partial(values_kernel, devices, len(olds), count...  5.8 us
    pallas_call x3, Pallas kernels, apply_terms(): pl.pallas_call(functools.partial(far_kernel, first, devices, len(olds), c...  5.5 us
  transfers between devices with their start and end apart: 55, of which 31 were waited for; matrix products, arithmetic and copies ran while one was open for 0% of the time, Pallas kernels for 13%

profile of v3, /device:TPU:0, one launch (start us, length us, event | category | flops | bytes accessed | tf_op | source)
XLA Modules:
  0.0 163.9 jit_solution(5067463619039594901)
XLA Ops:
  0.6 4.1 %collective-permute-start.3 = (bf16[512,128]{1,0:T(8,128)(2,1)}, bf16[512,128]{1,0:T(8,128)(2,1)S(1)}, u32[]{:S(2)}, u32[]{:S(2)}) collective-permute-start(bf16[512,128]{1,0:T(8,128)(2,1)} %bitcast.7), channel_id=1, source_target_pairs={{0,4},{1,5},{2,6},{3,7},{4,0},{5,1},{6,2},{7,3},{8,12},{9,13},{10,... | collective-permute-start | bytes 393224 | tf_op jit(solution)/shard_map/ppermute | solution.py:39
  4.7 1.6 collective-permute-start.1
  6.3 1.5 collective-permute-start
  7.8 3.6 %collective-permute-done.3.refs_7_.refs_16_ = bf16[512,128]{1,0:T(8,128)(2,1)S(1)} collective-permute-done((bf16[512,128]{1,0:T(8,128)(2,1)}, bf16[512,128]{1,0:T(8,128)(2,1)S(1)}, u32[]{:S(2)}, u32[]{:S(2)}) %collective-permute-start.3) | collective-permute-done | bytes 131104 | tf_op jit(solution)/shard_map/ppermute | solution.py:39
  11.4 1.5 collective-permute-start.4
  14.2 6.6 %shard_map.68 = (s32[5,274]{1,0:T(8,128)S(1)}, bf16[128,128,128]{2,1,0:T(8,128)(2,1)S(1)}, bf16[128,128,128]{2,1,0:T(8,128)(2,1)S(1)}) custom-call(s32[1]{0:T(128)} %bitcast.me_ref, s32[1,4]{1,0:T(1,128)S(1)} %copy-done.2, s32[4,32]{1,0:T(4,128)S(1)} %bitcast.17, bf16[128,128,128]{2,1,0:T(8,128)(2,1)} %bitcast.18, bf16[128,128,128]{2,1,0:T(8,128)(2,1)} %bitcast.19), custom_call_target="tpu_custom_call" | custom-call | bytes 16777216 | tf_op jit(solution)/shard_map/pallas_call | solution.py:149
  23.0 3.6 %collective-permute-done.5.refs_9_.refs_18_ = bf16[512,128]{1,0:T(8,128)(2,1)S(1)} collective-permute-done((bf16[512,128]{1,0:T(8,128)(2,1)S(1)}, bf16[512,128]{1,0:T(8,128)(2,1)S(1)}, u32[]{:S(2)}, u32[]{:S(2)}) %collective-permute-start.5) | collective-permute-done | bytes 131104 | tf_op jit(solution)/shard_map/ppermute | solution.py:39
  26.7 1.4 collective-permute-done.6.refs_10_.refs_19_
  28.1 1.6 shard_map.69
  30.0 4.1 %shard_map.70 = (f32[512,128]{1,0:T(8,128)S(1)}, bf16[512,128]{1,0:T(8,128)(2,1)S(1)}, f32[512,128]{1,0:T(8,128)S(1)}, bf16[512,128]{1,0:T(8,128)(2,1)S(1)}, f32...) custom-call(s32[5,274]{1,0:T(8,128)S(1)} %get-tuple-element.60.refs_0_.plan_ref, ...), custom_call_target="tpu_custom_call" | custom-call | flops 268435456 | bytes 4194304 | tf_op jit(solution)/shard_map/pallas_call | solution.py:278
  40.4 2.8 %collective-permute-start.9 = (bf16[512,128]{1,0:T(8,128)(2,1)S(1)}, bf16[512,128]{1,0:T(8,128)(2,1)S(1)}, u32[]{:S(2)}, u32[]{:S(2)}) collective-permute-start(bf16[512,128]{1,0:T(8,128)(2,1)S(1)} %bitcast.13), channel_id=1, source_target_pairs={{0,8},{16,24},{8,0},{24,16},{1,9},{17,25},{9,1},{25,17},{2,10},{18... | collective-permute-start | bytes 393224 | tf_op jit(solution)/shard_map/ppermute | solution.py:47
  43.3 1.2 collective-permute-start.13
  45.3 2.9 %collective-permute-start.15 = (bf16[512,128]{1,0:T(8,128)(2,1)S(1)}, bf16[512,128]{1,0:T(8,128)(2,1)S(1)}, u32[]{:S(2)}, u32[]{:S(2)}) collective-permute-start(bf16[512,128]{1,0:T(8,128)(2,1)S(1)} %add_convert_fusion.6), channel_id=1, source_target_pairs={{0,4},{1,5},{2,6},{3,7},{4,0},{5,1},{6,2},{7,3},{8,12},{9,13},{10,... | collective-permute-start | bytes 393224 | tf_op jit(solution)/shard_map/ppermute | solution.py:39
  49.0 5.4 %collective-permute-done.15.refs_3_ = bf16[512,128]{1,0:T(8,128)(2,1)S(1)} collective-permute-done((bf16[512,128]{1,0:T(8,128)(2,1)S(1)}, bf16[512,128]{1,0:T(8,128)(2,1)S(1)}, u32[]{:S(2)}, u32[]{:S(2)}) %collective-permute-start.15) | collective-permute-done | bytes 131104 | tf_op jit(solution)/shard_map/ppermute | solution.py:39
  54.8 3.0 %collective-permute-start.17 = (bf16[528,128]{1,0:T(8,128)(2,1)S(1)}, bf16[528,128]{1,0:T(8,128)(2,1)S(1)}, u32[]{:S(2)}, u32[]{:S(2)}) collective-permute-start(bf16[528,128]{1,0:T(8,128)(2,1)S(1)} %get-tuple-element.76.refs_3_), channel_id=1, source_target_pairs={{0,2},{1,3},{2,0},{3,1},{4,6},{5,7},{6,4},{7,5},{8,10},{9,11},{10,... | collective-permute-start | bytes 405512 | tf_op jit(solution)/shard_map/ppermute | solution.py:39
  58.9 3.2 %collective-permute-done.19.refs_7_ = bf16[528,128]{1,0:T(8,128)(2,1)S(1)} collective-permute-done((bf16[528,128]{1,0:T(8,128)(2,1)S(1)}, bf16[528,128]{1,0:T(8,128)(2,1)S(1)}, u32[]{:S(2)}, u32[]{:S(2)}) %collective-permute-start.19) | collective-permute-done | bytes 135200 | tf_op jit(solution)/shard_map/ppermute | solution.py:39
  62.1 1.3 collective-permute-start.20
  64.4 2.7 %collective-permute-done.20.refs_8_ = bf16[528,128]{1,0:T(8,128)(2,1)S(1)} collective-permute-done((bf16[528,128]{1,0:T(8,128)(2,1)S(1)}, bf16[528,128]{1,0:T(8,128)(2,1)S(1)}, u32[]{:S(2)}, u32[]{:S(2)}) %collective-permute-start.20) | collective-permute-done | bytes 135200 | tf_op jit(solution)/shard_map/ppermute | solution.py:39
  67.1 1.3 collective-permute-done.21.refs_9_
  68.5 3.6 %collective-permute-done.22.refs_10_ = bf16[528,128]{1,0:T(8,128)(2,1)S(1)} collective-permute-done((bf16[528,128]{1,0:T(8,128)(2,1)S(1)}, bf16[528,128]{1,0:T(8,128)(2,1)S(1)}, u32[]{:S(2)}, u32[]{:S(2)}) %collective-permute-start.22) | collective-permute-done | bytes 135200 | tf_op jit(solution)/shard_map/ppermute | solution.py:39
  72.1 2.0 %shard_map.74 = (bf16[512,128]{1,0:T(8,128)(2,1)S(1)}, bf16[32,128,128]{2,1,0:T(8,128)(2,1)S(1)}, f32[4096,128]{1,0:T(8,128)S(1)}, bf16[512,128]{1,0:T(8,128)(2,1)S(1)}, f32[512,128]{1,0:T(8,128)S(1)}) custom-call(s32[5,274]{1,0:T(8,128)S(1)} %get-tuple-element.60.refs_0_.plan_ref, bf16[128,128,128]{2,1,0:T(8,128)(2,1)S(1)} %get-tuple-element.61.refs_1_.left_ref, ...), custom_call_target="tpu_custom_call" | custom-call | flops 268435456 | bytes 4194304 | tf_op jit(solution)/shard_map/pallas_call | solution.py:268
  75.2 4.1 %shard_map.75 = (f32[512,128]{1,0:T(8,128)S(1)}, bf16[512,128]{1,0:T(8,128)(2,1)S(1)}, f32[512,128]{1,0:T(8,128)S(1)}, bf16[512,128]{1,0:T(8,128)(2,1)S(1)}, f32...) custom-call(s32[5,274]{1,0:T(8,128)S(1)} %get-tuple-element.60.refs_0_.plan_ref, ...), custom_call_target="tpu_custom_call" | custom-call | flops 268435456 | bytes 4194304 | tf_op jit(solution)/shard_map/pallas_call | solution.py:278
  79.8 2.0 %collective-permute-start.28 = (bf16[512,128]{1,0:T(8,128)(2,1)S(1)}, bf16[512,128]{1,0:T(8,128)(2,1)S(1)}, u32[]{:S(2)}, u32[]{:S(2)}) collective-permute-start(bf16[512,128]{1,0:T(8,128)(2,1)S(1)} %get-tuple-element.90), channel_id=1, source_target_pairs={{0,1},{1,0},{2,3},{3,2},{4,5},{5,4},{6,7},{7,6},{8,9},{9,8},{10,11... | collective-permute-start | bytes 393224 | tf_op jit(solution)/shard_map/ppermute | solution.py:39
  81.9 1.9 %collective-permute-start.30 = (bf16[512,128]{1,0:T(8,128)(2,1)S(1)}, bf16[512,128]{1,0:T(8,128)(2,1)S(1)}, u32[]{:S(2)}, u32[]{:S(2)}) collective-permute-start(bf16[512,128]{1,0:T(8,128)(2,1)S(1)} %get-tuple-element.92), channel_id=1, source_target_pairs={{0,1},{1,0},{2,3},{3,2},{4,5},{5,4},{6,7},{7,6},{8,9},{9,8},{10,11... | collective-permute-start | bytes 393224 | tf_op jit(solution)/shard_map/ppermute | solution.py:39
  85.4 2.6 %collective-permute-start.25 = (bf16[512,128]{1,0:T(8,128)(2,1)S(1)}, bf16[512,128]{1,0:T(8,128)(2,1)S(1)}, u32[]{:S(2)}, u32[]{:S(2)}) collective-permute-start(bf16[512,128]{1,0:T(8,128)(2,1)S(1)} %get-tuple-element.85), channel_id=1, source_target_pairs={{0,8},{16,24},{8,0},{24,16},{1,9},{17,25},{9,1},{25,17},{2,10},{18... | collective-permute-start | bytes 393224 | tf_op jit(solution)/shard_map/ppermute | solution.py:47
  88.5 2.7 %collective-permute-start.31 = (bf16[512,128]{1,0:T(8,128)(2,1)S(1)}, bf16[512,128]{1,0:T(8,128)(2,1)S(1)}, u32[]{:S(2)}, u32[]{:S(2)}) collective-permute-start(bf16[512,128]{1,0:T(8,128)(2,1)S(1)} %add_convert_fusion.3), channel_id=1, source_target_pairs={{0,4},{1,5},{2,6},{3,7},{4,0},{5,1},{6,2},{7,3},{8,12},{9,13},{10,... | collective-permute-start | bytes 393224 | tf_op jit(solution)/shard_map/ppermute | solution.py:39
  92.0 3.7 %collective-permute-done.29.refs_2_ = bf16[512,128]{1,0:T(8,128)(2,1)S(1)} collective-permute-done((bf16[512,128]{1,0:T(8,128)(2,1)S(1)}, bf16[512,128]{1,0:T(8,128)(2,1)S(1)}, u32[]{:S(2)}, u32[]{:S(2)}) %collective-permute-start.29) | collective-permute-done | bytes 131104 | tf_op jit(solution)/shard_map/ppermute | solution.py:39
  95.7 1.8 %collective-permute-done.31.refs_3_ = bf16[512,128]{1,0:T(8,128)(2,1)S(1)} collective-permute-done((bf16[512,128]{1,0:T(8,128)(2,1)S(1)}, bf16[512,128]{1,0:T(8,128)(2,1)S(1)}, u32[]{:S(2)}, u32[]{:S(2)}) %collective-permute-start.31) | collective-permute-done | bytes 131104 | tf_op jit(solution)/shard_map/ppermute | solution.py:39
  98.0 2.4 %collective-permute-start.33 = (bf16[528,128]{1,0:T(8,128)(2,1)S(1)}, bf16[528,128]{1,0:T(8,128)(2,1)S(1)}, u32[]{:S(2)}, u32[]{:S(2)}) collective-permute-start(bf16[528,128]{1,0:T(8,128)(2,1)S(1)} %get-tuple-element.93.refs_3_), channel_id=1, source_target_pairs={{0,2},{1,3},{2,0},{3,1},{4,6},{5,7},{6,4},{7,5},{8,10},{9,11},{10,... | collective-permute-start | bytes 405512 | tf_op jit(solution)/shard_map/ppermute | solution.py:39
  101.4 3.5 %collective-permute-done.35.refs_7_ = bf16[528,128]{1,0:T(8,128)(2,1)S(1)} collective-permute-done((bf16[528,128]{1,0:T(8,128)(2,1)S(1)}, bf16[528,128]{1,0:T(8,128)(2,1)S(1)}, u32[]{:S(2)}, u32[]{:S(2)}) %collective-permute-start.35) | collective-permute-done | bytes 135200 | tf_op jit(solution)/shard_map/ppermute | solution.py:39
  104.9 1.8 %collective-permute-start.36 = (bf16[528,128]{1,0:T(8,128)(2,1)S(1)}, bf16[528,128]{1,0:T(8,128)(2,1)S(1)}, u32[]{:S(2)}, u32[]{:S(2)}) collective-permute-start(bf16[528,128]{1,0:T(8,128)(2,1)S(1)} %collective-permute-done.35.refs_7_), channel_id=1, source_target_pairs={{0,1},{1,0},{2,3},{3,2},{4,5},{5,4},{6,7},{7,6},{8,9},{9,8},{10,11... | collective-permute-start | bytes 405512 | tf_op jit(solution)/shard_map/ppermute | solution.py:39
  107.0 4.3 %collective-permute-done.36.refs_8_ = bf16[528,128]{1,0:T(8,128)(2,1)S(1)} collective-permute-done((bf16[528,128]{1,0:T(8,128)(2,1)S(1)}, bf16[528,128]{1,0:T(8,128)(2,1)S(1)}, u32[]{:S(2)}, u32[]{:S(2)}) %collective-permute-start.36) | collective-permute-done | bytes 135200 | tf_op jit(solution)/shard_map/ppermute | solution.py:39
  111.3 1.4 collective-permute-done.37.refs_9_
  112.7 3.6 %collective-permute-done.38.refs_10_ = bf16[528,128]{1,0:T(8,128)(2,1)S(1)} collective-permute-done((bf16[528,128]{1,0:T(8,128)(2,1)S(1)}, bf16[528,128]{1,0:T(8,128)(2,1)S(1)}, u32[]{:S(2)}, u32[]{:S(2)}) %collective-permute-start.38) | collective-permute-done | bytes 135200 | tf_op jit(solution)/shard_map/ppermute | solution.py:39
  116.3 1.9 %shard_map.79 = (bf16[512,128]{1,0:T(8,128)(2,1)S(1)}, bf16[32,128,128]{2,1,0:T(8,128)(2,1)S(1)}, f32[4096,128]{1,0:T(8,128)S(1)}, bf16[512,128]{1,0:T(8,128)(2,1)S(1)}, f32[512,128]{1,0:T(8,128)S(1)}) custom-call(s32[5,274]{1,0:T(8,128)S(1)} %get-tuple-element.60.refs_0_.plan_ref, bf16[128,128,128]{2,1,0:T(8,128)(2,1)S(1)} %get-tuple-element.61.refs_1_.left_ref, ...), custom_call_target="tpu_custom_call" | custom-call | flops 268435456 | bytes 4194304 | tf_op jit(solution)/shard_map/pallas_call | solution.py:268
  118.2 1.3 collective-permute-start.39
  119.6 4.1 %shard_map.80 = (f32[512,128]{1,0:T(8,128)S(1)}, bf16[512,128]{1,0:T(8,128)(2,1)S(1)}, f32[512,128]{1,0:T(8,128)S(1)}, bf16[512,128]{1,0:T(8,128)(2,1)S(1)}, f32...) custom-call(s32[5,274]{1,0:T(8,128)S(1)} %get-tuple-element.60.refs_0_.plan_ref, ...), custom_call_target="tpu_custom_call" | custom-call | flops 268435456 | bytes 4194304 | tf_op jit(solution)/shard_map/pallas_call | solution.py:278
  124.1 1.7 %collective-permute-start.44 = (bf16[512,128]{1,0:T(8,128)(2,1)S(1)}, bf16[512,128]{1,0:T(8,128)(2,1)S(1)}, u32[]{:S(2)}, u32[]{:S(2)}) collective-permute-start(bf16[512,128]{1,0:T(8,128)(2,1)S(1)} %get-tuple-element.108), channel_id=1, source_target_pairs={{0,1},{1,0},{2,3},{3,2},{4,5},{5,4},{6,7},{7,6},{8,9},{9,8},{10,11... | collective-permute-start | bytes 393224 | tf_op jit(solution)/shard_map/ppermute | solution.py:39
  126.2 1.7 %collective-permute-start.46 = (bf16[512,128]{1,0:T(8,128)(2,1)S(1)}, bf16[512,128]{1,0:T(8,128)(2,1)S(1)}, u32[]{:S(2)}, u32[]{:S(2)}) collective-permute-start(bf16[512,128]{1,0:T(8,128)(2,1)S(1)} %get-tuple-element.110), channel_id=1, source_target_pairs={{0,1},{1,0},{2,3},{3,2},{4,5},{5,4},{6,7},{7,6},{8,9},{9,8},{10,11... | collective-permute-start | bytes 393224 | tf_op jit(solution)/shard_map/ppermute | solution.py:39
  133.2 3.7 %collective-permute-done.45.refs_2_ = bf16[512,128]{1,0:T(8,128)(2,1)S(1)} collective-permute-done((bf16[512,128]{1,0:T(8,128)(2,1)S(1)}, bf16[512,128]{1,0:T(8,128)(2,1)S(1)}, u32[]{:S(2)}, u32[]{:S(2)}) %collective-permute-start.45) | collective-permute-done | bytes 131104 | tf_op jit(solution)/shard_map/ppermute | solution.py:39
  136.9 3.2 %collective-permute-done.47.refs_3_ = bf16[512,128]{1,0:T(8,128)(2,1)S(1)} collective-permute-done((bf16[512,128]{1,0:T(8,128)(2,1)S(1)}, bf16[512,128]{1,0:T(8,128)(2,1)S(1)}, u32[]{:S(2)}, u32[]{:S(2)}) %collective-permute-start.47) | collective-permute-done | bytes 131104 | tf_op jit(solution)/shard_map/ppermute | solution.py:39
  140.7 2.5 %collective-permute-start.49 = (bf16[528,128]{1,0:T(8,128)(2,1)S(1)}, bf16[528,128]{1,0:T(8,128)(2,1)S(1)}, u32[]{:S(2)}, u32[]{:S(2)}) collective-permute-start(bf16[528,128]{1,0:T(8,128)(2,1)S(1)} %get-tuple-element.111.refs_3_), channel_id=1, source_target_pairs={{0,2},{1,3},{2,0},{3,1},{4,6},{5,7},{6,4},{7,5},{8,10},{9,11},{10,... | collective-permute-start | bytes 405512 | tf_op jit(solution)/shard_map/ppermute | solution.py:39
  144.0 3.4 %collective-permute-done.51.refs_7_ = bf16[528,128]{1,0:T(8,128)(2,1)S(1)} collective-permute-done((bf16[528,128]{1,0:T(8,128)(2,1)S(1)}, bf16[528,128]{1,0:T(8,128)(2,1)S(1)}, u32[]{:S(2)}, u32[]{:S(2)}) %collective-permute-start.51) | collective-permute-done | bytes 135200 | tf_op jit(solution)/shard_map/ppermute | solution.py:39
  147.5 1.4 collective-permute-start.52
  150.5 2.0 %collective-permute-done.52.refs_8_ = bf16[528,128]{1,0:T(8,128)(2,1)S(1)} collective-permute-done((bf16[528,128]{1,0:T(8,128)(2,1)S(1)}, bf16[528,128]{1,0:T(8,128)(2,1)S(1)}, u32[]{:S(2)}, u32[]{:S(2)}) %collective-permute-start.52) | collective-permute-done | bytes 135200 | tf_op jit(solution)/shard_map/ppermute | solution.py:39
  152.5 1.4 collective-permute-done.53.refs_9_
  154.3 3.2 %collective-permute-done.54.refs_10_ = bf16[528,128]{1,0:T(8,128)(2,1)S(1)} collective-permute-done((bf16[528,128]{1,0:T(8,128)(2,1)S(1)}, bf16[528,128]{1,0:T(8,128)(2,1)S(1)}, u32[]{:S(2)}, u32[]{:S(2)}) %collective-permute-start.54) | collective-permute-done | bytes 135200 | tf_op jit(solution)/shard_map/ppermute | solution.py:39
  157.5 5.8 %shard_map.84 = (bf16[512,128]{1,0:T(8,128)(2,1)}, f32[4,128]{1,0:T(4,128)S(1)}) custom-call(s32[5,274]{1,0:T(8,128)S(1)} %get-tuple-element.60.refs_0_.plan_ref, bf16[128,128,128]{2,1,0:T(8,128)(2,1)S(1)} %get-tuple-element.61.refs_1_.left_ref, bf16[128,128,128]{2,1,0:T(8,128)(2,1)S(1)} %get-tuple-element.62.refs_2_.right_ref, ...), custom_call_target="tpu_custom_call" | custom-call | flops 536870912 | bytes 4194304 | tf_op jit(solution)/shard_map/pallas_call | solution.py:320
  (95 shorter events, 31.0 us)
Async XLA Ops:
  0.6 10.7 %collective-permute-start.3 = (bf16[512,128]{1,0:T(8,128)(2,1)}, bf16[512,128]{1,0:T(8,128)(2,1)S(1)}, u32[]{:S(2)}, u32[]{:S(2)}) collective-permute-start(bf16[512,128]{1,0:T(8,128)(2,1)} %bitcast.7), channel_id=1, source_target_pairs={{0,4},{1,5},{2,6},{3,7},{4,0},{5,1},{6,2},{7,3},{8,12},{9,13},{10,... | collective-permute-start | bytes 393224 | tf_op jit(solution)/shard_map/ppermute | solution.py:39
  4.7 16.1 %collective-permute-start.1 = (bf16[512,128]{1,0:T(8,128)(2,1)}, bf16[512,128]{1,0:T(8,128)(2,1)S(1)}, u32[]{:S(2)}, u32[]{:S(2)}) collective-permute-start(bf16[512,128]{1,0:T(8,128)(2,1)} %bitcast.8), channel_id=1, source_target_pairs={{0,2},{1,3},{2,0},{3,1},{4,6},{5,7},{6,4},{7,5},{8,10},{9,11},{10,... | collective-permute-start | bytes 393224 | tf_op jit(solution)/shard_map/ppermute | solution.py:39
  6.3 15.0 %collective-permute-start = (bf16[512,128]{1,0:T(8,128)(2,1)}, bf16[512,128]{1,0:T(8,128)(2,1)S(1)}, u32[]{:S(2)}, u32[]{:S(2)}) collective-permute-start(bf16[512,128]{1,0:T(8,128)(2,1)} %bitcast.9), channel_id=1, source_target_pairs={{0,1},{1,0},{2,3},{3,2},{4,5},{5,4},{6,7},{7,6},{8,9},{9,8},{10,11... | collective-permute-start | bytes 393224 | tf_op jit(solution)/shard_map/ppermute | solution.py:39
  11.4 10.7 %collective-permute-start.4 = (bf16[512,128]{1,0:T(8,128)(2,1)S(1)}, bf16[512,128]{1,0:T(8,128)(2,1)S(1)}, u32[]{:S(2)}, u32[]{:S(2)}) collective-permute-start(bf16[512,128]{1,0:T(8,128)(2,1)S(1)} %collective-permute-done.3.refs_7_.refs_16_), channel_id=1, source_target_pairs={{0,1},{1,0},{2,3},{3,2},{4,5},{5,4},{6,7},{7,6},{8,9},{9,8},{10,11... | collective-permute-start | bytes 393224 | tf_op jit(solution)/shard_map/ppermute | solution.py:39
  20.9 5.8 %collective-permute-start.5 = (bf16[512,128]{1,0:T(8,128)(2,1)S(1)}, bf16[512,128]{1,0:T(8,128)(2,1)S(1)}, u32[]{:S(2)}, u32[]{:S(2)}) collective-permute-start(bf16[512,128]{1,0:T(8,128)(2,1)S(1)} %collective-permute-done.3.refs_7_.refs_16_), channel_id=1, source_target_pairs={{0,2},{1,3},{2,0},{3,1},{4,6},{5,7},{6,4},{7,5},{8,10},{9,11},{10,... | collective-permute-start | bytes 393224 | tf_op jit(solution)/shard_map/ppermute | solution.py:39
  21.3 5.3 %collective-permute-start.2 = (bf16[512,128]{1,0:T(8,128)(2,1)S(1)}, bf16[512,128]{1,0:T(8,128)(2,1)S(1)}, u32[]{:S(2)}, u32[]{:S(2)}) collective-permute-start(bf16[512,128]{1,0:T(8,128)(2,1)S(1)} %collective-permute-done.1.refs_5_.refs_14_), channel_id=1, source_target_pairs={{0,1},{1,0},{2,3},{3,2},{4,5},{5,4},{6,7},{7,6},{8,9},{9,8},{10,11... | collective-permute-start | bytes 393224 | tf_op jit(solution)/shard_map/ppermute | solution.py:39
  22.1 6.0 %collective-permute-start.6 = (bf16[512,128]{1,0:T(8,128)(2,1)S(1)}, bf16[512,128]{1,0:T(8,128)(2,1)S(1)}, u32[]{:S(2)}, u32[]{:S(2)}) collective-permute-start(bf16[512,128]{1,0:T(8,128)(2,1)S(1)} %collective-permute-done.4.refs_8_.refs_17_), channel_id=1, source_target_pairs={{0,2},{1,3},{2,0},{3,1},{4,6},{5,7},{6,4},{7,5},{8,10},{9,11},{10,... | collective-permute-start | bytes 393224 | tf_op jit(solution)/shard_map/ppermute | solution.py:39
  29.7 5.0 %collective-permute-start.7 = (bf16[512,128]{1,0:T(8,128)(2,1)S(1)}, bf16[512,128]{1,0:T(8,128)(2,1)S(1)}, u32[]{:S(2)}, u32[]{:S(2)}) collective-permute-start(bf16[512,128]{1,0:T(8,128)(2,1)S(1)} %get-tuple-element.67), channel_id=1, source_target_pairs={{0,1},{1,0},{2,3},{3,2},{4,5},{5,4},{6,7},{7,6},{8,9},{9,8},{10,11... | collective-permute-start | bytes 393224 | tf_op jit(solution)/shard_map/ppermute | solution.py:39
  34.7 5.0 %collective-permute-start.8 = (bf16[512,128]{1,0:T(8,128)(2,1)S(1)}, bf16[512,128]{1,0:T(8,128)(2,1)S(1)}, u32[]{:S(2)}, u32[]{:S(2)}) collective-permute-start(bf16[512,128]{1,0:T(8,128)(2,1)S(1)} %add_convert_fusion.8), channel_id=1, source_target_pairs={{0,2},{1,3},{2,0},{3,1},{4,6},{5,7},{6,4},{7,5},{8,10},{9,11},{10,... | collective-permute-start | bytes 393224 | tf_op jit(solution)/shard_map/ppermute | solution.py:39
  35.8 7.4 %collective-permute-start.12 = (bf16[512,128]{1,0:T(8,128)(2,1)S(1)}, bf16[512,128]{1,0:T(8,128)(2,1)S(1)}, u32[]{:S(2)}, u32[]{:S(2)}) collective-permute-start(bf16[512,128]{1,0:T(8,128)(2,1)S(1)} %get-tuple-element.73), channel_id=1, source_target_pairs={{0,1},{1,0},{2,3},{3,2},{4,5},{5,4},{6,7},{7,6},{8,9},{9,8},{10,11... | collective-permute-start | bytes 393224 | tf_op jit(solution)/shard_map/ppermute | solution.py:39
  36.8 12.2 %collective-permute-start.11 = (bf16[512,128]{1,0:T(8,128)(2,1)S(1)}, bf16[512,128]{1,0:T(8,128)(2,1)S(1)}, u32[]{:S(2)}, u32[]{:S(2)}) collective-permute-start(bf16[512,128]{1,0:T(8,128)(2,1)S(1)} %get-tuple-element.70), channel_id=1, source_target_pairs={{0,1},{1,0},{2,3},{3,2},{4,5},{5,4},{6,7},{7,6},{8,9},{9,8},{10,11... | collective-permute-start | bytes 393224 | tf_op jit(solution)/shard_map/ppermute | solution.py:39
  37.9 7.4 %collective-permute-start.14 = (bf16[512,128]{1,0:T(8,128)(2,1)S(1)}, bf16[512,128]{1,0:T(8,128)(2,1)S(1)}, u32[]{:S(2)}, u32[]{:S(2)}) collective-permute-start(bf16[512,128]{1,0:T(8,128)(2,1)S(1)} %get-tuple-element.75), channel_id=1, source_target_pairs={{0,1},{1,0},{2,3},{3,2},{4,5},{5,4},{6,7},{7,6},{8,9},{9,8},{10,11... | collective-permute-start | bytes 393224 | tf_op jit(solution)/shard_map/ppermute | solution.py:39
  39.8 8.4 %collective-permute-start.10 = (bf16[512,128]{1,0:T(8,128)(2,1)S(1)}, bf16[512,128]{1,0:T(8,128)(2,1)S(1)}, u32[]{:S(2)}, u32[]{:S(2)}) collective-permute-start(bf16[512,128]{1,0:T(8,128)(2,1)S(1)} %bitcast.12), channel_id=1, source_target_pairs={{8,16},{16,8},{9,17},{17,9},{10,18},{18,10},{11,19},{19,11},{12,20... | collective-permute-start | bytes 393224 | tf_op jit(solution)/shard_map/ppermute | solution.py:47
  40.4 7.8 %collective-permute-start.9 = (bf16[512,128]{1,0:T(8,128)(2,1)S(1)}, bf16[512,128]{1,0:T(8,128)(2,1)S(1)}, u32[]{:S(2)}, u32[]{:S(2)}) collective-permute-start(bf16[512,128]{1,0:T(8,128)(2,1)S(1)} %bitcast.13), channel_id=1, source_target_pairs={{0,8},{16,24},{8,0},{24,16},{1,9},{17,25},{9,1},{25,17},{2,10},{18... | collective-permute-start | bytes 393224 | tf_op jit(solution)/shard_map/ppermute | solution.py:47
  43.3 5.7 %collective-permute-start.13 = (bf16[512,128]{1,0:T(8,128)(2,1)S(1)}, bf16[512,128]{1,0:T(8,128)(2,1)S(1)}, u32[]{:S(2)}, u32[]{:S(2)}) collective-permute-start(bf16[512,128]{1,0:T(8,128)(2,1)S(1)} %add_convert_fusion.7), channel_id=1, source_target_pairs={{0,2},{1,3},{2,0},{3,1},{4,6},{5,7},{6,4},{7,5},{8,10},{9,11},{10,... | collective-permute-start | bytes 393224 | tf_op jit(solution)/shard_map/ppermute | solution.py:39
  45.3 9.1 %collective-permute-start.15 = (bf16[512,128]{1,0:T(8,128)(2,1)S(1)}, bf16[512,128]{1,0:T(8,128)(2,1)S(1)}, u32[]{:S(2)}, u32[]{:S(2)}) collective-permute-start(bf16[512,128]{1,0:T(8,128)(2,1)S(1)} %add_convert_fusion.6), channel_id=1, source_target_pairs={{0,4},{1,5},{2,6},{3,7},{4,0},{5,1},{6,2},{7,3},{8,12},{9,13},{10,... | collective-permute-start | bytes 393224 | tf_op jit(solution)/shard_map/ppermute | solution.py:39
  54.7 7.4 %collective-permute-start.19 = (bf16[528,128]{1,0:T(8,128)(2,1)S(1)}, bf16[528,128]{1,0:T(8,128)(2,1)S(1)}, u32[]{:S(2)}, u32[]{:S(2)}) collective-permute-start(bf16[528,128]{1,0:T(8,128)(2,1)S(1)} %get-tuple-element.76.refs_3_), channel_id=1, source_target_pairs={{0,4},{1,5},{2,6},{3,7},{4,0},{5,1},{6,2},{7,3},{8,12},{9,13},{10,... | collective-permute-start | bytes 405512 | tf_op jit(solution)/shard_map/ppermute | solution.py:39
  54.8 8.6 %collective-permute-start.17 = (bf16[528,128]{1,0:T(8,128)(2,1)S(1)}, bf16[528,128]{1,0:T(8,128)(2,1)S(1)}, u32[]{:S(2)}, u32[]{:S(2)}) collective-permute-start(bf16[528,128]{1,0:T(8,128)(2,1)S(1)} %get-tuple-element.76.refs_3_), channel_id=1, source_target_pairs={{0,2},{1,3},{2,0},{3,1},{4,6},{5,7},{6,4},{7,5},{8,10},{9,11},{10,... | collective-permute-start | bytes 405512 | tf_op jit(solution)/shard_map/ppermute | solution.py:39
  57.8 5.6 %collective-permute-start.16 = (bf16[528,128]{1,0:T(8,128)(2,1)S(1)}, bf16[528,128]{1,0:T(8,128)(2,1)S(1)}, u32[]{:S(2)}, u32[]{:S(2)}) collective-permute-start(bf16[528,128]{1,0:T(8,128)(2,1)S(1)} %get-tuple-element.76.refs_3_), channel_id=1, source_target_pairs={{0,1},{1,0},{2,3},{3,2},{4,5},{5,4},{6,7},{7,6},{8,9},{9,8},{10,11... | collective-permute-start | bytes 405512 | tf_op jit(solution)/shard_map/ppermute | solution.py:39
  62.1 5.0 %collective-permute-start.20 = (bf16[528,128]{1,0:T(8,128)(2,1)S(1)}, bf16[528,128]{1,0:T(8,128)(2,1)S(1)}, u32[]{:S(2)}, u32[]{:S(2)}) collective-permute-start(bf16[528,128]{1,0:T(8,128)(2,1)S(1)} %collective-permute-done.19.refs_7_), channel_id=1, source_target_pairs={{0,1},{1,0},{2,3},{3,2},{4,5},{5,4},{6,7},{7,6},{8,9},{9,8},{10,11... | collective-permute-start | bytes 405512 | tf_op jit(solution)/shard_map/ppermute | solution.py:39
  63.4 5.0 %collective-permute-start.21 = (bf16[528,128]{1,0:T(8,128)(2,1)S(1)}, bf16[528,128]{1,0:T(8,128)(2,1)S(1)}, u32[]{:S(2)}, u32[]{:S(2)}) collective-permute-start(bf16[528,128]{1,0:T(8,128)(2,1)S(1)} %collective-permute-done.19.refs_7_), channel_id=1, source_target_pairs={{0,2},{1,3},{2,0},{3,1},{4,6},{5,7},{6,4},{7,5},{8,10},{9,11},{10,... | collective-permute-start | bytes 405512 | tf_op jit(solution)/shard_map/ppermute | solution.py:39
  63.4 5.1 %collective-permute-start.18 = (bf16[528,128]{1,0:T(8,128)(2,1)S(1)}, bf16[528,128]{1,0:T(8,128)(2,1)S(1)}, u32[]{:S(2)}, u32[]{:S(2)}) collective-permute-start(bf16[528,128]{1,0:T(8,128)(2,1)S(1)} %collective-permute-done.17.refs_5_), channel_id=1, source_target_pairs={{0,1},{1,0},{2,3},{3,2},{4,5},{5,4},{6,7},{7,6},{8,9},{9,8},{10,11... | collective-permute-start | bytes 405512 | tf_op jit(solution)/shard_map/ppermute | solution.py:39
  74.1 5.6 %collective-permute-start.23 = (bf16[512,128]{1,0:T(8,128)(2,1)S(1)}, bf16[512,128]{1,0:T(8,128)(2,1)S(1)}, u32[]{:S(2)}, u32[]{:S(2)}) collective-permute-start(bf16[512,128]{1,0:T(8,128)(2,1)S(1)} %get-tuple-element.84), channel_id=1, source_target_pairs={{0,1},{1,0},{2,3},{3,2},{4,5},{5,4},{6,7},{7,6},{8,9},{9,8},{10,11... | collective-permute-start | bytes 393224 | tf_op jit(solution)/shard_map/ppermute | solution.py:39
  79.7 5.0 %collective-permute-start.24 = (bf16[512,128]{1,0:T(8,128)(2,1)S(1)}, bf16[512,128]{1,0:T(8,128)(2,1)S(1)}, u32[]{:S(2)}, u32[]{:S(2)}) collective-permute-start(bf16[512,128]{1,0:T(8,128)(2,1)S(1)} %add_convert_fusion.5), channel_id=1, source_target_pairs={{0,2},{1,3},{2,0},{3,1},{4,6},{5,7},{6,4},{7,5},{8,10},{9,11},{10,... | collective-permute-start | bytes 393224 | tf_op jit(solution)/shard_map/ppermute | solution.py:39
  79.8 8.2 %collective-permute-start.28 = (bf16[512,128]{1,0:T(8,128)(2,1)S(1)}, bf16[512,128]{1,0:T(8,128)(2,1)S(1)}, u32[]{:S(2)}, u32[]{:S(2)}) collective-permute-start(bf16[512,128]{1,0:T(8,128)(2,1)S(1)} %get-tuple-element.90), channel_id=1, source_target_pairs={{0,1},{1,0},{2,3},{3,2},{4,5},{5,4},{6,7},{7,6},{8,9},{9,8},{10,11... | collective-permute-start | bytes 393224 | tf_op jit(solution)/shard_map/ppermute | solution.py:39
  81.8 10.2 %collective-permute-start.27 = (bf16[512,128]{1,0:T(8,128)(2,1)S(1)}, bf16[512,128]{1,0:T(8,128)(2,1)S(1)}, u32[]{:S(2)}, u32[]{:S(2)}) collective-permute-start(bf16[512,128]{1,0:T(8,128)(2,1)S(1)} %get-tuple-element.87), channel_id=1, source_target_pairs={{0,1},{1,0},{2,3},{3,2},{4,5},{5,4},{6,7},{7,6},{8,9},{9,8},{10,11... | collective-permute-start | bytes 393224 | tf_op jit(solution)/shard_map/ppermute | solution.py:39
  81.9 6.6 %collective-permute-start.30 = (bf16[512,128]{1,0:T(8,128)(2,1)S(1)}, bf16[512,128]{1,0:T(8,128)(2,1)S(1)}, u32[]{:S(2)}, u32[]{:S(2)}) collective-permute-start(bf16[512,128]{1,0:T(8,128)(2,1)S(1)} %get-tuple-element.92), channel_id=1, source_target_pairs={{0,1},{1,0},{2,3},{3,2},{4,5},{5,4},{6,7},{7,6},{8,9},{9,8},{10,11... | collective-permute-start | bytes 393224 | tf_op jit(solution)/shard_map/ppermute | solution.py:39
  84.7 6.5 %collective-permute-start.26 = (bf16[512,128]{1,0:T(8,128)(2,1)S(1)}, bf16[512,128]{1,0:T(8,128)(2,1)S(1)}, u32[]{:S(2)}, u32[]{:S(2)}) collective-permute-start(bf16[512,128]{1,0:T(8,128)(2,1)S(1)} %get-tuple-element.85), channel_id=1, source_target_pairs={{8,16},{16,8},{9,17},{17,9},{10,18},{18,10},{11,19},{19,11},{12,20... | collective-permute-start | bytes 393224 | tf_op jit(solution)/shard_map/ppermute | solution.py:47
  85.4 5.8 %collective-permute-start.25 = (bf16[512,128]{1,0:T(8,128)(2,1)S(1)}, bf16[512,128]{1,0:T(8,128)(2,1)S(1)}, u32[]{:S(2)}, u32[]{:S(2)}) collective-permute-start(bf16[512,128]{1,0:T(8,128)(2,1)S(1)} %get-tuple-element.85), channel_id=1, source_target_pairs={{0,8},{16,24},{8,0},{24,16},{1,9},{17,25},{9,1},{25,17},{2,10},{18... | collective-permute-start | bytes 393224 | tf_op jit(solution)/shard_map/ppermute | solution.py:47
  88.0 7.6 %collective-permute-start.29 = (bf16[512,128]{1,0:T(8,128)(2,1)S(1)}, bf16[512,128]{1,0:T(8,128)(2,1)S(1)}, u32[]{:S(2)}, u32[]{:S(2)}) collective-permute-start(bf16[512,128]{1,0:T(8,128)(2,1)S(1)} %add_convert_fusion.4), channel_id=1, source_target_pairs={{0,2},{1,3},{2,0},{3,1},{4,6},{5,7},{6,4},{7,5},{8,10},{9,11},{10,... | collective-permute-start | bytes 393224 | tf_op jit(solution)/shard_map/ppermute | solution.py:39
  88.5 9.0 %collective-permute-start.31 = (bf16[512,128]{1,0:T(8,128)(2,1)S(1)}, bf16[512,128]{1,0:T(8,128)(2,1)S(1)}, u32[]{:S(2)}, u32[]{:S(2)}) collective-permute-start(bf16[512,128]{1,0:T(8,128)(2,1)S(1)} %add_convert_fusion.3), channel_id=1, source_target_pairs={{0,4},{1,5},{2,6},{3,7},{4,0},{5,1},{6,2},{7,3},{8,12},{9,13},{10,... | collective-permute-start | bytes 393224 | tf_op jit(solution)/shard_map/ppermute | solution.py:39
  97.8 7.1 %collective-permute-start.35 = (bf16[528,128]{1,0:T(8,128)(2,1)S(1)}, bf16[528,128]{1,0:T(8,128)(2,1)S(1)}, u32[]{:S(2)}, u32[]{:S(2)}) collective-permute-start(bf16[528,128]{1,0:T(8,128)(2,1)S(1)} %get-tuple-element.93.refs_3_), channel_id=1, source_target_pairs={{0,4},{1,5},{2,6},{3,7},{4,0},{5,1},{6,2},{7,3},{8,12},{9,13},{10,... | collective-permute-start | bytes 405512 | tf_op jit(solution)/shard_map/ppermute | solution.py:39
  98.0 8.6 %collective-permute-start.33 = (bf16[528,128]{1,0:T(8,128)(2,1)S(1)}, bf16[528,128]{1,0:T(8,128)(2,1)S(1)}, u32[]{:S(2)}, u32[]{:S(2)}) collective-permute-start(bf16[528,128]{1,0:T(8,128)(2,1)S(1)} %get-tuple-element.93.refs_3_), channel_id=1, source_target_pairs={{0,2},{1,3},{2,0},{3,1},{4,6},{5,7},{6,4},{7,5},{8,10},{9,11},{10,... | collective-permute-start | bytes 405512 | tf_op jit(solution)/shard_map/ppermute | solution.py:39
  100.4 6.3 %collective-permute-start.32 = (bf16[528,128]{1,0:T(8,128)(2,1)S(1)}, bf16[528,128]{1,0:T(8,128)(2,1)S(1)}, u32[]{:S(2)}, u32[]{:S(2)}) collective-permute-start(bf16[528,128]{1,0:T(8,128)(2,1)S(1)} %get-tuple-element.93.refs_3_), channel_id=1, source_target_pairs={{0,1},{1,0},{2,3},{3,2},{4,5},{5,4},{6,7},{7,6},{8,9},{9,8},{10,11... | collective-permute-start | bytes 405512 | tf_op jit(solution)/shard_map/ppermute | solution.py:39
  104.9 6.4 %collective-permute-start.36 = (bf16[528,128]{1,0:T(8,128)(2,1)S(1)}, bf16[528,128]{1,0:T(8,128)(2,1)S(1)}, u32[]{:S(2)}, u32[]{:S(2)}) collective-permute-start(bf16[528,128]{1,0:T(8,128)(2,1)S(1)} %collective-permute-done.35.refs_7_), channel_id=1, source_target_pairs={{0,1},{1,0},{2,3},{3,2},{4,5},{5,4},{6,7},{7,6},{8,9},{9,8},{10,11... | collective-permute-start | bytes 405512 | tf_op jit(solution)/shard_map/ppermute | solution.py:39
  106.7 6.1 %collective-permute-start.37 = (bf16[528,128]{1,0:T(8,128)(2,1)S(1)}, bf16[528,128]{1,0:T(8,128)(2,1)S(1)}, u32[]{:S(2)}, u32[]{:S(2)}) collective-permute-start(bf16[528,128]{1,0:T(8,128)(2,1)S(1)} %collective-permute-done.35.refs_7_), channel_id=1, source_target_pairs={{0,2},{1,3},{2,0},{3,1},{4,6},{5,7},{6,4},{7,5},{8,10},{9,11},{10,... | collective-permute-start | bytes 405512 | tf_op jit(solution)/shard_map/ppermute | solution.py:39
  106.7 6.1 %collective-permute-start.34 = (bf16[528,128]{1,0:T(8,128)(2,1)S(1)}, bf16[528,128]{1,0:T(8,128)(2,1)S(1)}, u32[]{:S(2)}, u32[]{:S(2)}) collective-permute-start(bf16[528,128]{1,0:T(8,128)(2,1)S(1)} %collective-permute-done.33.refs_5_), channel_id=1, source_target_pairs={{0,1},{1,0},{2,3},{3,2},{4,5},{5,4},{6,7},{7,6},{8,9},{9,8},{10,11... | collective-permute-start | bytes 405512 | tf_op jit(solution)/shard_map/ppermute | solution.py:39
  118.2 5.7 %collective-permute-start.39 = (bf16[512,128]{1,0:T(8,128)(2,1)S(1)}, bf16[512,128]{1,0:T(8,128)(2,1)S(1)}, u32[]{:S(2)}, u32[]{:S(2)}) collective-permute-start(bf16[512,128]{1,0:T(8,128)(2,1)S(1)} %get-tuple-element.102), channel_id=1, source_target_pairs={{0,1},{1,0},{2,3},{3,2},{4,5},{5,4},{6,7},{7,6},{8,9},{9,8},{10,11... | collective-permute-start | bytes 393224 | tf_op jit(solution)/shard_map/ppermute | solution.py:39
  124.0 5.0 %collective-permute-start.40 = (bf16[512,128]{1,0:T(8,128)(2,1)S(1)}, bf16[512,128]{1,0:T(8,128)(2,1)S(1)}, u32[]{:S(2)}, u32[]{:S(2)}) collective-permute-start(bf16[512,128]{1,0:T(8,128)(2,1)S(1)} %add_convert_fusion.2), channel_id=1, source_target_pairs={{0,2},{1,3},{2,0},{3,1},{4,6},{5,7},{6,4},{7,5},{8,10},{9,11},{10,... | collective-permute-start | bytes 393224 | tf_op jit(solution)/shard_map/ppermute | solution.py:39
  124.1 6.1 %collective-permute-start.44 = (bf16[512,128]{1,0:T(8,128)(2,1)S(1)}, bf16[512,128]{1,0:T(8,128)(2,1)S(1)}, u32[]{:S(2)}, u32[]{:S(2)}) collective-permute-start(bf16[512,128]{1,0:T(8,128)(2,1)S(1)} %get-tuple-element.108), channel_id=1, source_target_pairs={{0,1},{1,0},{2,3},{3,2},{4,5},{5,4},{6,7},{7,6},{8,9},{9,8},{10,11... | collective-permute-start | bytes 393224 | tf_op jit(solution)/shard_map/ppermute | solution.py:39
  125.8 7.4 %collective-permute-start.43 = (bf16[512,128]{1,0:T(8,128)(2,1)S(1)}, bf16[512,128]{1,0:T(8,128)(2,1)S(1)}, u32[]{:S(2)}, u32[]{:S(2)}) collective-permute-start(bf16[512,128]{1,0:T(8,128)(2,1)S(1)} %get-tuple-element.105), channel_id=1, source_target_pairs={{0,1},{1,0},{2,3},{3,2},{4,5},{5,4},{6,7},{7,6},{8,9},{9,8},{10,11... | collective-permute-start | bytes 393224 | tf_op jit(solution)/shard_map/ppermute | solution.py:39
  126.2 6.0 %collective-permute-start.46 = (bf16[512,128]{1,0:T(8,128)(2,1)S(1)}, bf16[512,128]{1,0:T(8,128)(2,1)S(1)}, u32[]{:S(2)}, u32[]{:S(2)}) collective-permute-start(bf16[512,128]{1,0:T(8,128)(2,1)S(1)} %get-tuple-element.110), channel_id=1, source_target_pairs={{0,1},{1,0},{2,3},{3,2},{4,5},{5,4},{6,7},{7,6},{8,9},{9,8},{10,11... | collective-permute-start | bytes 393224 | tf_op jit(solution)/shard_map/ppermute | solution.py:39
  130.2 6.6 %collective-permute-start.45 = (bf16[512,128]{1,0:T(8,128)(2,1)S(1)}, bf16[512,128]{1,0:T(8,128)(2,1)S(1)}, u32[]{:S(2)}, u32[]{:S(2)}) collective-permute-start(bf16[512,128]{1,0:T(8,128)(2,1)S(1)} %add_convert_fusion.1), channel_id=1, source_target_pairs={{0,2},{1,3},{2,0},{3,1},{4,6},{5,7},{6,4},{7,5},{8,10},{9,11},{10,... | collective-permute-start | bytes 393224 | tf_op jit(solution)/shard_map/ppermute | solution.py:39
  132.2 7.8 %collective-permute-start.47 = (bf16[512,128]{1,0:T(8,128)(2,1)S(1)}, bf16[512,128]{1,0:T(8,128)(2,1)S(1)}, u32[]{:S(2)}, u32[]{:S(2)}) collective-permute-start(bf16[512,128]{1,0:T(8,128)(2,1)S(1)} %add_convert_fusion), channel_id=1, source_target_pairs={{0,4},{1,5},{2,6},{3,7},{4,0},{5,1},{6,2},{7,3},{8,12},{9,13},{10,... | collective-permute-start | bytes 393224 | tf_op jit(solution)/shard_map/ppermute | solution.py:39
  140.4 7.1 %collective-permute-start.51 = (bf16[528,128]{1,0:T(8,128)(2,1)S(1)}, bf16[528,128]{1,0:T(8,128)(2,1)S(1)}, u32[]{:S(2)}, u32[]{:S(2)}) collective-permute-start(bf16[528,128]{1,0:T(8,128)(2,1)S(1)} %get-tuple-element.111.refs_3_), channel_id=1, source_target_pairs={{0,4},{1,5},{2,6},{3,7},{4,0},{5,1},{6,2},{7,3},{8,12},{9,13},{10,... | collective-permute-start | bytes 405512 | tf_op jit(solution)/shard_map/ppermute | solution.py:39
  140.7 8.2 %collective-permute-start.49 = (bf16[528,128]{1,0:T(8,128)(2,1)S(1)}, bf16[528,128]{1,0:T(8,128)(2,1)S(1)}, u32[]{:S(2)}, u32[]{:S(2)}) collective-permute-start(bf16[528,128]{1,0:T(8,128)(2,1)S(1)} %get-tuple-element.111.refs_3_), channel_id=1, source_target_pairs={{0,2},{1,3},{2,0},{3,1},{4,6},{5,7},{6,4},{7,5},{8,10},{9,11},{10,... | collective-permute-start | bytes 405512 | tf_op jit(solution)/shard_map/ppermute | solution.py:39
  143.1 6.1 %collective-permute-start.48 = (bf16[528,128]{1,0:T(8,128)(2,1)S(1)}, bf16[528,128]{1,0:T(8,128)(2,1)S(1)}, u32[]{:S(2)}, u32[]{:S(2)}) collective-permute-start(bf16[528,128]{1,0:T(8,128)(2,1)S(1)} %get-tuple-element.111.refs_3_), channel_id=1, source_target_pairs={{0,1},{1,0},{2,3},{3,2},{4,5},{5,4},{6,7},{7,6},{8,9},{9,8},{10,11... | collective-permute-start | bytes 405512 | tf_op jit(solution)/shard_map/ppermute | solution.py:39
  148.9 5.0 %collective-permute-start.53 = (bf16[528,128]{1,0:T(8,128)(2,1)S(1)}, bf16[528,128]{1,0:T(8,128)(2,1)S(1)}, u32[]{:S(2)}, u32[]{:S(2)}) collective-permute-start(bf16[528,128]{1,0:T(8,128)(2,1)S(1)} %collective-permute-done.51.refs_7_), channel_id=1, source_target_pairs={{0,2},{1,3},{2,0},{3,1},{4,6},{5,7},{6,4},{7,5},{8,10},{9,11},{10,... | collective-permute-start | bytes 405512 | tf_op jit(solution)/shard_map/ppermute | solution.py:39
  (10 other events, 46.4 us)

commit v4 on v3

--- a/solution.py
+++ b/solution.py
@@ -66,7 +66,7 @@
     for place in sorted(range(1, devices), key=depth):
         source = held[place ^ hop(place, GATHER_BY)]
         others = [held[other] for other in GATHER_AFTER.get(place, ())]
-        if place == 3:
+        if place in (5, 6):
             others += list(meanwhile)
         source = after(source, others)
         held[place] = traded(source, hop(place, GATHER_BY))
@@ -88,7 +88,7 @@
     return [pieces[0], *came[0][::-1]], arrived
 
 
-def plan_kernel(blocks_dev, me_ref, shifts_ref, active_ref, left_hbm, right_hbm, plan_ref, left_ref, turned_ref, right_ref, arrived):
+def plan_kernel(blocks_dev, me_ref, shifts_ref, active_ref, left_hbm, right_hbm, plan_ref, left_ref, right_ref, arrived):
     copies = [
         pltpu.make_async_copy(left_hbm, left_ref, arrived.at[0]),
         pltpu.make_async_copy(right_hbm, right_ref, arrived.at[1]),
@@ -131,6 +131,9 @@
     for copy in copies:
         copy.wait()
 
+
+def turn_kernel(plan_ref, right_ref, turned_ref):
+    room = plan_ref.shape[1] // 2
     for side in range(2):
 
         def turn(index, carried, side=side):
@@ -139,7 +142,18 @@
                 turned_ref[pair] = right_ref[pair].T
             return carried
 
-        lax.fori_loop(0, (found[side] + GROUP // 2) // (GROUP // 2), turn, 0)
+        lax.fori_loop(0, (plan_ref[0, (side + 1) * room - 1] + GROUP // 2) // (GROUP // 2), turn, 0)
+
+
+def turned(plan, rights):
+    return pl.pallas_call(
+        turn_kernel,
+        out_shape=kept(rights.shape, rights.dtype),
+        in_specs=[SMEM, VMEM],
+        out_specs=VMEM,
+        compiler_params=params(4),
+        cost_estimate=pl.CostEstimate(flops=0, bytes_accessed=8 << 20, transcendentals=0),
+    )(plan, pinned(rights))
 
 
 def make_plan(me, shifts, active, lefts, rights, blocks_dev):
@@ -155,10 +169,10 @@
         ],
         in_specs=[SMEM] * 3 + [far] * 2,
         out_specs=[SMEM, VMEM, VMEM],
-        scratch_shapes=[pltpu.VMEM(rights.shape, rights.dtype), pltpu.SemaphoreType.DMA((2,))],
-        compiler_params=params(8),
+        scratch_shapes=[pltpu.SemaphoreType.DMA((2,))],
+        compiler_params=params(4),
         cost_estimate=pl.CostEstimate(flops=0, bytes_accessed=16 << 20, transcendentals=0),
-    )(me, shifts, active, *(pltpu.with_memory_space_constraint(array, pltpu.HBM) for array in (lefts, rights)))
+    )(me, *(pltpu.with_memory_space_constraint(array, pltpu.HBM) for array in (shifts, active, lefts, rights)))
 
 
 def pair_product(index, plan_ref, left_ref, right_ref, low_ref):
@@ -307,9 +321,8 @@
 
     for side in range(2):
         grouped(side, plan_ref, left_ref, right_ref, low_ref, take)
-    terms = value_ref.shape[0]
-    for term in range(terms):
-        value_ref[term : term + 1, :] = jnp.full((1, width), jnp.sum(sum_ref[term]) * (1.0 / count))
+    for term in range(value_ref.shape[1]):
+        value_ref[0, term] = jnp.sum(sum_ref[term]) * (1.0 / count)
 
 
 def term_values(plan, lefts, rights, chunks, own, olds, count, terms):
@@ -319,9 +332,9 @@
     pairs_all = lefts.shape[0]
     return pl.pallas_call(
         functools.partial(values_kernel, devices, len(olds), count),
-        out_shape=[jax.ShapeDtypeStruct((rows, width), low_type), jax.ShapeDtypeStruct((terms, width), wide_type)],
+        out_shape=[jax.ShapeDtypeStruct((rows, width), low_type), jax.ShapeDtypeStruct((1, terms), wide_type)],
         in_specs=[SMEM] + [VMEM] * (3 + devices + len(olds)),
-        out_specs=[VMEM] * 2,
+        out_specs=[VMEM, SMEM],
         scratch_shapes=[
             pltpu.VMEM((total // width + 1, width, width), low_type),
             pltpu.VMEM((terms + 1, 8, width), wide_type),
@@ -422,6 +435,7 @@
     lefts = left_ops.reshape(terms * blocks_all, width, width)
     rights = right_ops.reshape(terms * blocks_all, width, width)
     plan, lefts, rights = make_plan(me, shifts, active[0], lefts, rights, blocks_dev)
+    rights = turned(plan, rights)
     chunks = gathered(own_low, [plan])
     own_source = own_low
     olds = []
@@ -438,7 +452,7 @@
         own_source, sent = total_applied(own_wide, coupled, added(parts))
         chunks = gathered(sent)
     state, values = term_values(plan, lefts, rights, chunks, own_source, olds, count, terms)
-    return state.reshape(psi_start.shape), values[:, 0].reshape(shifts.shape)
+    return state.reshape(psi_start.shape), values
 
 
 def solution(mesh):

time: 164 us -> 160 us (0.976)
  waiting for transfers between devices: 67 us -> 58 us
  starting transfers between devices: 60.4 us -> 68.2 us
  local copies, waits for them, and re-layouts: 1.96 us -> 0.01 us
    ppermute x49, waiting for transfers between devices: 67 us -> 58 us  [traded(): return lax.ppermute(block, 'op', route)]
    ppermute x6, starting transfers between devices: 7.88 us -> 11.9 us  [neighbours(): found.append(lax.ppermute(block, 'seg', pairs + [(j, i) for i, j in pairs]))]
    ppermute x49, starting transfers between devices: 52.5 us -> 56.3 us  [traded(): return lax.ppermute(block, 'op', route)]
    pallas_call x0 -> x1, Pallas kernels: none -> 2.45 us  [turned(): pl.pallas_call(turn_kernel, out_shape=kept(rights.shape, rights.dtype), i...]
    pallas_call x1, Pallas kernels: 6.63 us -> 4.97 us  [make_plan(): pl.pallas_call(functools.partial(plan_kernel, blocks_dev), out_shape=[jax...]
  transfers between devices with their start and end apart: 55 -> 55, of which waited for: 31 -> 28; matrix products, arithmetic and copies ran while one was open for 0% -> 0% of each run, Pallas kernels for 13% -> 14%
where the time goes in v4:
time: 160 us
  starting transfers between devices  68.2 us (43%)
  waiting for transfers between devices  58 us (36%)
  Pallas kernels  32.4 us (20%)
    ppermute x49, waiting for transfers between devices, traded(): return lax.ppermute(block, 'op', route)  58 us
    ppermute x49, starting transfers between devices, traded(): return lax.ppermute(block, 'op', route)  56.3 us
    pallas_call x3, Pallas kernels, apply_terms(): pl.pallas_call(functools.partial(near_kernel, term_scale), out_shape=[kep...  12.3 us
    ppermute x6, starting transfers between devices, neighbours(): found.append(lax.ppermute(block, 'seg', pairs + [(j, i) for i, j in pairs]))  11.9 us
    pallas_call x1, Pallas kernels, term_values(): pl.pallas_call(functools.partial(values_kernel, devices, len(olds), count...  5.41 us
    pallas_call x1, Pallas kernels, make_plan(): pl.pallas_call(functools.partial(plan_kernel, blocks_dev), out_shape=[jax...  4.97 us
    pallas_call x3, Pallas kernels, apply_terms(): pl.pallas_call(functools.partial(far_kernel, first, devices, len(olds), c...  4.34 us
  transfers between devices with their start and end apart: 55, of which 28 were waited for; matrix products, arithmetic and copies ran while one was open for 0% of the time, Pallas kernels for 14%

profile of v4, /device:TPU:0, one launch (start us, length us, event | category | flops | bytes accessed | tf_op | source)
XLA Modules:
  0.0 159.9 jit_solution(11405274154543100825)
XLA Ops:
  0.6 4.1 %collective-permute-start.3 = (bf16[512,128]{1,0:T(8,128)(2,1)}, bf16[512,128]{1,0:T(8,128)(2,1)S(1)}, u32[]{:S(2)}, u32[]{:S(2)}) collective-permute-start(bf16[512,128]{1,0:T(8,128)(2,1)} %bitcast.6), channel_id=1, source_target_pairs={{0,4},{1,5},{2,6},{3,7},{4,0},{5,1},{6,2},{7,3},{8,12},{9,13},{10,... | collective-permute-start | bytes 393224 | tf_op jit(solution)/shard_map/ppermute | solution.py:39
  4.7 1.6 collective-permute-start.1
  6.3 1.5 collective-permute-start
  7.8 5.0 %shard_map.68 = (s32[5,274]{1,0:T(8,128)S(1)}, bf16[128,128,128]{2,1,0:T(8,128)(2,1)S(1)}, bf16[128,128,128]{2,1,0:T(8,128)(2,1)S(1)}) custom-call(s32[1]{0:T(128)} %bitcast.me_ref, s32[1,4]{1,0:T(1,128)} %shifts_ref.1, s32[4,32]{1,0:T(4,128)} %bitcast.18, bf16[128,128,128]{2,1,0:T(8,128)(2,1)} %bitcast.16, bf16[128,128,128]{2,1,0:T(8,128)(2,1)} %bitcast.17), custom_call_target="tpu_custom_call" | custom-call | bytes 16777216 | tf_op jit(solution)/shard_map/pallas_call | solution.py:163
  13.4 1.5 collective-permute-start.2
  15.3 3.3 %collective-permute-done.4.refs_8_.refs_17_ = bf16[512,128]{1,0:T(8,128)(2,1)S(1)} collective-permute-done((bf16[512,128]{1,0:T(8,128)(2,1)S(1)}, bf16[512,128]{1,0:T(8,128)(2,1)S(1)}, u32[]{:S(2)}, u32[]{:S(2)}) %collective-permute-start.4) | collective-permute-done | bytes 131104 | tf_op jit(solution)/shard_map/ppermute | solution.py:39
  19.1 2.4 %shard_map.69.refs_2_.right_ref = bf16[128,128,128]{2,1,0:T(8,128)(2,1)S(1)} custom-call(s32[5,274]{1,0:T(8,128)S(1)} %get-tuple-element.61.plan_ref.refs_0_, bf16[128,128,128]{2,1,0:T(8,128)(2,1)S(1)} %get-tuple-element.63.right_ref), custom_call_target="tpu_custom_call" | custom-call | bytes 8388608 | tf_op jit(solution)/shard_map/pallas_call | solution.py:149
  21.6 2.0 %collective-permute-done.6.refs_10_.refs_19_ = bf16[512,128]{1,0:T(8,128)(2,1)S(1)} collective-permute-done((bf16[512,128]{1,0:T(8,128)(2,1)S(1)}, bf16[512,128]{1,0:T(8,128)(2,1)S(1)}, u32[]{:S(2)}, u32[]{:S(2)}) %collective-permute-start.6) | collective-permute-done | bytes 131104 | tf_op jit(solution)/shard_map/ppermute | solution.py:39
  25.5 4.1 %shard_map.71 = (f32[512,128]{1,0:T(8,128)S(1)}, bf16[512,128]{1,0:T(8,128)(2,1)S(1)}, f32[512,128]{1,0:T(8,128)S(1)}, bf16[512,128]{1,0:T(8,128)(2,1)S(1)}, f32...) custom-call(s32[5,274]{1,0:T(8,128)S(1)} %get-tuple-element.61.plan_ref.refs_0_, ...), custom_call_target="tpu_custom_call" | custom-call | flops 268435456 | bytes 4194304 | tf_op jit(solution)/shard_map/pallas_call | solution.py:292
  33.6 2.0 %collective-permute-done.8 = bf16[512,128]{1,0:T(8,128)(2,1)S(1)} collective-permute-done((bf16[512,128]{1,0:T(8,128)(2,1)S(1)}, bf16[512,128]{1,0:T(8,128)(2,1)S(1)}, u32[]{:S(2)}, u32[]{:S(2)}) %collective-permute-start.8) | collective-permute-done | bytes 131104 | tf_op jit(solution)/shard_map/ppermute | solution.py:39
  36.3 3.7 %collective-permute-start.9 = (bf16[512,128]{1,0:T(8,128)(2,1)S(1)}, bf16[512,128]{1,0:T(8,128)(2,1)S(1)}, u32[]{:S(2)}, u32[]{:S(2)}) collective-permute-start(bf16[512,128]{1,0:T(8,128)(2,1)S(1)} %bitcast.12), channel_id=1, source_target_pairs={{0,8},{16,24},{8,0},{24,16},{1,9},{17,25},{9,1},{25,17},{2,10},{18... | collective-permute-start | bytes 393224 | tf_op jit(solution)/shard_map/ppermute | solution.py:47
  40.2 2.3 %collective-permute-start.15 = (bf16[512,128]{1,0:T(8,128)(2,1)S(1)}, bf16[512,128]{1,0:T(8,128)(2,1)S(1)}, u32[]{:S(2)}, u32[]{:S(2)}) collective-permute-start(bf16[512,128]{1,0:T(8,128)(2,1)S(1)} %add_convert_fusion.6), channel_id=1, source_target_pairs={{0,4},{1,5},{2,6},{3,7},{4,0},{5,1},{6,2},{7,3},{8,12},{9,13},{10,... | collective-permute-start | bytes 393224 | tf_op jit(solution)/shard_map/ppermute | solution.py:39
  43.2 5.1 %collective-permute-done.13.refs_2_ = bf16[512,128]{1,0:T(8,128)(2,1)S(1)} collective-permute-done((bf16[512,128]{1,0:T(8,128)(2,1)S(1)}, bf16[512,128]{1,0:T(8,128)(2,1)S(1)}, u32[]{:S(2)}, u32[]{:S(2)}) %collective-permute-start.13) | collective-permute-done | bytes 131104 | tf_op jit(solution)/shard_map/ppermute | solution.py:39
  48.6 1.3 collective-permute-start.19
  50.0 3.2 %collective-permute-start.17 = (bf16[528,128]{1,0:T(8,128)(2,1)S(1)}, bf16[528,128]{1,0:T(8,128)(2,1)S(1)}, u32[]{:S(2)}, u32[]{:S(2)}) collective-permute-start(bf16[528,128]{1,0:T(8,128)(2,1)S(1)} %get-tuple-element.78.refs_3_), channel_id=1, source_target_pairs={{0,2},{1,3},{2,0},{3,1},{4,6},{5,7},{6,4},{7,5},{8,10},{9,11},{10,... | collective-permute-start | bytes 405512 | tf_op jit(solution)/shard_map/ppermute | solution.py:39
  53.2 1.3 collective-permute-start.16
  54.4 2.5 %collective-permute-done.19.refs_7_ = bf16[528,128]{1,0:T(8,128)(2,1)S(1)} collective-permute-done((bf16[528,128]{1,0:T(8,128)(2,1)S(1)}, bf16[528,128]{1,0:T(8,128)(2,1)S(1)}, u32[]{:S(2)}, u32[]{:S(2)}) %collective-permute-start.19) | collective-permute-done | bytes 135200 | tf_op jit(solution)/shard_map/ppermute | solution.py:39
  56.9 1.8 %collective-permute-start.20 = (bf16[528,128]{1,0:T(8,128)(2,1)S(1)}, bf16[528,128]{1,0:T(8,128)(2,1)S(1)}, u32[]{:S(2)}, u32[]{:S(2)}) collective-permute-start(bf16[528,128]{1,0:T(8,128)(2,1)S(1)} %collective-permute-done.19.refs_7_), channel_id=1, source_target_pairs={{0,1},{1,0},{2,3},{3,2},{4,5},{5,4},{6,7},{7,6},{8,9},{9,8},{10,11... | collective-permute-start | bytes 405512 | tf_op jit(solution)/shard_map/ppermute | solution.py:39
  60.0 2.5 %collective-permute-done.20.refs_8_ = bf16[528,128]{1,0:T(8,128)(2,1)S(1)} collective-permute-done((bf16[528,128]{1,0:T(8,128)(2,1)S(1)}, bf16[528,128]{1,0:T(8,128)(2,1)S(1)}, u32[]{:S(2)}, u32[]{:S(2)}) %collective-permute-start.20) | collective-permute-done | bytes 135200 | tf_op jit(solution)/shard_map/ppermute | solution.py:39
  64.4 3.1 %collective-permute-done.22.refs_10_ = bf16[528,128]{1,0:T(8,128)(2,1)S(1)} collective-permute-done((bf16[528,128]{1,0:T(8,128)(2,1)S(1)}, bf16[528,128]{1,0:T(8,128)(2,1)S(1)}, u32[]{:S(2)}, u32[]{:S(2)}) %collective-permute-start.22) | collective-permute-done | bytes 135200 | tf_op jit(solution)/shard_map/ppermute | solution.py:39
  67.5 1.6 shard_map.75
  69.1 1.3 collective-permute-start.23
  70.4 4.1 %shard_map.76 = (f32[512,128]{1,0:T(8,128)S(1)}, bf16[512,128]{1,0:T(8,128)(2,1)S(1)}, f32[512,128]{1,0:T(8,128)S(1)}, bf16[512,128]{1,0:T(8,128)(2,1)S(1)}, f32...) custom-call(s32[5,274]{1,0:T(8,128)S(1)} %get-tuple-element.61.plan_ref.refs_0_, ...), custom_call_target="tpu_custom_call" | custom-call | flops 268435456 | bytes 4194304 | tf_op jit(solution)/shard_map/pallas_call | solution.py:292
  74.8 1.5 collective-permute-start.24
  76.9 1.4 collective-permute-start.27
  80.5 2.8 %collective-permute-start.25 = (bf16[512,128]{1,0:T(8,128)(2,1)S(1)}, bf16[512,128]{1,0:T(8,128)(2,1)S(1)}, u32[]{:S(2)}, u32[]{:S(2)}) collective-permute-start(bf16[512,128]{1,0:T(8,128)(2,1)S(1)} %get-tuple-element.87), channel_id=1, source_target_pairs={{0,8},{16,24},{8,0},{24,16},{1,9},{17,25},{9,1},{25,17},{2,10},{18... | collective-permute-start | bytes 393224 | tf_op jit(solution)/shard_map/ppermute | solution.py:47
  84.1 3.7 %collective-permute-start.31 = (bf16[512,128]{1,0:T(8,128)(2,1)S(1)}, bf16[512,128]{1,0:T(8,128)(2,1)S(1)}, u32[]{:S(2)}, u32[]{:S(2)}) collective-permute-start(bf16[512,128]{1,0:T(8,128)(2,1)S(1)} %add_convert_fusion.3), channel_id=1, source_target_pairs={{0,4},{1,5},{2,6},{3,7},{4,0},{5,1},{6,2},{7,3},{8,12},{9,13},{10,... | collective-permute-start | bytes 393224 | tf_op jit(solution)/shard_map/ppermute | solution.py:39
  88.5 2.6 %collective-permute-done.29.refs_2_ = bf16[512,128]{1,0:T(8,128)(2,1)S(1)} collective-permute-done((bf16[512,128]{1,0:T(8,128)(2,1)S(1)}, bf16[512,128]{1,0:T(8,128)(2,1)S(1)}, u32[]{:S(2)}, u32[]{:S(2)}) %collective-permute-start.29) | collective-permute-done | bytes 131104 | tf_op jit(solution)/shard_map/ppermute | solution.py:39
  91.1 2.6 %collective-permute-done.31.refs_3_ = bf16[512,128]{1,0:T(8,128)(2,1)S(1)} collective-permute-done((bf16[512,128]{1,0:T(8,128)(2,1)S(1)}, bf16[512,128]{1,0:T(8,128)(2,1)S(1)}, u32[]{:S(2)}, u32[]{:S(2)}) %collective-permute-start.31) | collective-permute-done | bytes 131104 | tf_op jit(solution)/shard_map/ppermute | solution.py:39
  94.1 2.9 %collective-permute-start.33 = (bf16[528,128]{1,0:T(8,128)(2,1)S(1)}, bf16[528,128]{1,0:T(8,128)(2,1)S(1)}, u32[]{:S(2)}, u32[]{:S(2)}) collective-permute-start(bf16[528,128]{1,0:T(8,128)(2,1)S(1)} %get-tuple-element.95.refs_3_), channel_id=1, source_target_pairs={{0,2},{1,3},{2,0},{3,1},{4,6},{5,7},{6,4},{7,5},{8,10},{9,11},{10,... | collective-permute-start | bytes 405512 | tf_op jit(solution)/shard_map/ppermute | solution.py:39
  98.0 3.4 %collective-permute-done.35.refs_7_ = bf16[528,128]{1,0:T(8,128)(2,1)S(1)} collective-permute-done((bf16[528,128]{1,0:T(8,128)(2,1)S(1)}, bf16[528,128]{1,0:T(8,128)(2,1)S(1)}, u32[]{:S(2)}, u32[]{:S(2)}) %collective-permute-start.35) | collective-permute-done | bytes 135200 | tf_op jit(solution)/shard_map/ppermute | solution.py:39
  103.6 2.7 %collective-permute-done.36.refs_8_ = bf16[528,128]{1,0:T(8,128)(2,1)S(1)} collective-permute-done((bf16[528,128]{1,0:T(8,128)(2,1)S(1)}, bf16[528,128]{1,0:T(8,128)(2,1)S(1)}, u32[]{:S(2)}, u32[]{:S(2)}) %collective-permute-start.36) | collective-permute-done | bytes 135200 | tf_op jit(solution)/shard_map/ppermute | solution.py:39
  107.8 3.6 %collective-permute-done.38.refs_10_ = bf16[528,128]{1,0:T(8,128)(2,1)S(1)} collective-permute-done((bf16[528,128]{1,0:T(8,128)(2,1)S(1)}, bf16[528,128]{1,0:T(8,128)(2,1)S(1)}, u32[]{:S(2)}, u32[]{:S(2)}) %collective-permute-start.38) | collective-permute-done | bytes 135200 | tf_op jit(solution)/shard_map/ppermute | solution.py:39
  111.4 1.5 shard_map.80
  113.9 4.1 %shard_map.81 = (f32[512,128]{1,0:T(8,128)S(1)}, bf16[512,128]{1,0:T(8,128)(2,1)S(1)}, f32[512,128]{1,0:T(8,128)S(1)}, bf16[512,128]{1,0:T(8,128)(2,1)S(1)}, f32...) custom-call(s32[5,274]{1,0:T(8,128)S(1)} %get-tuple-element.61.plan_ref.refs_0_, ...), custom_call_target="tpu_custom_call" | custom-call | flops 268435456 | bytes 4194304 | tf_op jit(solution)/shard_map/pallas_call | solution.py:292
  118.5 1.5 collective-permute-start.44
  120.5 1.5 collective-permute-start.46
  123.9 3.4 %collective-permute-start.41 = (bf16[512,128]{1,0:T(8,128)(2,1)S(1)}, bf16[512,128]{1,0:T(8,128)(2,1)S(1)}, u32[]{:S(2)}, u32[]{:S(2)}) collective-permute-start(bf16[512,128]{1,0:T(8,128)(2,1)S(1)} %get-tuple-element.105), channel_id=1, source_target_pairs={{0,8},{16,24},{8,0},{24,16},{1,9},{17,25},{9,1},{25,17},{2,10},{18... | collective-permute-start | bytes 393224 | tf_op jit(solution)/shard_map/ppermute | solution.py:47
  127.6 2.8 %collective-permute-start.47 = (bf16[512,128]{1,0:T(8,128)(2,1)S(1)}, bf16[512,128]{1,0:T(8,128)(2,1)S(1)}, u32[]{:S(2)}, u32[]{:S(2)}) collective-permute-start(bf16[512,128]{1,0:T(8,128)(2,1)S(1)} %add_convert_fusion), channel_id=1, source_target_pairs={{0,4},{1,5},{2,6},{3,7},{4,0},{5,1},{6,2},{7,3},{8,12},{9,13},{10,... | collective-permute-start | bytes 393224 | tf_op jit(solution)/shard_map/ppermute | solution.py:39
  131.1 4.2 %collective-permute-done.45.refs_2_ = bf16[512,128]{1,0:T(8,128)(2,1)S(1)} collective-permute-done((bf16[512,128]{1,0:T(8,128)(2,1)S(1)}, bf16[512,128]{1,0:T(8,128)(2,1)S(1)}, u32[]{:S(2)}, u32[]{:S(2)}) %collective-permute-start.45) | collective-permute-done | bytes 131104 | tf_op jit(solution)/shard_map/ppermute | solution.py:39
  135.3 1.4 collective-permute-done.47.refs_3_
  137.3 2.7 %collective-permute-start.49 = (bf16[528,128]{1,0:T(8,128)(2,1)S(1)}, bf16[528,128]{1,0:T(8,128)(2,1)S(1)}, u32[]{:S(2)}, u32[]{:S(2)}) collective-permute-start(bf16[528,128]{1,0:T(8,128)(2,1)S(1)} %get-tuple-element.113.refs_3_), channel_id=1, source_target_pairs={{0,2},{1,3},{2,0},{3,1},{4,6},{5,7},{6,4},{7,5},{8,10},{9,11},{10,... | collective-permute-start | bytes 405512 | tf_op jit(solution)/shard_map/ppermute | solution.py:39
  140.0 1.3 collective-permute-start.48
  141.3 3.2 %collective-permute-done.51.refs_7_ = bf16[528,128]{1,0:T(8,128)(2,1)S(1)} collective-permute-done((bf16[528,128]{1,0:T(8,128)(2,1)S(1)}, bf16[528,128]{1,0:T(8,128)(2,1)S(1)}, u32[]{:S(2)}, u32[]{:S(2)}) %collective-permute-start.51) | collective-permute-done | bytes 135200 | tf_op jit(solution)/shard_map/ppermute | solution.py:39
  146.8 2.7 %collective-permute-done.52.refs_8_ = bf16[528,128]{1,0:T(8,128)(2,1)S(1)} collective-permute-done((bf16[528,128]{1,0:T(8,128)(2,1)S(1)}, bf16[528,128]{1,0:T(8,128)(2,1)S(1)}, u32[]{:S(2)}, u32[]{:S(2)}) %collective-permute-start.52) | collective-permute-done | bytes 135200 | tf_op jit(solution)/shard_map/ppermute | solution.py:39
  150.1 1.9 %collective-permute-done.53.refs_9_ = bf16[528,128]{1,0:T(8,128)(2,1)S(1)} collective-permute-done((bf16[528,128]{1,0:T(8,128)(2,1)S(1)}, bf16[528,128]{1,0:T(8,128)(2,1)S(1)}, u32[]{:S(2)}, u32[]{:S(2)}) %collective-permute-start.53) | collective-permute-done | bytes 135200 | tf_op jit(solution)/shard_map/ppermute | solution.py:39
  152.0 2.5 %collective-permute-done.54.refs_10_ = bf16[528,128]{1,0:T(8,128)(2,1)S(1)} collective-permute-done((bf16[528,128]{1,0:T(8,128)(2,1)S(1)}, bf16[528,128]{1,0:T(8,128)(2,1)S(1)}, u32[]{:S(2)}, u32[]{:S(2)}) %collective-permute-start.54) | collective-permute-done | bytes 135200 | tf_op jit(solution)/shard_map/ppermute | solution.py:39
  154.5 5.4 %shard_map.85 = (bf16[512,128]{1,0:T(8,128)(2,1)}, f32[1,4]{1,0:T(1,128)}) custom-call(s32[5,274]{1,0:T(8,128)S(1)} %get-tuple-element.61.plan_ref.refs_0_, bf16[128,128,128]{2,1,0:T(8,128)(2,1)S(1)} %get-tuple-element.62.refs_1_.left_ref, bf16[128,128,128]{2,1,0:T(8,128)(2,1)S(1)} %shard_map.69.refs_2_.right_ref, ...), custom_call_target="tpu_custom_call" | custom-call | flops 536870912 | bytes 4194304 | tf_op jit(solution)/shard_map/pallas_call | solution.py:333
  (91 shorter events, 30.4 us)
Async XLA Ops:
  0.6 12.1 %collective-permute-start.3 = (bf16[512,128]{1,0:T(8,128)(2,1)}, bf16[512,128]{1,0:T(8,128)(2,1)S(1)}, u32[]{:S(2)}, u32[]{:S(2)}) collective-permute-start(bf16[512,128]{1,0:T(8,128)(2,1)} %bitcast.6), channel_id=1, source_target_pairs={{0,4},{1,5},{2,6},{3,7},{4,0},{5,1},{6,2},{7,3},{8,12},{9,13},{10,... | collective-permute-start | bytes 393224 | tf_op jit(solution)/shard_map/ppermute | solution.py:39
  4.7 8.7 %collective-permute-start.1 = (bf16[512,128]{1,0:T(8,128)(2,1)}, bf16[512,128]{1,0:T(8,128)(2,1)S(1)}, u32[]{:S(2)}, u32[]{:S(2)}) collective-permute-start(bf16[512,128]{1,0:T(8,128)(2,1)} %bitcast.7), channel_id=1, source_target_pairs={{0,2},{1,3},{2,0},{3,1},{4,6},{5,7},{6,4},{7,5},{8,10},{9,11},{10,... | collective-permute-start | bytes 393224 | tf_op jit(solution)/shard_map/ppermute | solution.py:39
  6.3 7.1 %collective-permute-start = (bf16[512,128]{1,0:T(8,128)(2,1)}, bf16[512,128]{1,0:T(8,128)(2,1)S(1)}, u32[]{:S(2)}, u32[]{:S(2)}) collective-permute-start(bf16[512,128]{1,0:T(8,128)(2,1)} %bitcast.8), channel_id=1, source_target_pairs={{0,1},{1,0},{2,3},{3,2},{4,5},{5,4},{6,7},{7,6},{8,9},{9,8},{10,11... | collective-permute-start | bytes 393224 | tf_op jit(solution)/shard_map/ppermute | solution.py:39
  12.8 5.9 %collective-permute-start.4 = (bf16[512,128]{1,0:T(8,128)(2,1)S(1)}, bf16[512,128]{1,0:T(8,128)(2,1)S(1)}, u32[]{:S(2)}, u32[]{:S(2)}) collective-permute-start(bf16[512,128]{1,0:T(8,128)(2,1)S(1)} %collective-permute-done.3.refs_7_.refs_16_), channel_id=1, source_target_pairs={{0,1},{1,0},{2,3},{3,2},{4,5},{5,4},{6,7},{7,6},{8,9},{9,8},{10,11... | collective-permute-start | bytes 393224 | tf_op jit(solution)/shard_map/ppermute | solution.py:39
  13.4 8.2 %collective-permute-start.2 = (bf16[512,128]{1,0:T(8,128)(2,1)S(1)}, bf16[512,128]{1,0:T(8,128)(2,1)S(1)}, u32[]{:S(2)}, u32[]{:S(2)}) collective-permute-start(bf16[512,128]{1,0:T(8,128)(2,1)S(1)} %collective-permute-done.1.refs_5_.refs_14_), channel_id=1, source_target_pairs={{0,1},{1,0},{2,3},{3,2},{4,5},{5,4},{6,7},{7,6},{8,9},{9,8},{10,11... | collective-permute-start | bytes 393224 | tf_op jit(solution)/shard_map/ppermute | solution.py:39
  14.9 6.7 %collective-permute-start.5 = (bf16[512,128]{1,0:T(8,128)(2,1)S(1)}, bf16[512,128]{1,0:T(8,128)(2,1)S(1)}, u32[]{:S(2)}, u32[]{:S(2)}) collective-permute-start(bf16[512,128]{1,0:T(8,128)(2,1)S(1)} %collective-permute-done.3.refs_7_.refs_16_), channel_id=1, source_target_pairs={{0,2},{1,3},{2,0},{3,1},{4,6},{5,7},{6,4},{7,5},{8,10},{9,11},{10,... | collective-permute-start | bytes 393224 | tf_op jit(solution)/shard_map/ppermute | solution.py:39
  24.9 5.7 %collective-permute-start.7 = (bf16[512,128]{1,0:T(8,128)(2,1)S(1)}, bf16[512,128]{1,0:T(8,128)(2,1)S(1)}, u32[]{:S(2)}, u32[]{:S(2)}) collective-permute-start(bf16[512,128]{1,0:T(8,128)(2,1)S(1)} %get-tuple-element.69), channel_id=1, source_target_pairs={{0,1},{1,0},{2,3},{3,2},{4,5},{5,4},{6,7},{7,6},{8,9},{9,8},{10,11... | collective-permute-start | bytes 393224 | tf_op jit(solution)/shard_map/ppermute | solution.py:39
  30.6 5.0 %collective-permute-start.8 = (bf16[512,128]{1,0:T(8,128)(2,1)S(1)}, bf16[512,128]{1,0:T(8,128)(2,1)S(1)}, u32[]{:S(2)}, u32[]{:S(2)}) collective-permute-start(bf16[512,128]{1,0:T(8,128)(2,1)S(1)} %add_convert_fusion.8), channel_id=1, source_target_pairs={{0,2},{1,3},{2,0},{3,1},{4,6},{5,7},{6,4},{7,5},{8,10},{9,11},{10,... | collective-permute-start | bytes 393224 | tf_op jit(solution)/shard_map/ppermute | solution.py:39
  30.7 9.3 %collective-permute-start.12 = (bf16[512,128]{1,0:T(8,128)(2,1)S(1)}, bf16[512,128]{1,0:T(8,128)(2,1)S(1)}, u32[]{:S(2)}, u32[]{:S(2)}) collective-permute-start(bf16[512,128]{1,0:T(8,128)(2,1)S(1)} %get-tuple-element.75), channel_id=1, source_target_pairs={{0,1},{1,0},{2,3},{3,2},{4,5},{5,4},{6,7},{7,6},{8,9},{9,8},{10,11... | collective-permute-start | bytes 393224 | tf_op jit(solution)/shard_map/ppermute | solution.py:39
  31.6 11.7 %collective-permute-start.11 = (bf16[512,128]{1,0:T(8,128)(2,1)S(1)}, bf16[512,128]{1,0:T(8,128)(2,1)S(1)}, u32[]{:S(2)}, u32[]{:S(2)}) collective-permute-start(bf16[512,128]{1,0:T(8,128)(2,1)S(1)} %get-tuple-element.72), channel_id=1, source_target_pairs={{0,1},{1,0},{2,3},{3,2},{4,5},{5,4},{6,7},{7,6},{8,9},{9,8},{10,11... | collective-permute-start | bytes 393224 | tf_op jit(solution)/shard_map/ppermute | solution.py:39
  32.8 7.4 %collective-permute-start.14 = (bf16[512,128]{1,0:T(8,128)(2,1)S(1)}, bf16[512,128]{1,0:T(8,128)(2,1)S(1)}, u32[]{:S(2)}, u32[]{:S(2)}) collective-permute-start(bf16[512,128]{1,0:T(8,128)(2,1)S(1)} %get-tuple-element.77), channel_id=1, source_target_pairs={{0,1},{1,0},{2,3},{3,2},{4,5},{5,4},{6,7},{7,6},{8,9},{9,8},{10,11... | collective-permute-start | bytes 393224 | tf_op jit(solution)/shard_map/ppermute | solution.py:39
  35.6 6.9 %collective-permute-start.10 = (bf16[512,128]{1,0:T(8,128)(2,1)S(1)}, bf16[512,128]{1,0:T(8,128)(2,1)S(1)}, u32[]{:S(2)}, u32[]{:S(2)}) collective-permute-start(bf16[512,128]{1,0:T(8,128)(2,1)S(1)} %bitcast.11), channel_id=1, source_target_pairs={{8,16},{16,8},{9,17},{17,9},{10,18},{18,10},{11,19},{19,11},{12,20... | collective-permute-start | bytes 393224 | tf_op jit(solution)/shard_map/ppermute | solution.py:47
  36.3 6.2 %collective-permute-start.9 = (bf16[512,128]{1,0:T(8,128)(2,1)S(1)}, bf16[512,128]{1,0:T(8,128)(2,1)S(1)}, u32[]{:S(2)}, u32[]{:S(2)}) collective-permute-start(bf16[512,128]{1,0:T(8,128)(2,1)S(1)} %bitcast.12), channel_id=1, source_target_pairs={{0,8},{16,24},{8,0},{24,16},{1,9},{17,25},{9,1},{25,17},{2,10},{18... | collective-permute-start | bytes 393224 | tf_op jit(solution)/shard_map/ppermute | solution.py:47
  40.1 8.3 %collective-permute-start.13 = (bf16[512,128]{1,0:T(8,128)(2,1)S(1)}, bf16[512,128]{1,0:T(8,128)(2,1)S(1)}, u32[]{:S(2)}, u32[]{:S(2)}) collective-permute-start(bf16[512,128]{1,0:T(8,128)(2,1)S(1)} %add_convert_fusion.7), channel_id=1, source_target_pairs={{0,2},{1,3},{2,0},{3,1},{4,6},{5,7},{6,4},{7,5},{8,10},{9,11},{10,... | collective-permute-start | bytes 393224 | tf_op jit(solution)/shard_map/ppermute | solution.py:39
  40.2 8.2 %collective-permute-start.15 = (bf16[512,128]{1,0:T(8,128)(2,1)S(1)}, bf16[512,128]{1,0:T(8,128)(2,1)S(1)}, u32[]{:S(2)}, u32[]{:S(2)}) collective-permute-start(bf16[512,128]{1,0:T(8,128)(2,1)S(1)} %add_convert_fusion.6), channel_id=1, source_target_pairs={{0,4},{1,5},{2,6},{3,7},{4,0},{5,1},{6,2},{7,3},{8,12},{9,13},{10,... | collective-permute-start | bytes 393224 | tf_op jit(solution)/shard_map/ppermute | solution.py:39
  48.6 8.2 %collective-permute-start.19 = (bf16[528,128]{1,0:T(8,128)(2,1)S(1)}, bf16[528,128]{1,0:T(8,128)(2,1)S(1)}, u32[]{:S(2)}, u32[]{:S(2)}) collective-permute-start(bf16[528,128]{1,0:T(8,128)(2,1)S(1)} %get-tuple-element.78.refs_3_), channel_id=1, source_target_pairs={{0,4},{1,5},{2,6},{3,7},{4,0},{5,1},{6,2},{7,3},{8,12},{9,13},{10,... | collective-permute-start | bytes 405512 | tf_op jit(solution)/shard_map/ppermute | solution.py:39
  50.0 8.7 %collective-permute-start.17 = (bf16[528,128]{1,0:T(8,128)(2,1)S(1)}, bf16[528,128]{1,0:T(8,128)(2,1)S(1)}, u32[]{:S(2)}, u32[]{:S(2)}) collective-permute-start(bf16[528,128]{1,0:T(8,128)(2,1)S(1)} %get-tuple-element.78.refs_3_), channel_id=1, source_target_pairs={{0,2},{1,3},{2,0},{3,1},{4,6},{5,7},{6,4},{7,5},{8,10},{9,11},{10,... | collective-permute-start | bytes 405512 | tf_op jit(solution)/shard_map/ppermute | solution.py:39
  53.2 5.9 %collective-permute-start.16 = (bf16[528,128]{1,0:T(8,128)(2,1)S(1)}, bf16[528,128]{1,0:T(8,128)(2,1)S(1)}, u32[]{:S(2)}, u32[]{:S(2)}) collective-permute-start(bf16[528,128]{1,0:T(8,128)(2,1)S(1)} %get-tuple-element.78.refs_3_), channel_id=1, source_target_pairs={{0,1},{1,0},{2,3},{3,2},{4,5},{5,4},{6,7},{7,6},{8,9},{9,8},{10,11... | collective-permute-start | bytes 405512 | tf_op jit(solution)/shard_map/ppermute | solution.py:39
  56.9 5.6 %collective-permute-start.20 = (bf16[528,128]{1,0:T(8,128)(2,1)S(1)}, bf16[528,128]{1,0:T(8,128)(2,1)S(1)}, u32[]{:S(2)}, u32[]{:S(2)}) collective-permute-start(bf16[528,128]{1,0:T(8,128)(2,1)S(1)} %collective-permute-done.19.refs_7_), channel_id=1, source_target_pairs={{0,1},{1,0},{2,3},{3,2},{4,5},{5,4},{6,7},{7,6},{8,9},{9,8},{10,11... | collective-permute-start | bytes 405512 | tf_op jit(solution)/shard_map/ppermute | solution.py:39
  58.7 5.7 %collective-permute-start.21 = (bf16[528,128]{1,0:T(8,128)(2,1)S(1)}, bf16[528,128]{1,0:T(8,128)(2,1)S(1)}, u32[]{:S(2)}, u32[]{:S(2)}) collective-permute-start(bf16[528,128]{1,0:T(8,128)(2,1)S(1)} %collective-permute-done.19.refs_7_), channel_id=1, source_target_pairs={{0,2},{1,3},{2,0},{3,1},{4,6},{5,7},{6,4},{7,5},{8,10},{9,11},{10,... | collective-permute-start | bytes 405512 | tf_op jit(solution)/shard_map/ppermute | solution.py:39
  59.1 5.3 %collective-permute-start.18 = (bf16[528,128]{1,0:T(8,128)(2,1)S(1)}, bf16[528,128]{1,0:T(8,128)(2,1)S(1)}, u32[]{:S(2)}, u32[]{:S(2)}) collective-permute-start(bf16[528,128]{1,0:T(8,128)(2,1)S(1)} %collective-permute-done.17.refs_5_), channel_id=1, source_target_pairs={{0,1},{1,0},{2,3},{3,2},{4,5},{5,4},{6,7},{7,6},{8,9},{9,8},{10,11... | collective-permute-start | bytes 405512 | tf_op jit(solution)/shard_map/ppermute | solution.py:39
  69.1 5.6 %collective-permute-start.23 = (bf16[512,128]{1,0:T(8,128)(2,1)S(1)}, bf16[512,128]{1,0:T(8,128)(2,1)S(1)}, u32[]{:S(2)}, u32[]{:S(2)}) collective-permute-start(bf16[512,128]{1,0:T(8,128)(2,1)S(1)} %get-tuple-element.86), channel_id=1, source_target_pairs={{0,1},{1,0},{2,3},{3,2},{4,5},{5,4},{6,7},{7,6},{8,9},{9,8},{10,11... | collective-permute-start | bytes 393224 | tf_op jit(solution)/shard_map/ppermute | solution.py:39
  74.8 5.0 %collective-permute-start.24 = (bf16[512,128]{1,0:T(8,128)(2,1)S(1)}, bf16[512,128]{1,0:T(8,128)(2,1)S(1)}, u32[]{:S(2)}, u32[]{:S(2)}) collective-permute-start(bf16[512,128]{1,0:T(8,128)(2,1)S(1)} %add_convert_fusion.5), channel_id=1, source_target_pairs={{0,2},{1,3},{2,0},{3,1},{4,6},{5,7},{6,4},{7,5},{8,10},{9,11},{10,... | collective-permute-start | bytes 393224 | tf_op jit(solution)/shard_map/ppermute | solution.py:39
  76.3 7.0 %collective-permute-start.28 = (bf16[512,128]{1,0:T(8,128)(2,1)S(1)}, bf16[512,128]{1,0:T(8,128)(2,1)S(1)}, u32[]{:S(2)}, u32[]{:S(2)}) collective-permute-start(bf16[512,128]{1,0:T(8,128)(2,1)S(1)} %get-tuple-element.92), channel_id=1, source_target_pairs={{0,1},{1,0},{2,3},{3,2},{4,5},{5,4},{6,7},{7,6},{8,9},{9,8},{10,11... | collective-permute-start | bytes 393224 | tf_op jit(solution)/shard_map/ppermute | solution.py:39
  76.9 11.7 %collective-permute-start.27 = (bf16[512,128]{1,0:T(8,128)(2,1)S(1)}, bf16[512,128]{1,0:T(8,128)(2,1)S(1)}, u32[]{:S(2)}, u32[]{:S(2)}) collective-permute-start(bf16[512,128]{1,0:T(8,128)(2,1)S(1)} %get-tuple-element.89), channel_id=1, source_target_pairs={{0,1},{1,0},{2,3},{3,2},{4,5},{5,4},{6,7},{7,6},{8,9},{9,8},{10,11... | collective-permute-start | bytes 393224 | tf_op jit(solution)/shard_map/ppermute | solution.py:39
  78.3 5.8 %collective-permute-start.30 = (bf16[512,128]{1,0:T(8,128)(2,1)S(1)}, bf16[512,128]{1,0:T(8,128)(2,1)S(1)}, u32[]{:S(2)}, u32[]{:S(2)}) collective-permute-start(bf16[512,128]{1,0:T(8,128)(2,1)S(1)} %get-tuple-element.94), channel_id=1, source_target_pairs={{0,1},{1,0},{2,3},{3,2},{4,5},{5,4},{6,7},{7,6},{8,9},{9,8},{10,11... | collective-permute-start | bytes 393224 | tf_op jit(solution)/shard_map/ppermute | solution.py:39
  79.8 8.0 %collective-permute-start.26 = (bf16[512,128]{1,0:T(8,128)(2,1)S(1)}, bf16[512,128]{1,0:T(8,128)(2,1)S(1)}, u32[]{:S(2)}, u32[]{:S(2)}) collective-permute-start(bf16[512,128]{1,0:T(8,128)(2,1)S(1)} %get-tuple-element.87), channel_id=1, source_target_pairs={{8,16},{16,8},{9,17},{17,9},{10,18},{18,10},{11,19},{19,11},{12,20... | collective-permute-start | bytes 393224 | tf_op jit(solution)/shard_map/ppermute | solution.py:47
  80.5 7.3 %collective-permute-start.25 = (bf16[512,128]{1,0:T(8,128)(2,1)S(1)}, bf16[512,128]{1,0:T(8,128)(2,1)S(1)}, u32[]{:S(2)}, u32[]{:S(2)}) collective-permute-start(bf16[512,128]{1,0:T(8,128)(2,1)S(1)} %get-tuple-element.87), channel_id=1, source_target_pairs={{0,8},{16,24},{8,0},{24,16},{1,9},{17,25},{9,1},{25,17},{2,10},{18... | collective-permute-start | bytes 393224 | tf_op jit(solution)/shard_map/ppermute | solution.py:47
  83.3 7.9 %collective-permute-start.29 = (bf16[512,128]{1,0:T(8,128)(2,1)S(1)}, bf16[512,128]{1,0:T(8,128)(2,1)S(1)}, u32[]{:S(2)}, u32[]{:S(2)}) collective-permute-start(bf16[512,128]{1,0:T(8,128)(2,1)S(1)} %add_convert_fusion.4), channel_id=1, source_target_pairs={{0,2},{1,3},{2,0},{3,1},{4,6},{5,7},{6,4},{7,5},{8,10},{9,11},{10,... | collective-permute-start | bytes 393224 | tf_op jit(solution)/shard_map/ppermute | solution.py:39
  84.1 9.7 %collective-permute-start.31 = (bf16[512,128]{1,0:T(8,128)(2,1)S(1)}, bf16[512,128]{1,0:T(8,128)(2,1)S(1)}, u32[]{:S(2)}, u32[]{:S(2)}) collective-permute-start(bf16[512,128]{1,0:T(8,128)(2,1)S(1)} %add_convert_fusion.3), channel_id=1, source_target_pairs={{0,4},{1,5},{2,6},{3,7},{4,0},{5,1},{6,2},{7,3},{8,12},{9,13},{10,... | collective-permute-start | bytes 393224 | tf_op jit(solution)/shard_map/ppermute | solution.py:39
  94.1 7.3 %collective-permute-start.35 = (bf16[528,128]{1,0:T(8,128)(2,1)S(1)}, bf16[528,128]{1,0:T(8,128)(2,1)S(1)}, u32[]{:S(2)}, u32[]{:S(2)}) collective-permute-start(bf16[528,128]{1,0:T(8,128)(2,1)S(1)} %get-tuple-element.95.refs_3_), channel_id=1, source_target_pairs={{0,4},{1,5},{2,6},{3,7},{4,0},{5,1},{6,2},{7,3},{8,12},{9,13},{10,... | collective-permute-start | bytes 405512 | tf_op jit(solution)/shard_map/ppermute | solution.py:39
  94.1 8.1 %collective-permute-start.33 = (bf16[528,128]{1,0:T(8,128)(2,1)S(1)}, bf16[528,128]{1,0:T(8,128)(2,1)S(1)}, u32[]{:S(2)}, u32[]{:S(2)}) collective-permute-start(bf16[528,128]{1,0:T(8,128)(2,1)S(1)} %get-tuple-element.95.refs_3_), channel_id=1, source_target_pairs={{0,2},{1,3},{2,0},{3,1},{4,6},{5,7},{6,4},{7,5},{8,10},{9,11},{10,... | collective-permute-start | bytes 405512 | tf_op jit(solution)/shard_map/ppermute | solution.py:39
  97.0 5.4 %collective-permute-start.32 = (bf16[528,128]{1,0:T(8,128)(2,1)S(1)}, bf16[528,128]{1,0:T(8,128)(2,1)S(1)}, u32[]{:S(2)}, u32[]{:S(2)}) collective-permute-start(bf16[528,128]{1,0:T(8,128)(2,1)S(1)} %get-tuple-element.95.refs_3_), channel_id=1, source_target_pairs={{0,1},{1,0},{2,3},{3,2},{4,5},{5,4},{6,7},{7,6},{8,9},{9,8},{10,11... | collective-permute-start | bytes 405512 | tf_op jit(solution)/shard_map/ppermute | solution.py:39
  102.4 5.4 %collective-permute-start.34 = (bf16[528,128]{1,0:T(8,128)(2,1)S(1)}, bf16[528,128]{1,0:T(8,128)(2,1)S(1)}, u32[]{:S(2)}, u32[]{:S(2)}) collective-permute-start(bf16[528,128]{1,0:T(8,128)(2,1)S(1)} %collective-permute-done.33.refs_5_), channel_id=1, source_target_pairs={{0,1},{1,0},{2,3},{3,2},{4,5},{5,4},{6,7},{7,6},{8,9},{9,8},{10,11... | collective-permute-start | bytes 405512 | tf_op jit(solution)/shard_map/ppermute | solution.py:39
  112.9 5.3 %collective-permute-start.39 = (bf16[512,128]{1,0:T(8,128)(2,1)S(1)}, bf16[512,128]{1,0:T(8,128)(2,1)S(1)}, u32[]{:S(2)}, u32[]{:S(2)}) collective-permute-start(bf16[512,128]{1,0:T(8,128)(2,1)S(1)} %get-tuple-element.104), channel_id=1, source_target_pairs={{0,1},{1,0},{2,3},{3,2},{4,5},{5,4},{6,7},{7,6},{8,9},{9,8},{10,11... | collective-permute-start | bytes 393224 | tf_op jit(solution)/shard_map/ppermute | solution.py:39
  118.2 5.0 %collective-permute-start.40 = (bf16[512,128]{1,0:T(8,128)(2,1)S(1)}, bf16[512,128]{1,0:T(8,128)(2,1)S(1)}, u32[]{:S(2)}, u32[]{:S(2)}) collective-permute-start(bf16[512,128]{1,0:T(8,128)(2,1)S(1)} %add_convert_fusion.2), channel_id=1, source_target_pairs={{0,2},{1,3},{2,0},{3,1},{4,6},{5,7},{6,4},{7,5},{8,10},{9,11},{10,... | collective-permute-start | bytes 393224 | tf_op jit(solution)/shard_map/ppermute | solution.py:39
  118.5 8.9 %collective-permute-start.44 = (bf16[512,128]{1,0:T(8,128)(2,1)S(1)}, bf16[512,128]{1,0:T(8,128)(2,1)S(1)}, u32[]{:S(2)}, u32[]{:S(2)}) collective-permute-start(bf16[512,128]{1,0:T(8,128)(2,1)S(1)} %get-tuple-element.110), channel_id=1, source_target_pairs={{0,1},{1,0},{2,3},{3,2},{4,5},{5,4},{6,7},{7,6},{8,9},{9,8},{10,11... | collective-permute-start | bytes 393224 | tf_op jit(solution)/shard_map/ppermute | solution.py:39
  120.0 11.1 %collective-permute-start.43 = (bf16[512,128]{1,0:T(8,128)(2,1)S(1)}, bf16[512,128]{1,0:T(8,128)(2,1)S(1)}, u32[]{:S(2)}, u32[]{:S(2)}) collective-permute-start(bf16[512,128]{1,0:T(8,128)(2,1)S(1)} %get-tuple-element.107), channel_id=1, source_target_pairs={{0,1},{1,0},{2,3},{3,2},{4,5},{5,4},{6,7},{7,6},{8,9},{9,8},{10,11... | collective-permute-start | bytes 393224 | tf_op jit(solution)/shard_map/ppermute | solution.py:39
  120.5 7.0 %collective-permute-start.46 = (bf16[512,128]{1,0:T(8,128)(2,1)S(1)}, bf16[512,128]{1,0:T(8,128)(2,1)S(1)}, u32[]{:S(2)}, u32[]{:S(2)}) collective-permute-start(bf16[512,128]{1,0:T(8,128)(2,1)S(1)} %get-tuple-element.112), channel_id=1, source_target_pairs={{0,1},{1,0},{2,3},{3,2},{4,5},{5,4},{6,7},{7,6},{8,9},{9,8},{10,11... | collective-permute-start | bytes 393224 | tf_op jit(solution)/shard_map/ppermute | solution.py:39
  123.3 7.1 %collective-permute-start.42 = (bf16[512,128]{1,0:T(8,128)(2,1)S(1)}, bf16[512,128]{1,0:T(8,128)(2,1)S(1)}, u32[]{:S(2)}, u32[]{:S(2)}) collective-permute-start(bf16[512,128]{1,0:T(8,128)(2,1)S(1)} %get-tuple-element.105), channel_id=1, source_target_pairs={{8,16},{16,8},{9,17},{17,9},{10,18},{18,10},{11,19},{19,11},{12,20... | collective-permute-start | bytes 393224 | tf_op jit(solution)/shard_map/ppermute | solution.py:47
  123.9 6.4 %collective-permute-start.41 = (bf16[512,128]{1,0:T(8,128)(2,1)S(1)}, bf16[512,128]{1,0:T(8,128)(2,1)S(1)}, u32[]{:S(2)}, u32[]{:S(2)}) collective-permute-start(bf16[512,128]{1,0:T(8,128)(2,1)S(1)} %get-tuple-element.105), channel_id=1, source_target_pairs={{0,8},{16,24},{8,0},{24,16},{1,9},{17,25},{9,1},{25,17},{2,10},{18... | collective-permute-start | bytes 393224 | tf_op jit(solution)/shard_map/ppermute | solution.py:47
  127.4 8.0 %collective-permute-start.45 = (bf16[512,128]{1,0:T(8,128)(2,1)S(1)}, bf16[512,128]{1,0:T(8,128)(2,1)S(1)}, u32[]{:S(2)}, u32[]{:S(2)}) collective-permute-start(bf16[512,128]{1,0:T(8,128)(2,1)S(1)} %add_convert_fusion.1), channel_id=1, source_target_pairs={{0,2},{1,3},{2,0},{3,1},{4,6},{5,7},{6,4},{7,5},{8,10},{9,11},{10,... | collective-permute-start | bytes 393224 | tf_op jit(solution)/shard_map/ppermute | solution.py:39
  127.6 9.2 %collective-permute-start.47 = (bf16[512,128]{1,0:T(8,128)(2,1)S(1)}, bf16[512,128]{1,0:T(8,128)(2,1)S(1)}, u32[]{:S(2)}, u32[]{:S(2)}) collective-permute-start(bf16[512,128]{1,0:T(8,128)(2,1)S(1)} %add_convert_fusion), channel_id=1, source_target_pairs={{0,4},{1,5},{2,6},{3,7},{4,0},{5,1},{6,2},{7,3},{8,12},{9,13},{10,... | collective-permute-start | bytes 393224 | tf_op jit(solution)/shard_map/ppermute | solution.py:39
  137.1 7.4 %collective-permute-start.51 = (bf16[528,128]{1,0:T(8,128)(2,1)S(1)}, bf16[528,128]{1,0:T(8,128)(2,1)S(1)}, u32[]{:S(2)}, u32[]{:S(2)}) collective-permute-start(bf16[528,128]{1,0:T(8,128)(2,1)S(1)} %get-tuple-element.113.refs_3_), channel_id=1, source_target_pairs={{0,4},{1,5},{2,6},{3,7},{4,0},{5,1},{6,2},{7,3},{8,12},{9,13},{10,... | collective-permute-start | bytes 405512 | tf_op jit(solution)/shard_map/ppermute | solution.py:39
  137.3 8.2 %collective-permute-start.49 = (bf16[528,128]{1,0:T(8,128)(2,1)S(1)}, bf16[528,128]{1,0:T(8,128)(2,1)S(1)}, u32[]{:S(2)}, u32[]{:S(2)}) collective-permute-start(bf16[528,128]{1,0:T(8,128)(2,1)S(1)} %get-tuple-element.113.refs_3_), channel_id=1, source_target_pairs={{0,2},{1,3},{2,0},{3,1},{4,6},{5,7},{6,4},{7,5},{8,10},{9,11},{10,... | collective-permute-start | bytes 405512 | tf_op jit(solution)/shard_map/ppermute | solution.py:39
  140.0 6.4 %collective-permute-start.48 = (bf16[528,128]{1,0:T(8,128)(2,1)S(1)}, bf16[528,128]{1,0:T(8,128)(2,1)S(1)}, u32[]{:S(2)}, u32[]{:S(2)}) collective-permute-start(bf16[528,128]{1,0:T(8,128)(2,1)S(1)} %get-tuple-element.113.refs_3_), channel_id=1, source_target_pairs={{0,1},{1,0},{2,3},{3,2},{4,5},{5,4},{6,7},{7,6},{8,9},{9,8},{10,11... | collective-permute-start | bytes 405512 | tf_op jit(solution)/shard_map/ppermute | solution.py:39
  145.6 6.4 %collective-permute-start.53 = (bf16[528,128]{1,0:T(8,128)(2,1)S(1)}, bf16[528,128]{1,0:T(8,128)(2,1)S(1)}, u32[]{:S(2)}, u32[]{:S(2)}) collective-permute-start(bf16[528,128]{1,0:T(8,128)(2,1)S(1)} %collective-permute-done.51.refs_7_), channel_id=1, source_target_pairs={{0,2},{1,3},{2,0},{3,1},{4,6},{5,7},{6,4},{7,5},{8,10},{9,11},{10,... | collective-permute-start | bytes 405512 | tf_op jit(solution)/shard_map/ppermute | solution.py:39
  146.4 5.6 %collective-permute-start.50 = (bf16[528,128]{1,0:T(8,128)(2,1)S(1)}, bf16[528,128]{1,0:T(8,128)(2,1)S(1)}, u32[]{:S(2)}, u32[]{:S(2)}) collective-permute-start(bf16[528,128]{1,0:T(8,128)(2,1)S(1)} %collective-permute-done.49.refs_5_), channel_id=1, source_target_pairs={{0,1},{1,0},{2,3},{3,2},{4,5},{5,4},{6,7},{7,6},{8,9},{9,8},{10,11... | collective-permute-start | bytes 405512 | tf_op jit(solution)/shard_map/ppermute | solution.py:39
  (8 other events, 39.6 us)

commit v5 on v4

--- a/solution.py
+++ b/solution.py
@@ -222,15 +222,16 @@
 
 def grouped(side, plan_ref, left_ref, right_ref, low_ref, take):
     room = plan_ref.shape[1] // 2
+    size = (GROUP // 2, GROUP)[side]
 
     def group(index, carried):
-        first = side * room + index * GROUP
-        products = [pair_product(first + inner, plan_ref, left_ref, right_ref, low_ref) for inner in range(GROUP)]
+        first = side * room + index * size
+        products = [pair_product(first + inner, plan_ref, left_ref, right_ref, low_ref) for inner in range(size)]
         for inner, product in enumerate(products):
             take(first + inner, product)
         return carried
 
-    lax.fori_loop(0, (plan_ref[0, (side + 1) * room - 1] + GROUP - 1) // GROUP, group, 0)
+    lax.fori_loop(0, (plan_ref[0, (side + 1) * room - 1] + size - 1) // size, group, 0)
 
 
 def add_terms(side, term_scale, plan_ref, left_ref, right_ref, low_ref, piece_refs, sum_ref):

time: 160 us -> 161 us (level)
  waiting for transfers between devices: 58 us -> 54.5 us
  starting transfers between devices: 68.2 us -> 71.6 us
    ppermute x49, starting transfers between devices: 56.3 us -> 61.4 us  [traded(): return lax.ppermute(block, 'op', route)]
    ppermute x49, waiting for transfers between devices: 58 us -> 54.5 us  [traded(): return lax.ppermute(block, 'op', route)]
    ppermute x6, starting transfers between devices: 11.9 us -> 10.2 us  [neighbours(): found.append(lax.ppermute(block, 'seg', pairs + [(j, i) for i, j in pairs]))]
  transfers between devices with their start and end apart: 55 -> 55, of which waited for: 28 -> 27; matrix products, arithmetic and copies ran while one was open for 0% -> 0% of each run, Pallas kernels for 14% -> 14%
where the time goes in v5:
time: 161 us
  starting transfers between devices  71.6 us (44%)
  waiting for transfers between devices  54.5 us (34%)
  Pallas kernels  33.4 us (21%)
    ppermute x49, starting transfers between devices, traded(): return lax.ppermute(block, 'op', route)  61.4 us
    ppermute x49, waiting for transfers between devices, traded(): return lax.ppermute(block, 'op', route)  54.5 us
    pallas_call x3, Pallas kernels, apply_terms(): pl.pallas_call(functools.partial(near_kernel, term_scale), out_shape=[kep...  12.3 us
    ppermute x6, starting transfers between devices, neighbours(): found.append(lax.ppermute(block, 'seg', pairs + [(j, i) for i, j in pairs]))  10.2 us
    pallas_call x1, Pallas kernels, term_values(): pl.pallas_call(functools.partial(values_kernel, devices, len(olds), count...  5.67 us
    pallas_call x3, Pallas kernels, apply_terms(): pl.pallas_call(functools.partial(far_kernel, first, devices, len(olds), c...  5.09 us
    pallas_call x1, Pallas kernels, make_plan(): pl.pallas_call(functools.partial(plan_kernel, blocks_dev), out_shape=[jax...  4.97 us
  transfers between devices with their start and end apart: 55, of which 27 were waited for; matrix products, arithmetic and copies ran while one was open for 0% of the time, Pallas kernels for 14%

profile of v5, /device:TPU:0, one launch (start us, length us, event | category | flops | bytes accessed | tf_op | source)
XLA Modules:
  0.0 160.8 jit_solution(15674778959730952615)
XLA Ops:
  0.6 4.1 %collective-permute-start.3 = (bf16[512,128]{1,0:T(8,128)(2,1)}, bf16[512,128]{1,0:T(8,128)(2,1)S(1)}, u32[]{:S(2)}, u32[]{:S(2)}) collective-permute-start(bf16[512,128]{1,0:T(8,128)(2,1)} %bitcast.6), channel_id=1, source_target_pairs={{0,4},{1,5},{2,6},{3,7},{4,0},{5,1},{6,2},{7,3},{8,12},{9,13},{10,... | collective-permute-start | bytes 393224 | tf_op jit(solution)/shard_map/ppermute | solution.py:39
  4.7 1.6 collective-permute-start.1
  6.3 1.5 collective-permute-start
  7.8 5.0 %shard_map.68 = (s32[5,274]{1,0:T(8,128)S(1)}, bf16[128,128,128]{2,1,0:T(8,128)(2,1)S(1)}, bf16[128,128,128]{2,1,0:T(8,128)(2,1)S(1)}) custom-call(s32[1]{0:T(128)} %bitcast.me_ref, s32[1,4]{1,0:T(1,128)} %shifts_ref.1, s32[4,32]{1,0:T(4,128)} %bitcast.18, bf16[128,128,128]{2,1,0:T(8,128)(2,1)} %bitcast.16, bf16[128,128,128]{2,1,0:T(8,128)(2,1)} %bitcast.17), custom_call_target="tpu_custom_call" | custom-call | bytes 16777216 | tf_op jit(solution)/shard_map/pallas_call | solution.py:163
  13.4 1.5 collective-permute-start.2
  15.3 3.3 %collective-permute-done.4.refs_8_.refs_17_ = bf16[512,128]{1,0:T(8,128)(2,1)S(1)} collective-permute-done((bf16[512,128]{1,0:T(8,128)(2,1)S(1)}, bf16[512,128]{1,0:T(8,128)(2,1)S(1)}, u32[]{:S(2)}, u32[]{:S(2)}) %collective-permute-start.4) | collective-permute-done | bytes 131104 | tf_op jit(solution)/shard_map/ppermute | solution.py:39
  19.1 2.4 %shard_map.69.refs_2_.right_ref = bf16[128,128,128]{2,1,0:T(8,128)(2,1)S(1)} custom-call(s32[5,274]{1,0:T(8,128)S(1)} %get-tuple-element.61.plan_ref.refs_0_, bf16[128,128,128]{2,1,0:T(8,128)(2,1)S(1)} %get-tuple-element.63.right_ref), custom_call_target="tpu_custom_call" | custom-call | bytes 8388608 | tf_op jit(solution)/shard_map/pallas_call | solution.py:149
  21.6 2.0 %collective-permute-done.6.refs_10_.refs_19_ = bf16[512,128]{1,0:T(8,128)(2,1)S(1)} collective-permute-done((bf16[512,128]{1,0:T(8,128)(2,1)S(1)}, bf16[512,128]{1,0:T(8,128)(2,1)S(1)}, u32[]{:S(2)}, u32[]{:S(2)}) %collective-permute-start.6) | collective-permute-done | bytes 131104 | tf_op jit(solution)/shard_map/ppermute | solution.py:39
  23.6 1.5 shard_map.70
  26.0 4.1 %shard_map.71 = (f32[512,128]{1,0:T(8,128)S(1)}, bf16[512,128]{1,0:T(8,128)(2,1)S(1)}, f32[512,128]{1,0:T(8,128)S(1)}, bf16[512,128]{1,0:T(8,128)(2,1)S(1)}, f32...) custom-call(s32[5,274]{1,0:T(8,128)S(1)} %get-tuple-element.61.plan_ref.refs_0_, ...), custom_call_target="tpu_custom_call" | custom-call | flops 268435456 | bytes 4194304 | tf_op jit(solution)/shard_map/pallas_call | solution.py:293
  33.9 1.3 collective-permute-done.8
  35.9 3.6 %collective-permute-start.9 = (bf16[512,128]{1,0:T(8,128)(2,1)S(1)}, bf16[512,128]{1,0:T(8,128)(2,1)S(1)}, u32[]{:S(2)}, u32[]{:S(2)}) collective-permute-start(bf16[512,128]{1,0:T(8,128)(2,1)S(1)} %bitcast.12), channel_id=1, source_target_pairs={{0,8},{16,24},{8,0},{24,16},{1,9},{17,25},{9,1},{25,17},{2,10},{18... | collective-permute-start | bytes 393224 | tf_op jit(solution)/shard_map/ppermute | solution.py:47
  39.7 2.9 %collective-permute-start.15 = (bf16[512,128]{1,0:T(8,128)(2,1)S(1)}, bf16[512,128]{1,0:T(8,128)(2,1)S(1)}, u32[]{:S(2)}, u32[]{:S(2)}) collective-permute-start(bf16[512,128]{1,0:T(8,128)(2,1)S(1)} %add_convert_fusion.6), channel_id=1, source_target_pairs={{0,4},{1,5},{2,6},{3,7},{4,0},{5,1},{6,2},{7,3},{8,12},{9,13},{10,... | collective-permute-start | bytes 393224 | tf_op jit(solution)/shard_map/ppermute | solution.py:39
  43.4 4.4 %collective-permute-done.13.refs_2_ = bf16[512,128]{1,0:T(8,128)(2,1)S(1)} collective-permute-done((bf16[512,128]{1,0:T(8,128)(2,1)S(1)}, bf16[512,128]{1,0:T(8,128)(2,1)S(1)}, u32[]{:S(2)}, u32[]{:S(2)}) %collective-permute-start.13) | collective-permute-done | bytes 131104 | tf_op jit(solution)/shard_map/ppermute | solution.py:39
  48.1 1.3 collective-permute-start.19
  49.4 4.0 %collective-permute-start.17 = (bf16[528,128]{1,0:T(8,128)(2,1)S(1)}, bf16[528,128]{1,0:T(8,128)(2,1)S(1)}, u32[]{:S(2)}, u32[]{:S(2)}) collective-permute-start(bf16[528,128]{1,0:T(8,128)(2,1)S(1)} %get-tuple-element.78.refs_3_), channel_id=1, source_target_pairs={{0,2},{1,3},{2,0},{3,1},{4,6},{5,7},{6,4},{7,5},{8,10},{9,11},{10,... | collective-permute-start | bytes 405512 | tf_op jit(solution)/shard_map/ppermute | solution.py:39
  53.4 1.3 collective-permute-start.16
  54.7 1.7 %collective-permute-done.19.refs_7_ = bf16[528,128]{1,0:T(8,128)(2,1)S(1)} collective-permute-done((bf16[528,128]{1,0:T(8,128)(2,1)S(1)}, bf16[528,128]{1,0:T(8,128)(2,1)S(1)}, u32[]{:S(2)}, u32[]{:S(2)}) %collective-permute-start.19) | collective-permute-done | bytes 135200 | tf_op jit(solution)/shard_map/ppermute | solution.py:39
  56.4 2.5 %collective-permute-start.20 = (bf16[528,128]{1,0:T(8,128)(2,1)S(1)}, bf16[528,128]{1,0:T(8,128)(2,1)S(1)}, u32[]{:S(2)}, u32[]{:S(2)}) collective-permute-start(bf16[528,128]{1,0:T(8,128)(2,1)S(1)} %collective-permute-done.19.refs_7_), channel_id=1, source_target_pairs={{0,1},{1,0},{2,3},{3,2},{4,5},{5,4},{6,7},{7,6},{8,9},{9,8},{10,11... | collective-permute-start | bytes 405512 | tf_op jit(solution)/shard_map/ppermute | solution.py:39
  60.2 2.5 %collective-permute-done.20.refs_8_ = bf16[528,128]{1,0:T(8,128)(2,1)S(1)} collective-permute-done((bf16[528,128]{1,0:T(8,128)(2,1)S(1)}, bf16[528,128]{1,0:T(8,128)(2,1)S(1)}, u32[]{:S(2)}, u32[]{:S(2)}) %collective-permute-start.20) | collective-permute-done | bytes 135200 | tf_op jit(solution)/shard_map/ppermute | solution.py:39
  63.1 1.8 %collective-permute-done.21.refs_9_ = bf16[528,128]{1,0:T(8,128)(2,1)S(1)} collective-permute-done((bf16[528,128]{1,0:T(8,128)(2,1)S(1)}, bf16[528,128]{1,0:T(8,128)(2,1)S(1)}, u32[]{:S(2)}, u32[]{:S(2)}) %collective-permute-start.21) | collective-permute-done | bytes 135200 | tf_op jit(solution)/shard_map/ppermute | solution.py:39
  64.9 2.9 %collective-permute-done.22.refs_10_ = bf16[528,128]{1,0:T(8,128)(2,1)S(1)} collective-permute-done((bf16[528,128]{1,0:T(8,128)(2,1)S(1)}, bf16[528,128]{1,0:T(8,128)(2,1)S(1)}, u32[]{:S(2)}, u32[]{:S(2)}) %collective-permute-start.22) | collective-permute-done | bytes 135200 | tf_op jit(solution)/shard_map/ppermute | solution.py:39
  67.8 1.8 %shard_map.75 = (bf16[512,128]{1,0:T(8,128)(2,1)S(1)}, bf16[32,128,128]{2,1,0:T(8,128)(2,1)S(1)}, f32[4096,128]{1,0:T(8,128)S(1)}, bf16[512,128]{1,0:T(8,128)(2,1)S(1)}, f32[512,128]{1,0:T(8,128)S(1)}) custom-call(s32[5,274]{1,0:T(8,128)S(1)} %get-tuple-element.61.plan_ref.refs_0_, bf16[128,128,128]{2,1,0:T(8,128)(2,1)S(1)} %get-tuple-element.62.refs_1_.left_ref, ...), custom_call_target="tpu_custom_call" | custom-call | flops 268435456 | bytes 4194304 | tf_op jit(solution)/shard_map/pallas_call | solution.py:283
  69.6 1.6 collective-permute-start.23
  71.2 4.1 %shard_map.76 = (f32[512,128]{1,0:T(8,128)S(1)}, bf16[512,128]{1,0:T(8,128)(2,1)S(1)}, f32[512,128]{1,0:T(8,128)S(1)}, bf16[512,128]{1,0:T(8,128)(2,1)S(1)}, f32...) custom-call(s32[5,274]{1,0:T(8,128)S(1)} %get-tuple-element.61.plan_ref.refs_0_, ...), custom_call_target="tpu_custom_call" | custom-call | flops 268435456 | bytes 4194304 | tf_op jit(solution)/shard_map/pallas_call | solution.py:293
  75.5 1.9 %collective-permute-start.28 = (bf16[512,128]{1,0:T(8,128)(2,1)S(1)}, bf16[512,128]{1,0:T(8,128)(2,1)S(1)}, u32[]{:S(2)}, u32[]{:S(2)}) collective-permute-start(bf16[512,128]{1,0:T(8,128)(2,1)S(1)} %get-tuple-element.92), channel_id=1, source_target_pairs={{0,1},{1,0},{2,3},{3,2},{4,5},{5,4},{6,7},{7,6},{8,9},{9,8},{10,11... | collective-permute-start | bytes 393224 | tf_op jit(solution)/shard_map/ppermute | solution.py:39
  77.5 1.9 %collective-permute-start.30 = (bf16[512,128]{1,0:T(8,128)(2,1)S(1)}, bf16[512,128]{1,0:T(8,128)(2,1)S(1)}, u32[]{:S(2)}, u32[]{:S(2)}) collective-permute-start(bf16[512,128]{1,0:T(8,128)(2,1)S(1)} %get-tuple-element.94), channel_id=1, source_target_pairs={{0,1},{1,0},{2,3},{3,2},{4,5},{5,4},{6,7},{7,6},{8,9},{9,8},{10,11... | collective-permute-start | bytes 393224 | tf_op jit(solution)/shard_map/ppermute | solution.py:39
  81.0 2.1 %collective-permute-start.25 = (bf16[512,128]{1,0:T(8,128)(2,1)S(1)}, bf16[512,128]{1,0:T(8,128)(2,1)S(1)}, u32[]{:S(2)}, u32[]{:S(2)}) collective-permute-start(bf16[512,128]{1,0:T(8,128)(2,1)S(1)} %get-tuple-element.87), channel_id=1, source_target_pairs={{0,8},{16,24},{8,0},{24,16},{1,9},{17,25},{9,1},{25,17},{2,10},{18... | collective-permute-start | bytes 393224 | tf_op jit(solution)/shard_map/ppermute | solution.py:47
  83.2 2.1 %collective-permute-start.29 = (bf16[512,128]{1,0:T(8,128)(2,1)S(1)}, bf16[512,128]{1,0:T(8,128)(2,1)S(1)}, u32[]{:S(2)}, u32[]{:S(2)}) collective-permute-start(bf16[512,128]{1,0:T(8,128)(2,1)S(1)} %add_convert_fusion.4), channel_id=1, source_target_pairs={{0,2},{1,3},{2,0},{3,1},{4,6},{5,7},{6,4},{7,5},{8,10},{9,11},{10,... | collective-permute-start | bytes 393224 | tf_op jit(solution)/shard_map/ppermute | solution.py:39
  85.3 2.7 %collective-permute-start.31 = (bf16[512,128]{1,0:T(8,128)(2,1)S(1)}, bf16[512,128]{1,0:T(8,128)(2,1)S(1)}, u32[]{:S(2)}, u32[]{:S(2)}) collective-permute-start(bf16[512,128]{1,0:T(8,128)(2,1)S(1)} %add_convert_fusion.3), channel_id=1, source_target_pairs={{0,4},{1,5},{2,6},{3,7},{4,0},{5,1},{6,2},{7,3},{8,12},{9,13},{10,... | collective-permute-start | bytes 393224 | tf_op jit(solution)/shard_map/ppermute | solution.py:39
  88.8 2.1 %collective-permute-done.29.refs_2_ = bf16[512,128]{1,0:T(8,128)(2,1)S(1)} collective-permute-done((bf16[512,128]{1,0:T(8,128)(2,1)S(1)}, bf16[512,128]{1,0:T(8,128)(2,1)S(1)}, u32[]{:S(2)}, u32[]{:S(2)}) %collective-permute-start.29) | collective-permute-done | bytes 131104 | tf_op jit(solution)/shard_map/ppermute | solution.py:39
  90.9 3.4 %collective-permute-done.31.refs_3_ = bf16[512,128]{1,0:T(8,128)(2,1)S(1)} collective-permute-done((bf16[512,128]{1,0:T(8,128)(2,1)S(1)}, bf16[512,128]{1,0:T(8,128)(2,1)S(1)}, u32[]{:S(2)}, u32[]{:S(2)}) %collective-permute-start.31) | collective-permute-done | bytes 131104 | tf_op jit(solution)/shard_map/ppermute | solution.py:39
  94.9 2.6 %collective-permute-start.33 = (bf16[528,128]{1,0:T(8,128)(2,1)S(1)}, bf16[528,128]{1,0:T(8,128)(2,1)S(1)}, u32[]{:S(2)}, u32[]{:S(2)}) collective-permute-start(bf16[528,128]{1,0:T(8,128)(2,1)S(1)} %get-tuple-element.95.refs_3_), channel_id=1, source_target_pairs={{0,2},{1,3},{2,0},{3,1},{4,6},{5,7},{6,4},{7,5},{8,10},{9,11},{10,... | collective-permute-start | bytes 405512 | tf_op jit(solution)/shard_map/ppermute | solution.py:39
  98.3 3.6 %collective-permute-done.35.refs_7_ = bf16[528,128]{1,0:T(8,128)(2,1)S(1)} collective-permute-done((bf16[528,128]{1,0:T(8,128)(2,1)S(1)}, bf16[528,128]{1,0:T(8,128)(2,1)S(1)}, u32[]{:S(2)}, u32[]{:S(2)}) %collective-permute-start.35) | collective-permute-done | bytes 135200 | tf_op jit(solution)/shard_map/ppermute | solution.py:39
  104.2 2.7 %collective-permute-done.36.refs_8_ = bf16[528,128]{1,0:T(8,128)(2,1)S(1)} collective-permute-done((bf16[528,128]{1,0:T(8,128)(2,1)S(1)}, bf16[528,128]{1,0:T(8,128)(2,1)S(1)}, u32[]{:S(2)}, u32[]{:S(2)}) %collective-permute-start.36) | collective-permute-done | bytes 135200 | tf_op jit(solution)/shard_map/ppermute | solution.py:39
  108.3 3.6 %collective-permute-done.38.refs_10_ = bf16[528,128]{1,0:T(8,128)(2,1)S(1)} collective-permute-done((bf16[528,128]{1,0:T(8,128)(2,1)S(1)}, bf16[528,128]{1,0:T(8,128)(2,1)S(1)}, u32[]{:S(2)}, u32[]{:S(2)}) %collective-permute-start.38) | collective-permute-done | bytes 135200 | tf_op jit(solution)/shard_map/ppermute | solution.py:39
  111.9 1.8 %shard_map.80 = (bf16[512,128]{1,0:T(8,128)(2,1)S(1)}, bf16[32,128,128]{2,1,0:T(8,128)(2,1)S(1)}, f32[4096,128]{1,0:T(8,128)S(1)}, bf16[512,128]{1,0:T(8,128)(2,1)S(1)}, f32[512,128]{1,0:T(8,128)S(1)}) custom-call(s32[5,274]{1,0:T(8,128)S(1)} %get-tuple-element.61.plan_ref.refs_0_, bf16[128,128,128]{2,1,0:T(8,128)(2,1)S(1)} %get-tuple-element.62.refs_1_.left_ref, ...), custom_call_target="tpu_custom_call" | custom-call | flops 268435456 | bytes 4194304 | tf_op jit(solution)/shard_map/pallas_call | solution.py:283
  113.7 1.3 collective-permute-start.39
  115.0 4.1 %shard_map.81 = (f32[512,128]{1,0:T(8,128)S(1)}, bf16[512,128]{1,0:T(8,128)(2,1)S(1)}, f32[512,128]{1,0:T(8,128)S(1)}, bf16[512,128]{1,0:T(8,128)(2,1)S(1)}, f32...) custom-call(s32[5,274]{1,0:T(8,128)S(1)} %get-tuple-element.61.plan_ref.refs_0_, ...), custom_call_target="tpu_custom_call" | custom-call | flops 268435456 | bytes 4194304 | tf_op jit(solution)/shard_map/pallas_call | solution.py:293
  125.0 2.5 %collective-permute-start.41 = (bf16[512,128]{1,0:T(8,128)(2,1)S(1)}, bf16[512,128]{1,0:T(8,128)(2,1)S(1)}, u32[]{:S(2)}, u32[]{:S(2)}) collective-permute-start(bf16[512,128]{1,0:T(8,128)(2,1)S(1)} %get-tuple-element.105), channel_id=1, source_target_pairs={{0,8},{16,24},{8,0},{24,16},{1,9},{17,25},{9,1},{25,17},{2,10},{18... | collective-permute-start | bytes 393224 | tf_op jit(solution)/shard_map/ppermute | solution.py:47
  128.2 3.5 %collective-permute-start.47 = (bf16[512,128]{1,0:T(8,128)(2,1)S(1)}, bf16[512,128]{1,0:T(8,128)(2,1)S(1)}, u32[]{:S(2)}, u32[]{:S(2)}) collective-permute-start(bf16[512,128]{1,0:T(8,128)(2,1)S(1)} %add_convert_fusion), channel_id=1, source_target_pairs={{0,4},{1,5},{2,6},{3,7},{4,0},{5,1},{6,2},{7,3},{8,12},{9,13},{10,... | collective-permute-start | bytes 393224 | tf_op jit(solution)/shard_map/ppermute | solution.py:39
  132.5 3.0 %collective-permute-done.45.refs_2_ = bf16[512,128]{1,0:T(8,128)(2,1)S(1)} collective-permute-done((bf16[512,128]{1,0:T(8,128)(2,1)S(1)}, bf16[512,128]{1,0:T(8,128)(2,1)S(1)}, u32[]{:S(2)}, u32[]{:S(2)}) %collective-permute-start.45) | collective-permute-done | bytes 131104 | tf_op jit(solution)/shard_map/ppermute | solution.py:39
  135.5 2.0 %collective-permute-done.47.refs_3_ = bf16[512,128]{1,0:T(8,128)(2,1)S(1)} collective-permute-done((bf16[512,128]{1,0:T(8,128)(2,1)S(1)}, bf16[512,128]{1,0:T(8,128)(2,1)S(1)}, u32[]{:S(2)}, u32[]{:S(2)}) %collective-permute-start.47) | collective-permute-done | bytes 131104 | tf_op jit(solution)/shard_map/ppermute | solution.py:39
  137.9 2.7 %collective-permute-start.49 = (bf16[528,128]{1,0:T(8,128)(2,1)S(1)}, bf16[528,128]{1,0:T(8,128)(2,1)S(1)}, u32[]{:S(2)}, u32[]{:S(2)}) collective-permute-start(bf16[528,128]{1,0:T(8,128)(2,1)S(1)} %get-tuple-element.113.refs_3_), channel_id=1, source_target_pairs={{0,2},{1,3},{2,0},{3,1},{4,6},{5,7},{6,4},{7,5},{8,10},{9,11},{10,... | collective-permute-start | bytes 405512 | tf_op jit(solution)/shard_map/ppermute | solution.py:39
  141.9 3.1 %collective-permute-done.51.refs_7_ = bf16[528,128]{1,0:T(8,128)(2,1)S(1)} collective-permute-done((bf16[528,128]{1,0:T(8,128)(2,1)S(1)}, bf16[528,128]{1,0:T(8,128)(2,1)S(1)}, u32[]{:S(2)}, u32[]{:S(2)}) %collective-permute-start.51) | collective-permute-done | bytes 135200 | tf_op jit(solution)/shard_map/ppermute | solution.py:39
  147.5 2.6 %collective-permute-done.52.refs_8_ = bf16[528,128]{1,0:T(8,128)(2,1)S(1)} collective-permute-done((bf16[528,128]{1,0:T(8,128)(2,1)S(1)}, bf16[528,128]{1,0:T(8,128)(2,1)S(1)}, u32[]{:S(2)}, u32[]{:S(2)}) %collective-permute-start.52) | collective-permute-done | bytes 135200 | tf_op jit(solution)/shard_map/ppermute | solution.py:39
  151.6 3.5 %collective-permute-done.54.refs_10_ = bf16[528,128]{1,0:T(8,128)(2,1)S(1)} collective-permute-done((bf16[528,128]{1,0:T(8,128)(2,1)S(1)}, bf16[528,128]{1,0:T(8,128)(2,1)S(1)}, u32[]{:S(2)}, u32[]{:S(2)}) %collective-permute-start.54) | collective-permute-done | bytes 135200 | tf_op jit(solution)/shard_map/ppermute | solution.py:39
  155.1 5.7 %shard_map.85 = (bf16[512,128]{1,0:T(8,128)(2,1)}, f32[1,4]{1,0:T(1,128)}) custom-call(s32[5,274]{1,0:T(8,128)S(1)} %get-tuple-element.61.plan_ref.refs_0_, bf16[128,128,128]{2,1,0:T(8,128)(2,1)S(1)} %get-tuple-element.62.refs_1_.left_ref, bf16[128,128,128]{2,1,0:T(8,128)(2,1)S(1)} %shard_map.69.refs_2_.right_ref, ...), custom_call_target="tpu_custom_call" | custom-call | flops 536870912 | bytes 4194304 | tf_op jit(solution)/shard_map/pallas_call | solution.py:334
  (91 shorter events, 30.5 us)
Async XLA Ops:
  0.6 12.1 %collective-permute-start.3 = (bf16[512,128]{1,0:T(8,128)(2,1)}, bf16[512,128]{1,0:T(8,128)(2,1)S(1)}, u32[]{:S(2)}, u32[]{:S(2)}) collective-permute-start(bf16[512,128]{1,0:T(8,128)(2,1)} %bitcast.6), channel_id=1, source_target_pairs={{0,4},{1,5},{2,6},{3,7},{4,0},{5,1},{6,2},{7,3},{8,12},{9,13},{10,... | collective-permute-start | bytes 393224 | tf_op jit(solution)/shard_map/ppermute | solution.py:39
  4.7 8.7 %collective-permute-start.1 = (bf16[512,128]{1,0:T(8,128)(2,1)}, bf16[512,128]{1,0:T(8,128)(2,1)S(1)}, u32[]{:S(2)}, u32[]{:S(2)}) collective-permute-start(bf16[512,128]{1,0:T(8,128)(2,1)} %bitcast.7), channel_id=1, source_target_pairs={{0,2},{1,3},{2,0},{3,1},{4,6},{5,7},{6,4},{7,5},{8,10},{9,11},{10,... | collective-permute-start | bytes 393224 | tf_op jit(solution)/shard_map/ppermute | solution.py:39
  6.3 7.1 %collective-permute-start = (bf16[512,128]{1,0:T(8,128)(2,1)}, bf16[512,128]{1,0:T(8,128)(2,1)S(1)}, u32[]{:S(2)}, u32[]{:S(2)}) collective-permute-start(bf16[512,128]{1,0:T(8,128)(2,1)} %bitcast.8), channel_id=1, source_target_pairs={{0,1},{1,0},{2,3},{3,2},{4,5},{5,4},{6,7},{7,6},{8,9},{9,8},{10,11... | collective-permute-start | bytes 393224 | tf_op jit(solution)/shard_map/ppermute | solution.py:39
  12.8 5.9 %collective-permute-start.4 = (bf16[512,128]{1,0:T(8,128)(2,1)S(1)}, bf16[512,128]{1,0:T(8,128)(2,1)S(1)}, u32[]{:S(2)}, u32[]{:S(2)}) collective-permute-start(bf16[512,128]{1,0:T(8,128)(2,1)S(1)} %collective-permute-done.3.refs_7_.refs_16_), channel_id=1, source_target_pairs={{0,1},{1,0},{2,3},{3,2},{4,5},{5,4},{6,7},{7,6},{8,9},{9,8},{10,11... | collective-permute-start | bytes 393224 | tf_op jit(solution)/shard_map/ppermute | solution.py:39
  13.4 8.2 %collective-permute-start.2 = (bf16[512,128]{1,0:T(8,128)(2,1)S(1)}, bf16[512,128]{1,0:T(8,128)(2,1)S(1)}, u32[]{:S(2)}, u32[]{:S(2)}) collective-permute-start(bf16[512,128]{1,0:T(8,128)(2,1)S(1)} %collective-permute-done.1.refs_5_.refs_14_), channel_id=1, source_target_pairs={{0,1},{1,0},{2,3},{3,2},{4,5},{5,4},{6,7},{7,6},{8,9},{9,8},{10,11... | collective-permute-start | bytes 393224 | tf_op jit(solution)/shard_map/ppermute | solution.py:39
  14.9 6.7 %collective-permute-start.5 = (bf16[512,128]{1,0:T(8,128)(2,1)S(1)}, bf16[512,128]{1,0:T(8,128)(2,1)S(1)}, u32[]{:S(2)}, u32[]{:S(2)}) collective-permute-start(bf16[512,128]{1,0:T(8,128)(2,1)S(1)} %collective-permute-done.3.refs_7_.refs_16_), channel_id=1, source_target_pairs={{0,2},{1,3},{2,0},{3,1},{4,6},{5,7},{6,4},{7,5},{8,10},{9,11},{10,... | collective-permute-start | bytes 393224 | tf_op jit(solution)/shard_map/ppermute | solution.py:39
  25.1 5.0 %collective-permute-start.7 = (bf16[512,128]{1,0:T(8,128)(2,1)S(1)}, bf16[512,128]{1,0:T(8,128)(2,1)S(1)}, u32[]{:S(2)}, u32[]{:S(2)}) collective-permute-start(bf16[512,128]{1,0:T(8,128)(2,1)S(1)} %get-tuple-element.69), channel_id=1, source_target_pairs={{0,1},{1,0},{2,3},{3,2},{4,5},{5,4},{6,7},{7,6},{8,9},{9,8},{10,11... | collective-permute-start | bytes 393224 | tf_op jit(solution)/shard_map/ppermute | solution.py:39
  30.2 5.0 %collective-permute-start.8 = (bf16[512,128]{1,0:T(8,128)(2,1)S(1)}, bf16[512,128]{1,0:T(8,128)(2,1)S(1)}, u32[]{:S(2)}, u32[]{:S(2)}) collective-permute-start(bf16[512,128]{1,0:T(8,128)(2,1)S(1)} %add_convert_fusion.8), channel_id=1, source_target_pairs={{0,2},{1,3},{2,0},{3,1},{4,6},{5,7},{6,4},{7,5},{8,10},{9,11},{10,... | collective-permute-start | bytes 393224 | tf_op jit(solution)/shard_map/ppermute | solution.py:39
  30.7 8.8 %collective-permute-start.12 = (bf16[512,128]{1,0:T(8,128)(2,1)S(1)}, bf16[512,128]{1,0:T(8,128)(2,1)S(1)}, u32[]{:S(2)}, u32[]{:S(2)}) collective-permute-start(bf16[512,128]{1,0:T(8,128)(2,1)S(1)} %get-tuple-element.75), channel_id=1, source_target_pairs={{0,1},{1,0},{2,3},{3,2},{4,5},{5,4},{6,7},{7,6},{8,9},{9,8},{10,11... | collective-permute-start | bytes 393224 | tf_op jit(solution)/shard_map/ppermute | solution.py:39
  31.9 11.6 %collective-permute-start.11 = (bf16[512,128]{1,0:T(8,128)(2,1)S(1)}, bf16[512,128]{1,0:T(8,128)(2,1)S(1)}, u32[]{:S(2)}, u32[]{:S(2)}) collective-permute-start(bf16[512,128]{1,0:T(8,128)(2,1)S(1)} %get-tuple-element.72), channel_id=1, source_target_pairs={{0,1},{1,0},{2,3},{3,2},{4,5},{5,4},{6,7},{7,6},{8,9},{9,8},{10,11... | collective-permute-start | bytes 393224 | tf_op jit(solution)/shard_map/ppermute | solution.py:39
  32.7 7.0 %collective-permute-start.14 = (bf16[512,128]{1,0:T(8,128)(2,1)S(1)}, bf16[512,128]{1,0:T(8,128)(2,1)S(1)}, u32[]{:S(2)}, u32[]{:S(2)}) collective-permute-start(bf16[512,128]{1,0:T(8,128)(2,1)S(1)} %get-tuple-element.77), channel_id=1, source_target_pairs={{0,1},{1,0},{2,3},{3,2},{4,5},{5,4},{6,7},{7,6},{8,9},{9,8},{10,11... | collective-permute-start | bytes 393224 | tf_op jit(solution)/shard_map/ppermute | solution.py:39
  35.2 7.4 %collective-permute-start.10 = (bf16[512,128]{1,0:T(8,128)(2,1)S(1)}, bf16[512,128]{1,0:T(8,128)(2,1)S(1)}, u32[]{:S(2)}, u32[]{:S(2)}) collective-permute-start(bf16[512,128]{1,0:T(8,128)(2,1)S(1)} %bitcast.11), channel_id=1, source_target_pairs={{8,16},{16,8},{9,17},{17,9},{10,18},{18,10},{11,19},{19,11},{12,20... | collective-permute-start | bytes 393224 | tf_op jit(solution)/shard_map/ppermute | solution.py:47
  35.9 6.8 %collective-permute-start.9 = (bf16[512,128]{1,0:T(8,128)(2,1)S(1)}, bf16[512,128]{1,0:T(8,128)(2,1)S(1)}, u32[]{:S(2)}, u32[]{:S(2)}) collective-permute-start(bf16[512,128]{1,0:T(8,128)(2,1)S(1)} %bitcast.12), channel_id=1, source_target_pairs={{0,8},{16,24},{8,0},{24,16},{1,9},{17,25},{9,1},{25,17},{2,10},{18... | collective-permute-start | bytes 393224 | tf_op jit(solution)/shard_map/ppermute | solution.py:47
  39.5 8.3 %collective-permute-start.13 = (bf16[512,128]{1,0:T(8,128)(2,1)S(1)}, bf16[512,128]{1,0:T(8,128)(2,1)S(1)}, u32[]{:S(2)}, u32[]{:S(2)}) collective-permute-start(bf16[512,128]{1,0:T(8,128)(2,1)S(1)} %add_convert_fusion.7), channel_id=1, source_target_pairs={{0,2},{1,3},{2,0},{3,1},{4,6},{5,7},{6,4},{7,5},{8,10},{9,11},{10,... | collective-permute-start | bytes 393224 | tf_op jit(solution)/shard_map/ppermute | solution.py:39
  39.7 8.0 %collective-permute-start.15 = (bf16[512,128]{1,0:T(8,128)(2,1)S(1)}, bf16[512,128]{1,0:T(8,128)(2,1)S(1)}, u32[]{:S(2)}, u32[]{:S(2)}) collective-permute-start(bf16[512,128]{1,0:T(8,128)(2,1)S(1)} %add_convert_fusion.6), channel_id=1, source_target_pairs={{0,4},{1,5},{2,6},{3,7},{4,0},{5,1},{6,2},{7,3},{8,12},{9,13},{10,... | collective-permute-start | bytes 393224 | tf_op jit(solution)/shard_map/ppermute | solution.py:39
  48.1 8.4 %collective-permute-start.19 = (bf16[528,128]{1,0:T(8,128)(2,1)S(1)}, bf16[528,128]{1,0:T(8,128)(2,1)S(1)}, u32[]{:S(2)}, u32[]{:S(2)}) collective-permute-start(bf16[528,128]{1,0:T(8,128)(2,1)S(1)} %get-tuple-element.78.refs_3_), channel_id=1, source_target_pairs={{0,4},{1,5},{2,6},{3,7},{4,0},{5,1},{6,2},{7,3},{8,12},{9,13},{10,... | collective-permute-start | bytes 405512 | tf_op jit(solution)/shard_map/ppermute | solution.py:39
  49.4 9.5 %collective-permute-start.17 = (bf16[528,128]{1,0:T(8,128)(2,1)S(1)}, bf16[528,128]{1,0:T(8,128)(2,1)S(1)}, u32[]{:S(2)}, u32[]{:S(2)}) collective-permute-start(bf16[528,128]{1,0:T(8,128)(2,1)S(1)} %get-tuple-element.78.refs_3_), channel_id=1, source_target_pairs={{0,2},{1,3},{2,0},{3,1},{4,6},{5,7},{6,4},{7,5},{8,10},{9,11},{10,... | collective-permute-start | bytes 405512 | tf_op jit(solution)/shard_map/ppermute | solution.py:39
  53.4 6.2 %collective-permute-start.16 = (bf16[528,128]{1,0:T(8,128)(2,1)S(1)}, bf16[528,128]{1,0:T(8,128)(2,1)S(1)}, u32[]{:S(2)}, u32[]{:S(2)}) collective-permute-start(bf16[528,128]{1,0:T(8,128)(2,1)S(1)} %get-tuple-element.78.refs_3_), channel_id=1, source_target_pairs={{0,1},{1,0},{2,3},{3,2},{4,5},{5,4},{6,7},{7,6},{8,9},{9,8},{10,11... | collective-permute-start | bytes 405512 | tf_op jit(solution)/shard_map/ppermute | solution.py:39
  56.4 6.3 %collective-permute-start.20 = (bf16[528,128]{1,0:T(8,128)(2,1)S(1)}, bf16[528,128]{1,0:T(8,128)(2,1)S(1)}, u32[]{:S(2)}, u32[]{:S(2)}) collective-permute-start(bf16[528,128]{1,0:T(8,128)(2,1)S(1)} %collective-permute-done.19.refs_7_), channel_id=1, source_target_pairs={{0,1},{1,0},{2,3},{3,2},{4,5},{5,4},{6,7},{7,6},{8,9},{9,8},{10,11... | collective-permute-start | bytes 405512 | tf_op jit(solution)/shard_map/ppermute | solution.py:39
  59.0 6.0 %collective-permute-start.21 = (bf16[528,128]{1,0:T(8,128)(2,1)S(1)}, bf16[528,128]{1,0:T(8,128)(2,1)S(1)}, u32[]{:S(2)}, u32[]{:S(2)}) collective-permute-start(bf16[528,128]{1,0:T(8,128)(2,1)S(1)} %collective-permute-done.19.refs_7_), channel_id=1, source_target_pairs={{0,2},{1,3},{2,0},{3,1},{4,6},{5,7},{6,4},{7,5},{8,10},{9,11},{10,... | collective-permute-start | bytes 405512 | tf_op jit(solution)/shard_map/ppermute | solution.py:39
  59.6 5.3 %collective-permute-start.18 = (bf16[528,128]{1,0:T(8,128)(2,1)S(1)}, bf16[528,128]{1,0:T(8,128)(2,1)S(1)}, u32[]{:S(2)}, u32[]{:S(2)}) collective-permute-start(bf16[528,128]{1,0:T(8,128)(2,1)S(1)} %collective-permute-done.17.refs_5_), channel_id=1, source_target_pairs={{0,1},{1,0},{2,3},{3,2},{4,5},{5,4},{6,7},{7,6},{8,9},{9,8},{10,11... | collective-permute-start | bytes 405512 | tf_op jit(solution)/shard_map/ppermute | solution.py:39
  69.6 5.7 %collective-permute-start.23 = (bf16[512,128]{1,0:T(8,128)(2,1)S(1)}, bf16[512,128]{1,0:T(8,128)(2,1)S(1)}, u32[]{:S(2)}, u32[]{:S(2)}) collective-permute-start(bf16[512,128]{1,0:T(8,128)(2,1)S(1)} %get-tuple-element.86), channel_id=1, source_target_pairs={{0,1},{1,0},{2,3},{3,2},{4,5},{5,4},{6,7},{7,6},{8,9},{9,8},{10,11... | collective-permute-start | bytes 393224 | tf_op jit(solution)/shard_map/ppermute | solution.py:39
  75.3 5.0 %collective-permute-start.24 = (bf16[512,128]{1,0:T(8,128)(2,1)S(1)}, bf16[512,128]{1,0:T(8,128)(2,1)S(1)}, u32[]{:S(2)}, u32[]{:S(2)}) collective-permute-start(bf16[512,128]{1,0:T(8,128)(2,1)S(1)} %add_convert_fusion.5), channel_id=1, source_target_pairs={{0,2},{1,3},{2,0},{3,1},{4,6},{5,7},{6,4},{7,5},{8,10},{9,11},{10,... | collective-permute-start | bytes 393224 | tf_op jit(solution)/shard_map/ppermute | solution.py:39
  75.5 7.7 %collective-permute-start.28 = (bf16[512,128]{1,0:T(8,128)(2,1)S(1)}, bf16[512,128]{1,0:T(8,128)(2,1)S(1)}, u32[]{:S(2)}, u32[]{:S(2)}) collective-permute-start(bf16[512,128]{1,0:T(8,128)(2,1)S(1)} %get-tuple-element.92), channel_id=1, source_target_pairs={{0,1},{1,0},{2,3},{3,2},{4,5},{5,4},{6,7},{7,6},{8,9},{9,8},{10,11... | collective-permute-start | bytes 393224 | tf_op jit(solution)/shard_map/ppermute | solution.py:39
  77.5 11.3 %collective-permute-start.27 = (bf16[512,128]{1,0:T(8,128)(2,1)S(1)}, bf16[512,128]{1,0:T(8,128)(2,1)S(1)}, u32[]{:S(2)}, u32[]{:S(2)}) collective-permute-start(bf16[512,128]{1,0:T(8,128)(2,1)S(1)} %get-tuple-element.89), channel_id=1, source_target_pairs={{0,1},{1,0},{2,3},{3,2},{4,5},{5,4},{6,7},{7,6},{8,9},{9,8},{10,11... | collective-permute-start | bytes 393224 | tf_op jit(solution)/shard_map/ppermute | solution.py:39
  77.5 7.8 %collective-permute-start.30 = (bf16[512,128]{1,0:T(8,128)(2,1)S(1)}, bf16[512,128]{1,0:T(8,128)(2,1)S(1)}, u32[]{:S(2)}, u32[]{:S(2)}) collective-permute-start(bf16[512,128]{1,0:T(8,128)(2,1)S(1)} %get-tuple-element.94), channel_id=1, source_target_pairs={{0,1},{1,0},{2,3},{3,2},{4,5},{5,4},{6,7},{7,6},{8,9},{9,8},{10,11... | collective-permute-start | bytes 393224 | tf_op jit(solution)/shard_map/ppermute | solution.py:39
  80.4 7.6 %collective-permute-start.26 = (bf16[512,128]{1,0:T(8,128)(2,1)S(1)}, bf16[512,128]{1,0:T(8,128)(2,1)S(1)}, u32[]{:S(2)}, u32[]{:S(2)}) collective-permute-start(bf16[512,128]{1,0:T(8,128)(2,1)S(1)} %get-tuple-element.87), channel_id=1, source_target_pairs={{8,16},{16,8},{9,17},{17,9},{10,18},{18,10},{11,19},{19,11},{12,20... | collective-permute-start | bytes 393224 | tf_op jit(solution)/shard_map/ppermute | solution.py:47
  81.0 7.0 %collective-permute-start.25 = (bf16[512,128]{1,0:T(8,128)(2,1)S(1)}, bf16[512,128]{1,0:T(8,128)(2,1)S(1)}, u32[]{:S(2)}, u32[]{:S(2)}) collective-permute-start(bf16[512,128]{1,0:T(8,128)(2,1)S(1)} %get-tuple-element.87), channel_id=1, source_target_pairs={{0,8},{16,24},{8,0},{24,16},{1,9},{17,25},{9,1},{25,17},{2,10},{18... | collective-permute-start | bytes 393224 | tf_op jit(solution)/shard_map/ppermute | solution.py:47
  83.2 7.7 %collective-permute-start.29 = (bf16[512,128]{1,0:T(8,128)(2,1)S(1)}, bf16[512,128]{1,0:T(8,128)(2,1)S(1)}, u32[]{:S(2)}, u32[]{:S(2)}) collective-permute-start(bf16[512,128]{1,0:T(8,128)(2,1)S(1)} %add_convert_fusion.4), channel_id=1, source_target_pairs={{0,2},{1,3},{2,0},{3,1},{4,6},{5,7},{6,4},{7,5},{8,10},{9,11},{10,... | collective-permute-start | bytes 393224 | tf_op jit(solution)/shard_map/ppermute | solution.py:39
  85.3 9.0 %collective-permute-start.31 = (bf16[512,128]{1,0:T(8,128)(2,1)S(1)}, bf16[512,128]{1,0:T(8,128)(2,1)S(1)}, u32[]{:S(2)}, u32[]{:S(2)}) collective-permute-start(bf16[512,128]{1,0:T(8,128)(2,1)S(1)} %add_convert_fusion.3), channel_id=1, source_target_pairs={{0,4},{1,5},{2,6},{3,7},{4,0},{5,1},{6,2},{7,3},{8,12},{9,13},{10,... | collective-permute-start | bytes 393224 | tf_op jit(solution)/shard_map/ppermute | solution.py:39
  94.6 7.2 %collective-permute-start.35 = (bf16[528,128]{1,0:T(8,128)(2,1)S(1)}, bf16[528,128]{1,0:T(8,128)(2,1)S(1)}, u32[]{:S(2)}, u32[]{:S(2)}) collective-permute-start(bf16[528,128]{1,0:T(8,128)(2,1)S(1)} %get-tuple-element.95.refs_3_), channel_id=1, source_target_pairs={{0,4},{1,5},{2,6},{3,7},{4,0},{5,1},{6,2},{7,3},{8,12},{9,13},{10,... | collective-permute-start | bytes 405512 | tf_op jit(solution)/shard_map/ppermute | solution.py:39
  94.9 7.9 %collective-permute-start.33 = (bf16[528,128]{1,0:T(8,128)(2,1)S(1)}, bf16[528,128]{1,0:T(8,128)(2,1)S(1)}, u32[]{:S(2)}, u32[]{:S(2)}) collective-permute-start(bf16[528,128]{1,0:T(8,128)(2,1)S(1)} %get-tuple-element.95.refs_3_), channel_id=1, source_target_pairs={{0,2},{1,3},{2,0},{3,1},{4,6},{5,7},{6,4},{7,5},{8,10},{9,11},{10,... | collective-permute-start | bytes 405512 | tf_op jit(solution)/shard_map/ppermute | solution.py:39
  97.5 5.4 %collective-permute-start.32 = (bf16[528,128]{1,0:T(8,128)(2,1)S(1)}, bf16[528,128]{1,0:T(8,128)(2,1)S(1)}, u32[]{:S(2)}, u32[]{:S(2)}) collective-permute-start(bf16[528,128]{1,0:T(8,128)(2,1)S(1)} %get-tuple-element.95.refs_3_), channel_id=1, source_target_pairs={{0,1},{1,0},{2,3},{3,2},{4,5},{5,4},{6,7},{7,6},{8,9},{9,8},{10,11... | collective-permute-start | bytes 405512 | tf_op jit(solution)/shard_map/ppermute | solution.py:39
  101.8 5.0 %collective-permute-start.36 = (bf16[528,128]{1,0:T(8,128)(2,1)S(1)}, bf16[528,128]{1,0:T(8,128)(2,1)S(1)}, u32[]{:S(2)}, u32[]{:S(2)}) collective-permute-start(bf16[528,128]{1,0:T(8,128)(2,1)S(1)} %collective-permute-done.35.refs_7_), channel_id=1, source_target_pairs={{0,1},{1,0},{2,3},{3,2},{4,5},{5,4},{6,7},{7,6},{8,9},{9,8},{10,11... | collective-permute-start | bytes 405512 | tf_op jit(solution)/shard_map/ppermute | solution.py:39
  102.8 5.3 %collective-permute-start.37 = (bf16[528,128]{1,0:T(8,128)(2,1)S(1)}, bf16[528,128]{1,0:T(8,128)(2,1)S(1)}, u32[]{:S(2)}, u32[]{:S(2)}) collective-permute-start(bf16[528,128]{1,0:T(8,128)(2,1)S(1)} %collective-permute-done.35.refs_7_), channel_id=1, source_target_pairs={{0,2},{1,3},{2,0},{3,1},{4,6},{5,7},{6,4},{7,5},{8,10},{9,11},{10,... | collective-permute-start | bytes 405512 | tf_op jit(solution)/shard_map/ppermute | solution.py:39
  102.9 5.4 %collective-permute-start.34 = (bf16[528,128]{1,0:T(8,128)(2,1)S(1)}, bf16[528,128]{1,0:T(8,128)(2,1)S(1)}, u32[]{:S(2)}, u32[]{:S(2)}) collective-permute-start(bf16[528,128]{1,0:T(8,128)(2,1)S(1)} %collective-permute-done.33.refs_5_), channel_id=1, source_target_pairs={{0,1},{1,0},{2,3},{3,2},{4,5},{5,4},{6,7},{7,6},{8,9},{9,8},{10,11... | collective-permute-start | bytes 405512 | tf_op jit(solution)/shard_map/ppermute | solution.py:39
  113.7 5.5 %collective-permute-start.39 = (bf16[512,128]{1,0:T(8,128)(2,1)S(1)}, bf16[512,128]{1,0:T(8,128)(2,1)S(1)}, u32[]{:S(2)}, u32[]{:S(2)}) collective-permute-start(bf16[512,128]{1,0:T(8,128)(2,1)S(1)} %get-tuple-element.104), channel_id=1, source_target_pairs={{0,1},{1,0},{2,3},{3,2},{4,5},{5,4},{6,7},{7,6},{8,9},{9,8},{10,11... | collective-permute-start | bytes 393224 | tf_op jit(solution)/shard_map/ppermute | solution.py:39
  119.3 5.0 %collective-permute-start.40 = (bf16[512,128]{1,0:T(8,128)(2,1)S(1)}, bf16[512,128]{1,0:T(8,128)(2,1)S(1)}, u32[]{:S(2)}, u32[]{:S(2)}) collective-permute-start(bf16[512,128]{1,0:T(8,128)(2,1)S(1)} %add_convert_fusion.2), channel_id=1, source_target_pairs={{0,2},{1,3},{2,0},{3,1},{4,6},{5,7},{6,4},{7,5},{8,10},{9,11},{10,... | collective-permute-start | bytes 393224 | tf_op jit(solution)/shard_map/ppermute | solution.py:39
  120.1 7.4 %collective-permute-start.44 = (bf16[512,128]{1,0:T(8,128)(2,1)S(1)}, bf16[512,128]{1,0:T(8,128)(2,1)S(1)}, u32[]{:S(2)}, u32[]{:S(2)}) collective-permute-start(bf16[512,128]{1,0:T(8,128)(2,1)S(1)} %get-tuple-element.110), channel_id=1, source_target_pairs={{0,1},{1,0},{2,3},{3,2},{4,5},{5,4},{6,7},{7,6},{8,9},{9,8},{10,11... | collective-permute-start | bytes 393224 | tf_op jit(solution)/shard_map/ppermute | solution.py:39
  121.1 11.4 %collective-permute-start.43 = (bf16[512,128]{1,0:T(8,128)(2,1)S(1)}, bf16[512,128]{1,0:T(8,128)(2,1)S(1)}, u32[]{:S(2)}, u32[]{:S(2)}) collective-permute-start(bf16[512,128]{1,0:T(8,128)(2,1)S(1)} %get-tuple-element.107), channel_id=1, source_target_pairs={{0,1},{1,0},{2,3},{3,2},{4,5},{5,4},{6,7},{7,6},{8,9},{9,8},{10,11... | collective-permute-start | bytes 393224 | tf_op jit(solution)/shard_map/ppermute | solution.py:39
  122.1 6.1 %collective-permute-start.46 = (bf16[512,128]{1,0:T(8,128)(2,1)S(1)}, bf16[512,128]{1,0:T(8,128)(2,1)S(1)}, u32[]{:S(2)}, u32[]{:S(2)}) collective-permute-start(bf16[512,128]{1,0:T(8,128)(2,1)S(1)} %get-tuple-element.112), channel_id=1, source_target_pairs={{0,1},{1,0},{2,3},{3,2},{4,5},{5,4},{6,7},{7,6},{8,9},{9,8},{10,11... | collective-permute-start | bytes 393224 | tf_op jit(solution)/shard_map/ppermute | solution.py:39
  124.3 7.4 %collective-permute-start.42 = (bf16[512,128]{1,0:T(8,128)(2,1)S(1)}, bf16[512,128]{1,0:T(8,128)(2,1)S(1)}, u32[]{:S(2)}, u32[]{:S(2)}) collective-permute-start(bf16[512,128]{1,0:T(8,128)(2,1)S(1)} %get-tuple-element.105), channel_id=1, source_target_pairs={{8,16},{16,8},{9,17},{17,9},{10,18},{18,10},{11,19},{19,11},{12,20... | collective-permute-start | bytes 393224 | tf_op jit(solution)/shard_map/ppermute | solution.py:47
  125.0 6.8 %collective-permute-start.41 = (bf16[512,128]{1,0:T(8,128)(2,1)S(1)}, bf16[512,128]{1,0:T(8,128)(2,1)S(1)}, u32[]{:S(2)}, u32[]{:S(2)}) collective-permute-start(bf16[512,128]{1,0:T(8,128)(2,1)S(1)} %get-tuple-element.105), channel_id=1, source_target_pairs={{0,8},{16,24},{8,0},{24,16},{1,9},{17,25},{9,1},{25,17},{2,10},{18... | collective-permute-start | bytes 393224 | tf_op jit(solution)/shard_map/ppermute | solution.py:47
  127.5 7.9 %collective-permute-start.45 = (bf16[512,128]{1,0:T(8,128)(2,1)S(1)}, bf16[512,128]{1,0:T(8,128)(2,1)S(1)}, u32[]{:S(2)}, u32[]{:S(2)}) collective-permute-start(bf16[512,128]{1,0:T(8,128)(2,1)S(1)} %add_convert_fusion.1), channel_id=1, source_target_pairs={{0,2},{1,3},{2,0},{3,1},{4,6},{5,7},{6,4},{7,5},{8,10},{9,11},{10,... | collective-permute-start | bytes 393224 | tf_op jit(solution)/shard_map/ppermute | solution.py:39
  128.2 9.2 %collective-permute-start.47 = (bf16[512,128]{1,0:T(8,128)(2,1)S(1)}, bf16[512,128]{1,0:T(8,128)(2,1)S(1)}, u32[]{:S(2)}, u32[]{:S(2)}) collective-permute-start(bf16[512,128]{1,0:T(8,128)(2,1)S(1)} %add_convert_fusion), channel_id=1, source_target_pairs={{0,4},{1,5},{2,6},{3,7},{4,0},{5,1},{6,2},{7,3},{8,12},{9,13},{10,... | collective-permute-start | bytes 393224 | tf_op jit(solution)/shard_map/ppermute | solution.py:39
  137.7 7.3 %collective-permute-start.51 = (bf16[528,128]{1,0:T(8,128)(2,1)S(1)}, bf16[528,128]{1,0:T(8,128)(2,1)S(1)}, u32[]{:S(2)}, u32[]{:S(2)}) collective-permute-start(bf16[528,128]{1,0:T(8,128)(2,1)S(1)} %get-tuple-element.113.refs_3_), channel_id=1, source_target_pairs={{0,4},{1,5},{2,6},{3,7},{4,0},{5,1},{6,2},{7,3},{8,12},{9,13},{10,... | collective-permute-start | bytes 405512 | tf_op jit(solution)/shard_map/ppermute | solution.py:39
  137.9 8.3 %collective-permute-start.49 = (bf16[528,128]{1,0:T(8,128)(2,1)S(1)}, bf16[528,128]{1,0:T(8,128)(2,1)S(1)}, u32[]{:S(2)}, u32[]{:S(2)}) collective-permute-start(bf16[528,128]{1,0:T(8,128)(2,1)S(1)} %get-tuple-element.113.refs_3_), channel_id=1, source_target_pairs={{0,2},{1,3},{2,0},{3,1},{4,6},{5,7},{6,4},{7,5},{8,10},{9,11},{10,... | collective-permute-start | bytes 405512 | tf_op jit(solution)/shard_map/ppermute | solution.py:39
  140.7 5.9 %collective-permute-start.48 = (bf16[528,128]{1,0:T(8,128)(2,1)S(1)}, bf16[528,128]{1,0:T(8,128)(2,1)S(1)}, u32[]{:S(2)}, u32[]{:S(2)}) collective-permute-start(bf16[528,128]{1,0:T(8,128)(2,1)S(1)} %get-tuple-element.113.refs_3_), channel_id=1, source_target_pairs={{0,1},{1,0},{2,3},{3,2},{4,5},{5,4},{6,7},{7,6},{8,9},{9,8},{10,11... | collective-permute-start | bytes 405512 | tf_op jit(solution)/shard_map/ppermute | solution.py:39
  (8 other events, 39.6 us)
